TPU v7x, 256 devices: a whole 4x4x8 slice. The times are simulated.
256 devices in a mesh: member: 16 (over y_lo, z), lat: 4 (over x), lon: 4 (over y_hi, core).
Axes of the slice: x: 4, y: 4 (y_hi: 2, y_lo: 2; y = y_hi * 2 + y_lo), z: 8, core: 2. Of those that a mesh axis runs over, the one named last changes fastest.
Arguments:
- embeddings: bfloat16 [16, 83, 32, 512], P('member', None, 'lat', 'lon'), may hold values from -6 to 6
- entry_perturbation: bfloat16 [16, 83, 32, 512], P('member', None, 'lat', 'lon'), may hold values from -6 to 6
- target: bfloat16 [83, 32, 512], P(None, 'lat', 'lon'), may hold values from -9 to 9
- feature_scale_factor: float32 [83], replicated, may hold values from 0.5 to 1.5
- first_stencil_kernel: bfloat16 [9, 192, 83], replicated, may hold values from -0.21875 to 0.21875
- second_stencil_kernel: bfloat16 [9, 83, 192], replicated, may hold values from -0.15625 to 0.15625
Outputs:
- embedding_sensitivities: bfloat16 [16, 83, 32, 512], P('member', None, 'lat', 'lon')
- grad_weight_in: float32 [9, 192, 83], replicated
- grad_weight_out: float32 [9, 83, 192], replicated
All inputs are finite; a program needn't handle non-finite values.
Results may differ from a plain program's by a relative error of at most 0.0069.
Values may be sent and summed in bfloat16 or wider, within the bound.
No kernel may reach another device: no remote copies, remote signals or barrier semaphores. Data moves between devices by JAX's collectives and lax.ppermute only.
A program may use at most 64 MiB of HBM per device.

v0:
```python
import jax
import jax.numpy as jnp
from jax import lax
from jax.sharding import PartitionSpec as P

soft_eps = 0.01


def extended(block, sides, width, periodic):
    for axis, dim in sides:
        count = lax.axis_size(axis)
        forward = [(i, i + 1) for i in range(count - 1)]
        if periodic:
            forward.append((count - 1, 0))
        backward = [(target, source) for source, target in forward]
        low = lax.ppermute(
            lax.slice_in_dim(block, block.shape[dim] - width, None, axis=dim), axis, forward
        )
        high = lax.ppermute(lax.slice_in_dim(block, 0, width, axis=dim), axis, backward)
        block = jnp.concatenate([low, block, high], axis=dim)
    return block


def differentiable_derivative(values):
    return values / jnp.sqrt(values * values + soft_eps)


def normalize(embedded_map, feature_scale_factor):
    average = jnp.mean(embedded_map, axis=0, keepdims=True)
    centered = embedded_map - average
    variance = jnp.mean(centered * centered, axis=0, keepdims=True)
    return centered * lax.rsqrt(variance + 1e-05) * feature_scale_factor[:, None, None]


def window_cells(padded, row_off, col_off, block_height, block_breadth):
    return padded[:, row_off : row_off + block_height, col_off : col_off + block_breadth].reshape(
        padded.shape[0], block_height * block_breadth
    )


def apply_stencil_layers(padded, weight, block_height, block_breadth):
    totals = None
    for offset in range(9):
        partial_value = jnp.dot(
            weight[offset],
            window_cells(padded, offset // 3, offset % 3, block_height, block_breadth),
            preferred_element_type=jnp.float32,
        )
        totals = partial_value if totals is None else totals + partial_value
    return totals.reshape(weight.shape[1], block_height, block_breadth)


def transpose_conv(padded, weight, block_height, block_breadth):
    totals = None
    for offset in range(9):
        partial_value = jnp.dot(
            weight[offset].T,
            window_cells(padded, 2 - offset // 3, 2 - offset % 3, block_height, block_breadth),
            preferred_element_type=jnp.float32,
        )
        totals = partial_value if totals is None else totals + partial_value
    return totals.reshape(weight.shape[2], block_height, block_breadth)


def weight_grad(grad_out, padded, block_height, block_breadth):
    flat_grad = grad_out.reshape(grad_out.shape[0], block_height * block_breadth)
    terms = []
    for offset in range(9):
        terms.append(
            jnp.dot(
                flat_grad,
                window_cells(padded, offset // 3, offset % 3, block_height, block_breadth).T,
                preferred_element_type=jnp.float32,
            )
        )
    return jnp.stack(terms)


def with_rims(values, rim_width):
    lon_wide = extended(values, (("lon", 2),), rim_width, True)
    return extended(lon_wide, (("lat", 1),), rim_width, False)


def on_device(
    embeddings,
    entry_perturbation,
    target,
    feature_scale_factor,
    first_stencil_kernel,
    second_stencil_kernel,
):
    embedded_map = embeddings[0].astype(jnp.float32) + entry_perturbation[0].astype(jnp.float32)
    feature_depth, block_height, block_breadth = embedded_map.shape
    rescaled_map = normalize(embedded_map, feature_scale_factor).astype(jnp.bfloat16)
    normed_pad = with_rims(rescaled_map, 1)
    preceding_nonlinearity = apply_stencil_layers(
        normed_pad, first_stencil_kernel, block_height, block_breadth
    )
    padded_hidden = with_rims(jax.nn.gelu(preceding_nonlinearity).astype(jnp.bfloat16), 1)
    entry_prediction = embedded_map + apply_stencil_layers(
        padded_hidden, second_stencil_kernel, block_height, block_breadth
    )
    members = lax.axis_size("member")
    location_total = block_height * block_breadth
    location_vector = entry_prediction.reshape(feature_depth, location_total)
    measured_truth_values = target.astype(jnp.float32).reshape(feature_depth, location_total)
    cell_share = location_total // members
    spread = lax.all_to_all(
        location_vector[:, None, :], "member", split_axis=2, concat_axis=1, tiled=True
    )
    own_truth = lax.dynamic_slice_in_dim(
        measured_truth_values, lax.axis_index("member") * cell_share, cell_share, 1
    )

    def add_member(other, running):
        column = lax.dynamic_slice_in_dim(spread, other, 1, 1)
        return running + differentiable_derivative(spread - column)

    couple_difference_total = lax.fori_loop(0, members, add_member, jnp.zeros_like(spread))
    local_grad = differentiable_derivative(
        spread - own_truth[:, None, :]
    ) - couple_difference_total / (members - 1)
    location_sensitivity = lax.all_to_all(
        local_grad, "member", split_axis=1, concat_axis=2, tiled=True
    )
    prediction_sensitivity = location_sensitivity.reshape(
        feature_depth, block_height, block_breadth
    )
    truncated_sensitivity = prediction_sensitivity.astype(jnp.bfloat16)
    grad_hidden = transpose_conv(
        with_rims(truncated_sensitivity, 1), second_stencil_kernel, block_height, block_breadth
    )
    unused, gelu_pull = jax.vjp(jax.nn.gelu, preceding_nonlinearity)
    grad_pre = gelu_pull(grad_hidden)[0].astype(jnp.bfloat16)
    rescaled_sensitivity = transpose_conv(
        with_rims(grad_pre, 1), first_stencil_kernel, block_height, block_breadth
    )
    unused_two, rescale_reverse_mode = jax.vjp(
        lambda values: normalize(values, feature_scale_factor), embedded_map
    )
    embedding_sensitivities = (
        prediction_sensitivity + rescale_reverse_mode(rescaled_sensitivity)[0]
    ).astype(jnp.bfloat16)[None]
    grad_out = weight_grad(truncated_sensitivity, padded_hidden, block_height, block_breadth)
    grad_in = weight_grad(grad_pre, normed_pad, block_height, block_breadth)
    grad_in, grad_out = lax.psum((grad_in, grad_out), ("member", "lat", "lon"))
    total_cells = (
        members * block_height * lax.axis_size("lat") * block_breadth * lax.axis_size("lon")
    )
    grad_scale = 1.0 / jnp.sqrt(jnp.float32(total_cells))
    return (embedding_sensitivities, grad_in * grad_scale, grad_out * grad_scale)


def solution(mesh):
    placed = (
        P("member", None, "lat", "lon"),
        P("member", None, "lat", "lon"),
        P(None, "lat", "lon"),
        P(),
        P(),
        P(),
    )
    return jax.shard_map(
        on_device,
        mesh=mesh,
        in_specs=placed,
        out_specs=(P("member", None, "lat", "lon"), P(), P()),
        check_vma=False,
    )
```

profile of v0, /device:TPU:1, one launch (start us, length us, event | category | flops | bytes accessed | tf_op | source)
XLA Modules:
  0.0 419.5 jit_solution(15320614921632616086)
XLA Ops:
  7.2 1.0 fusion.192
  8.3 1.1 multiply_reduce_fusion
  9.4 1.1 multiply_convert_fusion.1
  10.7 4.4 %collective-permute-start = (bf16[83,8,1]{2,0,1:T(8,128)(2,1)S(1)}, bf16[83,8,1]{2,0,1:T(8,128)(2,1)S(1)}, u32[]{:S(2)}, u32[]{:S(2)}) collective-permute-start(bf16[83,8,1]{2,0,1:T(8,128)(2,1)S(1)} %get-tuple-element.157), channel_id=1, source_target_pairs={{0,1},{1,2},{2,3},{3,0},{4,5},{5,6},{6,7},{7,4},{8,9},{9,10},{10,1... | collective-permute-start | bytes 3992 | tf_op jit(solution)/shard_map/ppermute | solution.py:16
  15.9 1.6 collective-permute-done
  17.5 4.2 collective-permute-done.1
  21.8 2.9 collective-permute-start.2
  24.7 1.3 collective-permute-start.3
  27.0 2.5 collective-permute-done.3
  35.4 2.9 collective-permute-start.4
  38.5 8.4 %collective-permute-done.4 = bf16[192,8,1]{2,0,1:T(8,128)(2,1)S(1)} collective-permute-done((bf16[192,8,1]{2,0,1:T(8,128)(2,1)S(1)}, bf16[192,8,1]{2,0,1:T(8,128)(2,1)S(1)}, u32[]{:S(2)}, u32[]{:S(2)}) %collective-permute-start.4) | collective-permute-done | bytes 3104 | tf_op jit(solution)/shard_map/ppermute | solution.py:16
  47.6 3.2 collective-permute-start.6
  50.8 1.3 collective-permute-start.7
  52.9 3.8 collective-permute-done.7
  62.2 9.0 %all-to-all-start = ((f32[83,1,1024]{0,1,2:T(1,128)}), f32[83,1,1024]{0,1,2:T(1,128)S(1)}, u32[]{:S(2)}, u32[]{:S(2)}) async-start(f32[83,1,1024]{0,1,2:T(1,128)} %copy.111), calls=%async_computation | async-start | bytes 1048576 | tf_op jit(solution)/shard_map/all_to_all | solution.py:108
  71.5 1.9 copy.156
  74.1 10.7 %all-to-all-done = f32[83,1,1024]{0,1,2:T(1,128)S(1)} async-done(((f32[83,1,1024]{0,1,2:T(1,128)}), f32[83,1,1024]{0,1,2:T(1,128)S(1)}, u32[]{:S(2)}, u32[]{:S(2)}) %all-to-all-start) | async-done | bytes 340000 | tf_op jit(solution)/shard_map/all_to_all | solution.py:108
  84.8 5.7 %while.14 = (s32[]{:T(128)}, f32[83,16,64]{0,2,1:T(8,128)S(1)}, f32[83,16,64]{0,2,1:T(8,128)S(1)}, s32[]{:T(128)}, s32[]{:T(128)}) while((s32[]{:T(128)}, f32[83,16,64]{0,2,1:T(8,128)S(1)}, f32[83,16,64]{0,2,1:T(8,128)S(1)}, s32[]{:T(128)}, s32[]{:T(128)}) %tuple.85), condition=%wide.region_3.0_spmd.clone, body=%wide.region_2.0_spmd.clone.sunk | while | flops 509955 | bytes 1083723 | solution.py:119
  90.7 19.2 %all_to_all.21 = f32[83,16,64]{0,2,1:T(8,128)S(1)} all-to-all(f32[83,16,64]{0,2,1:T(8,128)S(1)} %multiply_subtract_fusion), channel_id=1, replica_groups=mesh['member'=16,'lat'=4,'lon'=4] {'member'}, dimensions={1} | all-to-all | bytes 679936 | tf_op jit(solution)/shard_map/all_to_all | solution.py:123
  111.0 5.7 %collective-permute-start.8 = (bf16[83,8,1]{0,2,1:T(2,128)(2,1)S(1)}, bf16[83,8,1]{0,2,1:T(2,128)(2,1)S(1)}, u32[]{:S(2)}, u32[]{:S(2)}) collective-permute-start(bf16[83,8,1]{0,2,1:T(2,128)(2,1)S(1)} %get-tuple-element.153), channel_id=1, source_target_pairs={{0,1},{1,2},{2,3},{3,0},{4,5},{5,6},{6,7},{7,4},{8,9},{9,10},{10,1... | collective-permute-start | bytes 3992 | tf_op jit(solution)/shard_map/ppermute | solution.py:16
  116.7 2.0 fusion.111
  121.3 1.3 collective-permute-start.10
  122.6 4.0 collective-permute-start.11
  136.7 1.1 fusion.8
  147.2 4.1 collective-permute-start.12
  152.2 7.7 %collective-permute-done.12 = bf16[192,8,1]{2,0,1:T(8,128)(2,1)S(1)} collective-permute-done((bf16[192,8,1]{2,0,1:T(8,128)(2,1)}, bf16[192,8,1]{2,0,1:T(8,128)(2,1)S(1)}, u32[]{:S(2)}, u32[]{:S(2)}) %collective-permute-start.12) | collective-permute-done | bytes 3104 | tf_op jit(solution)/shard_map/ppermute | solution.py:16
  159.8 1.3 collective-permute-done.13
  161.3 1.3 collective-permute-start.14
  162.6 4.8 %collective-permute-start.15 = (bf16[192,1,130]{2,0,1:T(8,128)(2,1)S(1)}, bf16[192,1,130]{2,0,1:T(8,128)(2,1)S(1)}, u32[]{:S(2)}, u32[]{:S(2)}) collective-permute-start(bf16[192,1,130]{2,0,1:T(8,128)(2,1)S(1)} %get-tuple-element.99), channel_id=1, source_target_pairs={{0,4},{4,8},{8,12},{1,5},{5,9},{9,13},{2,6},{6,10},{10,14},{3,7},{... | collective-permute-start | bytes 149768 | tf_op jit(solution)/shard_map/ppermute | solution.py:16
  168.5 1.2 collective-permute-done.15
  176.4 233.1 %all-reduce.3.cloned.1.call-done = (f32[9,192,83]{1,2,0:T(8,128)}, f32[9,83,192]{2,1,0:T(8,128)}) async-done(((f32[9,192,83]{1,2,0:T(8,128)}, f32[9,83,192]{2,1,0:T(8,128)}), (f32[9,192,83]{1,2,0:T(8,128)}, f32[9,83,192]{2,1,0:T(8,128)})) %all-reduce.3.cloned.1.call-update) | async-done | bytes 1147408 | tf_op jit(solution)/shard_map/psum | solution.py:146
  409.5 2.2 broadcast_multiply_fusion
  (233 shorter events, 53.8 us)
Async XLA Ops:
  8.2 6.8 %copy-start.6 = (bf16[1,83,8,128]{3,2,1,0:T(8,128)(2,1)S(1)}, bf16[1,83,8,128]{3,2,1,0:T(8,128)(2,1)}, u32[]{:S(2)}) copy-start(bf16[1,83,8,128]{3,2,1,0:T(8,128)(2,1)} %param.9) | copy-start | bytes 509956
  8.2 6.8 %copy-start.7 = (bf16[1,83,8,128]{3,2,1,0:T(8,128)(2,1)S(1)}, bf16[1,83,8,128]{3,2,1,0:T(8,128)(2,1)}, u32[]{:S(2)}) copy-start(bf16[1,83,8,128]{3,2,1,0:T(8,128)(2,1)} %param.8) | copy-start | bytes 509956
  8.2 6.8 %copy-start.29 = (f32[83]{0:T(128)S(1)}, f32[83]{0:T(128)}, u32[]{:S(2)}) copy-start(f32[83]{0:T(128)} %param.11) | copy-start | bytes 1000
  10.7 6.8 %collective-permute-start = (bf16[83,8,1]{2,0,1:T(8,128)(2,1)S(1)}, bf16[83,8,1]{2,0,1:T(8,128)(2,1)S(1)}, u32[]{:S(2)}, u32[]{:S(2)}) collective-permute-start(bf16[83,8,1]{2,0,1:T(8,128)(2,1)S(1)} %get-tuple-element.157), channel_id=1, source_target_pairs={{0,1},{1,2},{2,3},{3,0},{4,5},{5,6},{6,7},{7,4},{8,9},{9,10},{10,1... | collective-permute-start | bytes 3992 | tf_op jit(solution)/shard_map/ppermute | solution.py:16
  15.0 6.6 %collective-permute-start.1 = (bf16[83,8,1]{2,0,1:T(8,128)(2,1)S(1)}, bf16[83,8,1]{2,0,1:T(8,128)(2,1)S(1)}, u32[]{:S(2)}, u32[]{:S(2)}) collective-permute-start(bf16[83,8,1]{2,0,1:T(8,128)(2,1)S(1)} %get-tuple-element.158), channel_id=1, source_target_pairs={{1,0},{2,1},{3,2},{0,3},{5,4},{6,5},{7,6},{4,7},{9,8},{10,9},{11,1... | collective-permute-start | bytes 3992 | tf_op jit(solution)/shard_map/ppermute | solution.py:19
  21.8 5.2 %collective-permute-start.2 = (bf16[83,1,130]{2,0,1:T(8,128)(2,1)S(1)}, bf16[83,1,130]{2,0,1:T(8,128)(2,1)S(1)}, u32[]{:S(2)}, u32[]{:S(2)}) collective-permute-start(bf16[83,1,130]{2,0,1:T(8,128)(2,1)S(1)} %get-tuple-element.122), channel_id=1, source_target_pairs={{0,4},{4,8},{8,12},{1,5},{5,9},{9,13},{2,6},{6,10},{10,14},{3,7},{... | collective-permute-start | bytes 64748 | tf_op jit(solution)/shard_map/ppermute | solution.py:16
  24.7 4.8 %collective-permute-start.3 = (bf16[83,1,130]{2,0,1:T(8,128)(2,1)S(1)}, bf16[83,1,130]{2,0,1:T(8,128)(2,1)S(1)}, u32[]{:S(2)}, u32[]{:S(2)}) collective-permute-start(bf16[83,1,130]{2,0,1:T(8,128)(2,1)S(1)} %get-tuple-element.121), channel_id=1, source_target_pairs={{4,0},{8,4},{12,8},{5,1},{9,5},{13,9},{6,2},{10,6},{14,10},{7,3},{... | collective-permute-start | bytes 64748 | tf_op jit(solution)/shard_map/ppermute | solution.py:19
  35.4 11.5 %collective-permute-start.4 = (bf16[192,8,1]{2,0,1:T(8,128)(2,1)S(1)}, bf16[192,8,1]{2,0,1:T(8,128)(2,1)S(1)}, u32[]{:S(2)}, u32[]{:S(2)}) collective-permute-start(bf16[192,8,1]{2,0,1:T(8,128)(2,1)S(1)} %get-tuple-element.135), channel_id=1, source_target_pairs={{0,1},{1,2},{2,3},{3,0},{4,5},{5,6},{6,7},{7,4},{8,9},{9,10},{10,1... | collective-permute-start | bytes 9224 | tf_op jit(solution)/shard_map/ppermute | solution.py:16
  38.3 9.2 %collective-permute-start.5 = (bf16[192,8,1]{2,0,1:T(8,128)(2,1)S(1)}, bf16[192,8,1]{2,0,1:T(8,128)(2,1)S(1)}, u32[]{:S(2)}, u32[]{:S(2)}) collective-permute-start(bf16[192,8,1]{2,0,1:T(8,128)(2,1)S(1)} %get-tuple-element.136), channel_id=1, source_target_pairs={{1,0},{2,1},{3,2},{0,3},{5,4},{6,5},{7,6},{4,7},{9,8},{10,9},{11,1... | collective-permute-start | bytes 9224 | tf_op jit(solution)/shard_map/ppermute | solution.py:19
  38.5 22.5 %copy-start.13 = (f32[11,8,8,128]{3,1,2,0:T(8,128)}, f32[11,8,8,128]{3,1,2,0:T(8,128)S(1)}, u32[]{:S(2)}) copy-start(f32[11,8,8,128]{3,1,2,0:T(8,128)S(1)} %copy.185) | copy-start | bytes 1081348
  46.9 9.8 %copy-start.4 = (bf16[192,8,1]{2,0,1:T(8,128)(2,1)}, bf16[192,8,1]{2,0,1:T(8,128)(2,1)S(1)}, u32[]{:S(2)}) copy-start(bf16[192,8,1]{2,0,1:T(8,128)(2,1)S(1)} %collective-permute-done.4) | copy-start | bytes 9220
  47.5 9.2 %copy-start.2 = (bf16[192,8,1]{2,0,1:T(8,128)(2,1)}, bf16[192,8,1]{2,0,1:T(8,128)(2,1)S(1)}, u32[]{:S(2)}) copy-start(bf16[192,8,1]{2,0,1:T(8,128)(2,1)S(1)} %collective-permute-done.5) | copy-start | bytes 9220
  47.6 5.3 %collective-permute-start.6 = (bf16[192,1,130]{2,0,1:T(8,128)(2,1)S(1)}, bf16[192,1,130]{2,0,1:T(8,128)(2,1)S(1)}, u32[]{:S(2)}, u32[]{:S(2)}) collective-permute-start(bf16[192,1,130]{2,0,1:T(8,128)(2,1)S(1)} %get-tuple-element.104), channel_id=1, source_target_pairs={{0,4},{4,8},{8,12},{1,5},{5,9},{9,13},{2,6},{6,10},{10,14},{3,7},{... | collective-permute-start | bytes 149768 | tf_op jit(solution)/shard_map/ppermute | solution.py:16
  50.8 5.9 %collective-permute-start.7 = (bf16[192,1,130]{2,0,1:T(8,128)(2,1)S(1)}, bf16[192,1,130]{2,0,1:T(8,128)(2,1)S(1)}, u32[]{:S(2)}, u32[]{:S(2)}) collective-permute-start(bf16[192,1,130]{2,0,1:T(8,128)(2,1)S(1)} %get-tuple-element.103), channel_id=1, source_target_pairs={{4,0},{8,4},{12,8},{5,1},{9,5},{13,9},{6,2},{10,6},{14,10},{7,3},{... | collective-permute-start | bytes 149768 | tf_op jit(solution)/shard_map/ppermute | solution.py:19
  62.2 22.6 %all-to-all-start = ((f32[83,1,1024]{0,1,2:T(1,128)}), f32[83,1,1024]{0,1,2:T(1,128)S(1)}, u32[]{:S(2)}, u32[]{:S(2)}) async-start(f32[83,1,1024]{0,1,2:T(1,128)} %copy.111), calls=%async_computation | async-start | bytes 1048576 | tf_op jit(solution)/shard_map/all_to_all | solution.py:108
  71.2 338.3 %all-reduce.3.cloned.1.call-start = ((), (), s32[]{:S(2)}) async-start(), calls=%async_computation.2 | async-start | bytes 3244032 | tf_op jit(solution)/shard_map/psum | solution.py:146
  90.7 19.2 %copy-start.1 = (bf16[192,9,130]{2,0,1:T(8,128)(2,1)S(1)}, bf16[192,9,130]{2,0,1:T(8,128)(2,1)}, u32[]{:S(2)}) copy-start(bf16[192,9,130]{2,0,1:T(8,128)(2,1)} %copy-done) | copy-start | bytes 1347844
  110.6 8.1 %copy-start.5 = (bf16[192,8,1]{2,0,1:T(8,128)(2,1)S(1)}, bf16[192,8,1]{2,0,1:T(8,128)(2,1)}, u32[]{:S(2)}) copy-start(bf16[192,8,1]{2,0,1:T(8,128)(2,1)} %copy-done.4) | copy-start | bytes 9220
  111.0 9.9 %collective-permute-start.8 = (bf16[83,8,1]{0,2,1:T(2,128)(2,1)S(1)}, bf16[83,8,1]{0,2,1:T(2,128)(2,1)S(1)}, u32[]{:S(2)}, u32[]{:S(2)}) collective-permute-start(bf16[83,8,1]{0,2,1:T(2,128)(2,1)S(1)} %get-tuple-element.153), channel_id=1, source_target_pairs={{0,1},{1,2},{2,3},{3,0},{4,5},{5,6},{6,7},{7,4},{8,9},{9,10},{10,1... | collective-permute-start | bytes 3992 | tf_op jit(solution)/shard_map/ppermute | solution.py:16
  116.7 4.5 %collective-permute-start.9 = (bf16[83,8,1]{0,2,1:T(2,128)(2,1)S(1)}, bf16[83,8,1]{0,2,1:T(2,128)(2,1)S(1)}, u32[]{:S(2)}, u32[]{:S(2)}) collective-permute-start(bf16[83,8,1]{0,2,1:T(2,128)(2,1)S(1)} %get-tuple-element.154), channel_id=1, source_target_pairs={{1,0},{2,1},{3,2},{0,3},{5,4},{6,5},{7,6},{4,7},{9,8},{10,9},{11,1... | collective-permute-start | bytes 3992 | tf_op jit(solution)/shard_map/ppermute | solution.py:19
  121.3 5.5 %collective-permute-start.10 = (bf16[83,1,130]{0,2,1:T(8,128)(2,1)S(1)}, bf16[83,1,130]{0,2,1:T(8,128)(2,1)S(1)}, u32[]{:S(2)}, u32[]{:S(2)}) collective-permute-start(bf16[83,1,130]{0,2,1:T(8,128)(2,1)S(1)} %get-tuple-element.149), channel_id=1, source_target_pairs={{4,0},{8,4},{12,8},{5,1},{9,5},{13,9},{6,2},{10,6},{14,10},{7,3},{... | collective-permute-start | bytes 64748 | tf_op jit(solution)/shard_map/ppermute | solution.py:19
  122.6 5.0 %collective-permute-start.11 = (bf16[83,1,130]{0,2,1:T(8,128)(2,1)S(1)}, bf16[83,1,130]{0,2,1:T(8,128)(2,1)S(1)}, u32[]{:S(2)}, u32[]{:S(2)}) collective-permute-start(bf16[83,1,130]{0,2,1:T(8,128)(2,1)S(1)} %get-tuple-element.150), channel_id=1, source_target_pairs={{0,4},{4,8},{8,12},{1,5},{5,9},{9,13},{2,6},{6,10},{10,14},{3,7},{... | collective-permute-start | bytes 64748 | tf_op jit(solution)/shard_map/ppermute | solution.py:16
  132.8 10.7 %copy-start.20 = (bf16[192,1024]{1,0:T(8,128)(2,1)}, bf16[192,1024]{1,0:T(8,128)(2,1)S(1)}, u32[]{:S(2)}) copy-start(bf16[192,1024]{1,0:T(8,128)(2,1)S(1)} %get-tuple-element.118) | copy-start | bytes 1179652
  134.9 1.9 copy-start.3
  139.8 2.9 copy-start.19
  140.8 2.8 copy-start.28
  142.6 2.7 copy-start.10
  147.2 12.7 %collective-permute-start.12 = (bf16[192,8,1]{2,0,1:T(8,128)(2,1)}, bf16[192,8,1]{2,0,1:T(8,128)(2,1)S(1)}, u32[]{:S(2)}, u32[]{:S(2)}) collective-permute-start(bf16[192,8,1]{2,0,1:T(8,128)(2,1)} %get-tuple-element.131), channel_id=1, source_target_pairs={{0,1},{1,2},{2,3},{3,0},{4,5},{5,6},{6,7},{7,4},{8,9},{9,10},{10,1... | collective-permute-start | bytes 9224 | tf_op jit(solution)/shard_map/ppermute | solution.py:16
  151.2 9.9 %collective-permute-start.13 = (bf16[192,8,1]{2,0,1:T(8,128)(2,1)S(1)}, bf16[192,8,1]{2,0,1:T(8,128)(2,1)S(1)}, u32[]{:S(2)}, u32[]{:S(2)}) collective-permute-start(bf16[192,8,1]{2,0,1:T(8,128)(2,1)S(1)} %get-tuple-element.132), channel_id=1, source_target_pairs={{1,0},{2,1},{3,2},{0,3},{5,4},{6,5},{7,6},{4,7},{9,8},{10,9},{11,1... | collective-permute-start | bytes 9224 | tf_op jit(solution)/shard_map/ppermute | solution.py:19
  161.3 7.2 %collective-permute-start.14 = (bf16[192,1,130]{2,0,1:T(8,128)(2,1)S(1)}, bf16[192,1,130]{2,0,1:T(8,128)(2,1)S(1)}, u32[]{:S(2)}, u32[]{:S(2)}) collective-permute-start(bf16[192,1,130]{2,0,1:T(8,128)(2,1)S(1)} %get-tuple-element.100), channel_id=1, source_target_pairs={{4,0},{8,4},{12,8},{5,1},{9,5},{13,9},{6,2},{10,6},{14,10},{7,3},{... | collective-permute-start | bytes 149768 | tf_op jit(solution)/shard_map/ppermute | solution.py:19
  162.6 7.1 %collective-permute-start.15 = (bf16[192,1,130]{2,0,1:T(8,128)(2,1)S(1)}, bf16[192,1,130]{2,0,1:T(8,128)(2,1)S(1)}, u32[]{:S(2)}, u32[]{:S(2)}) collective-permute-start(bf16[192,1,130]{2,0,1:T(8,128)(2,1)S(1)} %get-tuple-element.99), channel_id=1, source_target_pairs={{0,4},{4,8},{8,12},{1,5},{5,9},{9,13},{2,6},{6,10},{10,14},{3,7},{... | collective-permute-start | bytes 149768 | tf_op jit(solution)/shard_map/ppermute | solution.py:16
  409.5 2.2 copy-start.25
  (16 other events, 15.5 us)
Sparse Core Ops, SparseCore 0:
  152.3 257.1 all-reduce.2
where the time goes:
time: 422 us; the launch traced here: 419 us
  waiting for transfers between devices  277 us (66%)
  starting transfers between devices  46.3 us (11%)
  matrix products  25.5 us (6%)
  blocking collectives  19.2 us (5%)
  local copies, waits for them, and re-layouts  18.2 us (4%)
  other arithmetic  17.4 us (4%)
  between operations  15.1 us (4%)
    psum x1, waiting for transfers between devices, on_device(): grad_in, grad_out = lax.psum((grad_in, grad_out), ('member', 'lat', 'lon'))  233 us
    ppermute x8, starting transfers between devices, extended(): lax.ppermute(lax.slice_in_dim(block, block.shape[dim] - width, None, axis...  31.9 us
    ppermute x8, waiting for transfers between devices, extended(): lax.ppermute(lax.slice_in_dim(block, block.shape[dim] - width, None, axis...  20 us
    all_to_all x1, blocking collectives, on_device(): lax.all_to_all(local_grad, 'member', split_axis=1, concat_axis=2, tiled=T...  19.2 us
    dot_general x18, matrix products, weight_grad(): jnp.dot(flat_grad, window_cells(padded, offset // 3, offset % 3, block_he...  14.6 us
    ppermute x8, waiting for transfers between devices, extended(): lax.ppermute(lax.slice_in_dim(block, 0, width, axis=dim), axis, backward)  13.4 us
    unnamed x87, local copies, waits for them, and re-layouts  11.3 us
    all_to_all x1, waiting for transfers between devices, on_device(): lax.all_to_all(location_vector[:, None, :], 'member', split_axis=2, conca...  10.7 us
  transfers between devices with their start and end apart: 18, of which 15 were waited for; matrix products, arithmetic and copies ran while one was open for 3% of the time, Pallas kernels for 0%

commit v1 on v0

--- a/solution.py
+++ b/solution.py
@@ -74,6 +74,45 @@
             )
         )
     return jnp.stack(terms)
+
+
+def summed_everywhere(grad_in, grad_out):
+    tail = grad_out.shape[2] - 128
+    rows_in = jnp.swapaxes(grad_in, 1, 2).reshape(-1, grad_in.shape[1])
+    rows_out = grad_out.reshape(-1, grad_out.shape[2])
+    count = rows_in.shape[0]
+    packed = jnp.concatenate(
+        [
+            rows_in[:, :128],
+            rows_out[:, :128],
+            jnp.concatenate([rows_in[:, 128:], rows_out[:, 128:]], axis=1),
+        ]
+    )
+    places = lax.axis_size("lat") * lax.axis_size("lon")
+    members = lax.axis_size("member")
+    height = -(-packed.shape[0] // (places * 16)) * 16
+    packed = jnp.pad(packed, ((0, places * height - packed.shape[0]), (0, 0)))
+    sent = packed.reshape(places, height, 128).astype(jnp.bfloat16)
+
+    def swap(values, axes):
+        return lax.all_to_all(values, axes, split_axis=0, concat_axis=0, tiled=True)
+
+    def total(values):
+        return jnp.sum(values.astype(jnp.float32), axis=0).astype(jnp.bfloat16)
+
+    def everywhere(values, copies):
+        return jnp.broadcast_to(values[None], (copies,) + values.shape)
+
+    own = total(swap(sent, ("lat", "lon")))
+    own = total(swap(everywhere(own, members), ("member",)))
+    whole = swap(everywhere(own, places), ("lat", "lon")).reshape(-1, 128).astype(jnp.float32)
+    shared = whole[2 * count : 3 * count]
+    full_in = jnp.concatenate([whole[:count], shared[:, :tail]], axis=1)
+    full_out = jnp.concatenate([whole[count : 2 * count], shared[:, tail:]], axis=1)
+    return (
+        jnp.swapaxes(full_in.reshape(9, -1, full_in.shape[1]), 1, 2),
+        full_out.reshape(grad_out.shape),
+    )
 
 
 def with_rims(values, rim_width):
@@ -143,7 +182,7 @@
     ).astype(jnp.bfloat16)[None]
     grad_out = weight_grad(truncated_sensitivity, padded_hidden, block_height, block_breadth)
     grad_in = weight_grad(grad_pre, normed_pad, block_height, block_breadth)
-    grad_in, grad_out = lax.psum((grad_in, grad_out), ("member", "lat", "lon"))
+    grad_in, grad_out = summed_everywhere(grad_in, grad_out)
     total_cells = (
         members * block_height * lax.axis_size("lat") * block_breadth * lax.axis_size("lon")
     )

time: 422 us -> 217 us (0.51)
  waiting for transfers between devices: 277 us -> 63.3 us
  starting transfers between devices: 46.3 us -> 67.4 us
  between operations: 15.1 us -> 1.91 us
  local copies, waits for them, and re-layouts: 18.2 us -> 25.1 us
    psum x1 -> x0, waiting for transfers between devices: 233 us -> none  [on_device(): grad_in, grad_out = lax.psum((grad_in, grad_out), ('member', 'lat', 'lon'))]
    all_to_all x0 -> x3, waiting for transfers between devices: none -> 24 us  [swap(): return lax.all_to_all(values, axes, split_axis=0, concat_axis=0, tiled=True)]
    all_to_all x0 -> x3, starting transfers between devices: none -> 22.4 us  [swap(): return lax.all_to_all(values, axes, split_axis=0, concat_axis=0, tiled=True)]
    ppermute x8, waiting for transfers between devices: 20 us -> 11.8 us  [extended(): lax.ppermute(lax.slice_in_dim(block, block.shape[dim] - width, None, axis...]
    unnamed x87 -> x89, local copies, waits for them, and re-layouts: 11.3 us -> 9.06 us
  transfers between devices with their start and end apart: 18 -> 20, of which waited for: 15 -> 13; matrix products, arithmetic and copies ran while one was open for 3% -> 7% of each run, Pallas kernels for 0% -> 0%
where the time goes in v1:
time: 217 us; the launch traced here: 216 us
  starting transfers between devices  67.4 us (31%)
  waiting for transfers between devices  63.3 us (29%)
  local copies, waits for them, and re-layouts  25.1 us (12%)
  matrix products  23.8 us (11%)
  blocking collectives  19.2 us (9%)
  other arithmetic  14.8 us (7%)
    ppermute x8, starting transfers between devices, extended(): lax.ppermute(lax.slice_in_dim(block, block.shape[dim] - width, None, axis...  30.8 us
    all_to_all x3, waiting for transfers between devices, swap(): return lax.all_to_all(values, axes, split_axis=0, concat_axis=0, tiled=True)  24 us
    all_to_all x3, starting transfers between devices, swap(): return lax.all_to_all(values, axes, split_axis=0, concat_axis=0, tiled=True)  22.4 us
    all_to_all x1, blocking collectives, on_device(): lax.all_to_all(local_grad, 'member', split_axis=1, concat_axis=2, tiled=T...  19.2 us
    ppermute x8, waiting for transfers between devices, extended(): lax.ppermute(lax.slice_in_dim(block, 0, width, axis=dim), axis, backward)  16.6 us
    dot_general x18, matrix products, weight_grad(): jnp.dot(flat_grad, window_cells(padded, offset // 3, offset % 3, block_he...  12.8 us
    ppermute x8, waiting for transfers between devices, extended(): lax.ppermute(lax.slice_in_dim(block, block.shape[dim] - width, None, axis...  11.8 us
    all_to_all x1, waiting for transfers between devices, on_device(): lax.all_to_all(location_vector[:, None, :], 'member', split_axis=2, conca...  10.9 us
  transfers between devices with their start and end apart: 20, of which 13 were waited for; matrix products, arithmetic and copies ran while one was open for 7% of the time, Pallas kernels for 0%

profile of v1, /device:TPU:1, one launch (start us, length us, event | category | flops | bytes accessed | tf_op | source)
XLA Modules:
  0.0 216.1 jit_solution(8913462142754766427)
XLA Ops:
  4.1 4.4 %collective-permute-start = (bf16[83,8,1]{2,0,1:T(8,128)(2,1)S(1)}, bf16[83,8,1]{2,0,1:T(8,128)(2,1)S(1)}, u32[]{:S(2)}, u32[]{:S(2)}) collective-permute-start(bf16[83,8,1]{2,0,1:T(8,128)(2,1)S(1)} %get-tuple-element.162), channel_id=1, source_target_pairs={{0,1},{1,2},{2,3},{3,0},{4,5},{5,6},{6,7},{7,4},{8,9},{9,10},{10,1... | collective-permute-start | bytes 3992 | tf_op jit(solution)/shard_map/ppermute | solution.py:16
  8.7 2.2 %collective-permute-done = bf16[83,8,1]{2,0,1:T(8,128)(2,1)S(1)} collective-permute-done((bf16[83,8,1]{2,0,1:T(8,128)(2,1)S(1)}, bf16[83,8,1]{2,0,1:T(8,128)(2,1)S(1)}, u32[]{:S(2)}, u32[]{:S(2)}) %collective-permute-start) | collective-permute-done | bytes 1360 | tf_op jit(solution)/shard_map/ppermute | solution.py:16
  10.9 4.2 %collective-permute-done.1 = bf16[83,8,1]{2,0,1:T(8,128)(2,1)S(1)} collective-permute-done((bf16[83,8,1]{2,0,1:T(8,128)(2,1)S(1)}, bf16[83,8,1]{2,0,1:T(8,128)(2,1)S(1)}, u32[]{:S(2)}, u32[]{:S(2)}) %collective-permute-start.1) | collective-permute-done | bytes 1360 | tf_op jit(solution)/shard_map/ppermute | solution.py:19
  15.2 2.9 %collective-permute-start.2 = (bf16[83,1,130]{2,0,1:T(8,128)(2,1)S(1)}, bf16[83,1,130]{2,0,1:T(8,128)(2,1)S(1)}, u32[]{:S(2)}, u32[]{:S(2)}) collective-permute-start(bf16[83,1,130]{2,0,1:T(8,128)(2,1)S(1)} %get-tuple-element.127), channel_id=1, source_target_pairs={{0,4},{4,8},{8,12},{1,5},{5,9},{9,13},{2,6},{6,10},{10,14},{3,7},{... | collective-permute-start | bytes 64748 | tf_op jit(solution)/shard_map/ppermute | solution.py:16
  18.2 1.3 collective-permute-start.3
  20.4 2.6 %collective-permute-done.3 = bf16[83,1,130]{2,0,1:T(8,128)(2,1)S(1)} collective-permute-done((bf16[83,1,130]{2,0,1:T(8,128)(2,1)S(1)}, bf16[83,1,130]{2,0,1:T(8,128)(2,1)S(1)}, u32[]{:S(2)}, u32[]{:S(2)}) %collective-permute-start.3) | collective-permute-done | bytes 21612 | tf_op jit(solution)/shard_map/ppermute | solution.py:19
  28.8 2.9 %collective-permute-start.4 = (bf16[192,8,1]{2,0,1:T(8,128)(2,1)S(1)}, bf16[192,8,1]{2,0,1:T(8,128)(2,1)S(1)}, u32[]{:S(2)}, u32[]{:S(2)}) collective-permute-start(bf16[192,8,1]{2,0,1:T(8,128)(2,1)S(1)} %get-tuple-element.140), channel_id=1, source_target_pairs={{0,1},{1,2},{2,3},{3,0},{4,5},{5,6},{6,7},{7,4},{8,9},{9,10},{10,1... | collective-permute-start | bytes 9224 | tf_op jit(solution)/shard_map/ppermute | solution.py:16
  31.8 8.4 %collective-permute-done.4 = bf16[192,8,1]{2,0,1:T(8,128)(2,1)S(1)} collective-permute-done((bf16[192,8,1]{2,0,1:T(8,128)(2,1)S(1)}, bf16[192,8,1]{2,0,1:T(8,128)(2,1)S(1)}, u32[]{:S(2)}, u32[]{:S(2)}) %collective-permute-start.4) | collective-permute-done | bytes 3104 | tf_op jit(solution)/shard_map/ppermute | solution.py:16
  41.0 3.2 %collective-permute-start.6 = (bf16[192,1,130]{2,0,1:T(8,128)(2,1)S(1)}, bf16[192,1,130]{2,0,1:T(8,128)(2,1)S(1)}, u32[]{:S(2)}, u32[]{:S(2)}) collective-permute-start(bf16[192,1,130]{2,0,1:T(8,128)(2,1)S(1)} %get-tuple-element.109), channel_id=1, source_target_pairs={{0,4},{4,8},{8,12},{1,5},{5,9},{9,13},{2,6},{6,10},{10,14},{3,7},{... | collective-permute-start | bytes 149768 | tf_op jit(solution)/shard_map/ppermute | solution.py:16
  44.2 1.3 collective-permute-start.7
  46.3 3.8 %collective-permute-done.7 = bf16[192,1,130]{2,0,1:T(8,128)(2,1)S(1)} collective-permute-done((bf16[192,1,130]{2,0,1:T(8,128)(2,1)S(1)}, bf16[192,1,130]{2,0,1:T(8,128)(2,1)S(1)}, u32[]{:S(2)}, u32[]{:S(2)}) %collective-permute-start.7) | collective-permute-done | bytes 49952 | tf_op jit(solution)/shard_map/ppermute | solution.py:19
  55.6 9.0 %all-to-all-start = ((f32[83,1,1024]{0,1,2:T(1,128)}), f32[83,1,1024]{0,1,2:T(1,128)S(1)}, u32[]{:S(2)}, u32[]{:S(2)}) async-start(f32[83,1,1024]{0,1,2:T(1,128)} %copy.172), calls=%async_computation | async-start | bytes 1048576 | tf_op jit(solution)/shard_map/all_to_all | solution.py:147
  64.6 1.9 copy.217
  67.3 10.9 %all-to-all-done = f32[83,1,1024]{0,1,2:T(1,128)S(1)} async-done(((f32[83,1,1024]{0,1,2:T(1,128)}), f32[83,1,1024]{0,1,2:T(1,128)S(1)}, u32[]{:S(2)}, u32[]{:S(2)}) %all-to-all-start) | async-done | bytes 340000 | tf_op jit(solution)/shard_map/all_to_all | solution.py:147
  78.2 5.7 %while.14 = (s32[]{:T(128)}, f32[83,16,64]{0,2,1:T(8,128)S(1)}, f32[83,16,64]{0,2,1:T(8,128)S(1)}, s32[]{:T(128)}, s32[]{:T(128)}) while((s32[]{:T(128)}, f32[83,16,64]{0,2,1:T(8,128)S(1)}, f32[83,16,64]{0,2,1:T(8,128)S(1)}, s32[]{:T(128)}, s32[]{:T(128)}) %tuple.85), condition=%wide.region_3.0_spmd.clone, body=%wide.region_2.0_spmd.clone.sunk | while | flops 509955 | bytes 1083723 | solution.py:158
  84.0 19.2 %all_to_all.36 = f32[83,16,64]{0,2,1:T(8,128)S(1)} all-to-all(f32[83,16,64]{0,2,1:T(8,128)S(1)} %multiply_subtract_fusion), channel_id=1, replica_groups=mesh['member'=16,'lat'=4,'lon'=4] {'member'}, dimensions={1} | all-to-all | bytes 679936 | tf_op jit(solution)/shard_map/all_to_all | solution.py:162
  106.2 5.6 %collective-permute-start.8 = (bf16[83,8,1]{0,2,1:T(2,128)(2,1)S(1)}, bf16[83,8,1]{0,2,1:T(2,128)(2,1)S(1)}, u32[]{:S(2)}, u32[]{:S(2)}) collective-permute-start(bf16[83,8,1]{0,2,1:T(2,128)(2,1)S(1)} %get-tuple-element.158), channel_id=1, source_target_pairs={{0,1},{1,2},{2,3},{3,0},{4,5},{5,6},{6,7},{7,4},{8,9},{9,10},{10,1... | collective-permute-start | bytes 3992 | tf_op jit(solution)/shard_map/ppermute | solution.py:16
  111.9 2.0 fusion.111
  116.4 1.3 collective-permute-start.10
  117.7 4.0 %collective-permute-start.11 = (bf16[83,1,130]{0,2,1:T(8,128)(2,1)S(1)}, bf16[83,1,130]{0,2,1:T(8,128)(2,1)S(1)}, u32[]{:S(2)}, u32[]{:S(2)}) collective-permute-start(bf16[83,1,130]{0,2,1:T(8,128)(2,1)S(1)} %get-tuple-element.155), channel_id=1, source_target_pairs={{0,4},{4,8},{8,12},{1,5},{5,9},{9,13},{2,6},{6,10},{10,14},{3,7},{... | collective-permute-start | bytes 64748 | tf_op jit(solution)/shard_map/ppermute | solution.py:16
  127.7 1.8 fusion.22
  139.9 1.2 reshape.322
  141.2 3.8 %collective-permute-start.12 = (bf16[192,8,1]{2,0,1:T(8,128)(2,1)}, bf16[192,8,1]{2,0,1:T(8,128)(2,1)S(1)}, u32[]{:S(2)}, u32[]{:S(2)}) collective-permute-start(bf16[192,8,1]{2,0,1:T(8,128)(2,1)} %get-tuple-element.136), channel_id=1, source_target_pairs={{0,1},{1,2},{2,3},{3,0},{4,5},{5,6},{6,7},{7,4},{8,9},{9,10},{10,1... | collective-permute-start | bytes 9224 | tf_op jit(solution)/shard_map/ppermute | solution.py:16
  145.2 1.8 concatenate.115
  147.8 8.2 %all-to-all-start.2 = ((bf16[16,144,128]{2,1,0:T(8,128)(2,1)}), bf16[16,144,128]{2,1,0:T(8,128)(2,1)S(1)}, u32[]{:S(2)}, u32[]{:S(2)}) async-start(bf16[16,144,128]{2,1,0:T(8,128)(2,1)} %bitcast.79), calls=%async_computation.2 | async-start | bytes 1179648 | tf_op jit(solution)/shard_map/all_to_all | solution.py:98
  156.2 1.3 collective-permute-start.14
  157.5 4.0 %collective-permute-start.15 = (bf16[192,1,130]{2,0,1:T(8,128)(2,1)S(1)}, bf16[192,1,130]{2,0,1:T(8,128)(2,1)S(1)}, u32[]{:S(2)}, u32[]{:S(2)}) collective-permute-start(bf16[192,1,130]{2,0,1:T(8,128)(2,1)S(1)} %get-tuple-element.104), channel_id=1, source_target_pairs={{0,4},{4,8},{8,12},{1,5},{5,9},{9,13},{2,6},{6,10},{10,14},{3,7},{... | collective-permute-start | bytes 149768 | tf_op jit(solution)/shard_map/ppermute | solution.py:16
  162.0 4.9 %collective-permute-done.14 = bf16[192,1,130]{2,0,1:T(8,128)(2,1)S(1)} collective-permute-done((bf16[192,1,130]{2,0,1:T(8,128)(2,1)S(1)}, bf16[192,1,130]{2,0,1:T(8,128)(2,1)S(1)}, u32[]{:S(2)}, u32[]{:S(2)}) %collective-permute-start.14) | collective-permute-done | bytes 49952 | tf_op jit(solution)/shard_map/ppermute | solution.py:19
  172.0 4.0 %all-to-all-start.3 = ((bf16[16,144,128]{2,1,0:T(8,128)(2,1)}), bf16[16,144,128]{2,1,0:T(8,128)(2,1)S(1)}, u32[]{:S(2)}, u32[]{:S(2)}) async-start(bf16[16,144,128]{2,1,0:T(8,128)(2,1)} %broadcast_in_dim.16), calls=%async_computation.3 | async-start | bytes 1179648 | tf_op jit(solution)/shard_map/all_to_all | solution.py:98
  177.6 13.2 %all-to-all-done.3 = bf16[16,144,128]{2,1,0:T(8,128)(2,1)S(1)} async-done(((bf16[16,144,128]{2,1,0:T(8,128)(2,1)}), bf16[16,144,128]{2,1,0:T(8,128)(2,1)S(1)}, u32[]{:S(2)}, u32[]{:S(2)}) %all-to-all-start.3) | async-done | bytes 589856 | tf_op jit(solution)/shard_map/all_to_all | solution.py:98
  191.8 10.2 %all-to-all-start.4 = ((bf16[16,144,128]{2,1,0:T(8,128)(2,1)}), bf16[16,144,128]{2,1,0:T(8,128)(2,1)S(1)}, u32[]{:S(2)}, u32[]{:S(2)}) async-start(bf16[16,144,128]{2,1,0:T(8,128)(2,1)} %broadcast_in_dim.17), calls=%async_computation.4 | async-start | bytes 1179648 | tf_op jit(solution)/shard_map/all_to_all | solution.py:98
  202.9 10.7 %all-to-all-done.4 = bf16[16,144,128]{2,1,0:T(8,128)(2,1)S(1)} async-done(((bf16[16,144,128]{2,1,0:T(8,128)(2,1)}), bf16[16,144,128]{2,1,0:T(8,128)(2,1)S(1)}, u32[]{:S(2)}, u32[]{:S(2)}) %all-to-all-start.4) | async-done | bytes 589856 | tf_op jit(solution)/shard_map/all_to_all | solution.py:98
  (258 shorter events, 57.5 us)
Async XLA Ops:
  0.6 7.9 %copy-start.7 = (bf16[1,83,8,128]{3,2,1,0:T(8,128)(2,1)S(1)}, bf16[1,83,8,128]{3,2,1,0:T(8,128)(2,1)}, u32[]{:S(2)}) copy-start(bf16[1,83,8,128]{3,2,1,0:T(8,128)(2,1)} %param.8) | copy-start | bytes 509956
  0.6 7.9 %copy-start.6 = (bf16[1,83,8,128]{3,2,1,0:T(8,128)(2,1)S(1)}, bf16[1,83,8,128]{3,2,1,0:T(8,128)(2,1)}, u32[]{:S(2)}) copy-start(bf16[1,83,8,128]{3,2,1,0:T(8,128)(2,1)} %param.9) | copy-start | bytes 509956
  0.7 7.8 %copy-start.30 = (f32[83]{0:T(128)S(1)}, f32[83]{0:T(128)}, u32[]{:S(2)}) copy-start(f32[83]{0:T(128)} %param.11) | copy-start | bytes 1000
  4.1 6.8 %collective-permute-start = (bf16[83,8,1]{2,0,1:T(8,128)(2,1)S(1)}, bf16[83,8,1]{2,0,1:T(8,128)(2,1)S(1)}, u32[]{:S(2)}, u32[]{:S(2)}) collective-permute-start(bf16[83,8,1]{2,0,1:T(8,128)(2,1)S(1)} %get-tuple-element.162), channel_id=1, source_target_pairs={{0,1},{1,2},{2,3},{3,0},{4,5},{5,6},{6,7},{7,4},{8,9},{9,10},{10,1... | collective-permute-start | bytes 3992 | tf_op jit(solution)/shard_map/ppermute | solution.py:16
  8.5 6.6 %collective-permute-start.1 = (bf16[83,8,1]{2,0,1:T(8,128)(2,1)S(1)}, bf16[83,8,1]{2,0,1:T(8,128)(2,1)S(1)}, u32[]{:S(2)}, u32[]{:S(2)}) collective-permute-start(bf16[83,8,1]{2,0,1:T(8,128)(2,1)S(1)} %get-tuple-element.163), channel_id=1, source_target_pairs={{1,0},{2,1},{3,2},{0,3},{5,4},{6,5},{7,6},{4,7},{9,8},{10,9},{11,1... | collective-permute-start | bytes 3992 | tf_op jit(solution)/shard_map/ppermute | solution.py:19
  8.6 9.5 %copy-start.26 = (bf16[1,83,8,128]{3,1,2,0:T(8,128)(2,1)}, bf16[1,83,8,128]{3,1,2,0:T(8,128)(2,1)S(1)}, u32[]{:S(2)}) copy-start(bf16[1,83,8,128]{3,1,2,0:T(8,128)(2,1)S(1)} %get-tuple-element.144) | copy-start | bytes 509956
  15.2 4.7 %collective-permute-start.2 = (bf16[83,1,130]{2,0,1:T(8,128)(2,1)S(1)}, bf16[83,1,130]{2,0,1:T(8,128)(2,1)S(1)}, u32[]{:S(2)}, u32[]{:S(2)}) collective-permute-start(bf16[83,1,130]{2,0,1:T(8,128)(2,1)S(1)} %get-tuple-element.127), channel_id=1, source_target_pairs={{0,4},{4,8},{8,12},{1,5},{5,9},{9,13},{2,6},{6,10},{10,14},{3,7},{... | collective-permute-start | bytes 64748 | tf_op jit(solution)/shard_map/ppermute | solution.py:16
  18.2 4.8 %collective-permute-start.3 = (bf16[83,1,130]{2,0,1:T(8,128)(2,1)S(1)}, bf16[83,1,130]{2,0,1:T(8,128)(2,1)S(1)}, u32[]{:S(2)}, u32[]{:S(2)}) collective-permute-start(bf16[83,1,130]{2,0,1:T(8,128)(2,1)S(1)} %get-tuple-element.126), channel_id=1, source_target_pairs={{4,0},{8,4},{12,8},{5,1},{9,5},{13,9},{6,2},{10,6},{14,10},{7,3},{... | collective-permute-start | bytes 64748 | tf_op jit(solution)/shard_map/ppermute | solution.py:19
  28.8 11.5 %collective-permute-start.4 = (bf16[192,8,1]{2,0,1:T(8,128)(2,1)S(1)}, bf16[192,8,1]{2,0,1:T(8,128)(2,1)S(1)}, u32[]{:S(2)}, u32[]{:S(2)}) collective-permute-start(bf16[192,8,1]{2,0,1:T(8,128)(2,1)S(1)} %get-tuple-element.140), channel_id=1, source_target_pairs={{0,1},{1,2},{2,3},{3,0},{4,5},{5,6},{6,7},{7,4},{8,9},{9,10},{10,1... | collective-permute-start | bytes 9224 | tf_op jit(solution)/shard_map/ppermute | solution.py:16
  31.6 9.2 %collective-permute-start.5 = (bf16[192,8,1]{2,0,1:T(8,128)(2,1)S(1)}, bf16[192,8,1]{2,0,1:T(8,128)(2,1)S(1)}, u32[]{:S(2)}, u32[]{:S(2)}) collective-permute-start(bf16[192,8,1]{2,0,1:T(8,128)(2,1)S(1)} %get-tuple-element.141), channel_id=1, source_target_pairs={{1,0},{2,1},{3,2},{0,3},{5,4},{6,5},{7,6},{4,7},{9,8},{10,9},{11,1... | collective-permute-start | bytes 9224 | tf_op jit(solution)/shard_map/ppermute | solution.py:19
  31.8 22.5 %copy-start.13 = (f32[11,8,8,128]{3,1,2,0:T(8,128)}, f32[11,8,8,128]{3,1,2,0:T(8,128)S(1)}, u32[]{:S(2)}) copy-start(f32[11,8,8,128]{3,1,2,0:T(8,128)S(1)} %copy.246) | copy-start | bytes 1081348
  40.2 9.9 %copy-start.4 = (bf16[192,8,1]{2,0,1:T(8,128)(2,1)}, bf16[192,8,1]{2,0,1:T(8,128)(2,1)S(1)}, u32[]{:S(2)}) copy-start(bf16[192,8,1]{2,0,1:T(8,128)(2,1)S(1)} %collective-permute-done.4) | copy-start | bytes 9220
  40.9 9.2 %copy-start.2 = (bf16[192,8,1]{2,0,1:T(8,128)(2,1)}, bf16[192,8,1]{2,0,1:T(8,128)(2,1)S(1)}, u32[]{:S(2)}) copy-start(bf16[192,8,1]{2,0,1:T(8,128)(2,1)S(1)} %collective-permute-done.5) | copy-start | bytes 9220
  41.0 5.3 %collective-permute-start.6 = (bf16[192,1,130]{2,0,1:T(8,128)(2,1)S(1)}, bf16[192,1,130]{2,0,1:T(8,128)(2,1)S(1)}, u32[]{:S(2)}, u32[]{:S(2)}) collective-permute-start(bf16[192,1,130]{2,0,1:T(8,128)(2,1)S(1)} %get-tuple-element.109), channel_id=1, source_target_pairs={{0,4},{4,8},{8,12},{1,5},{5,9},{9,13},{2,6},{6,10},{10,14},{3,7},{... | collective-permute-start | bytes 149768 | tf_op jit(solution)/shard_map/ppermute | solution.py:16
  44.2 5.9 %collective-permute-start.7 = (bf16[192,1,130]{2,0,1:T(8,128)(2,1)S(1)}, bf16[192,1,130]{2,0,1:T(8,128)(2,1)S(1)}, u32[]{:S(2)}, u32[]{:S(2)}) collective-permute-start(bf16[192,1,130]{2,0,1:T(8,128)(2,1)S(1)} %get-tuple-element.108), channel_id=1, source_target_pairs={{4,0},{8,4},{12,8},{5,1},{9,5},{13,9},{6,2},{10,6},{14,10},{7,3},{... | collective-permute-start | bytes 149768 | tf_op jit(solution)/shard_map/ppermute | solution.py:19
  55.6 22.6 %all-to-all-start = ((f32[83,1,1024]{0,1,2:T(1,128)}), f32[83,1,1024]{0,1,2:T(1,128)S(1)}, u32[]{:S(2)}, u32[]{:S(2)}) async-start(f32[83,1,1024]{0,1,2:T(1,128)} %copy.172), calls=%async_computation | async-start | bytes 1048576 | tf_op jit(solution)/shard_map/all_to_all | solution.py:147
  84.0 19.2 %copy-start.1 = (bf16[192,9,130]{2,0,1:T(8,128)(2,1)S(1)}, bf16[192,9,130]{2,0,1:T(8,128)(2,1)}, u32[]{:S(2)}) copy-start(bf16[192,9,130]{2,0,1:T(8,128)(2,1)} %copy-done) | copy-start | bytes 1347844
  104.2 9.6 %copy-start.5 = (bf16[192,8,1]{2,0,1:T(8,128)(2,1)S(1)}, bf16[192,8,1]{2,0,1:T(8,128)(2,1)}, u32[]{:S(2)}) copy-start(bf16[192,8,1]{2,0,1:T(8,128)(2,1)} %copy-done.4) | copy-start | bytes 9220
  106.2 9.6 %collective-permute-start.8 = (bf16[83,8,1]{0,2,1:T(2,128)(2,1)S(1)}, bf16[83,8,1]{0,2,1:T(2,128)(2,1)S(1)}, u32[]{:S(2)}, u32[]{:S(2)}) collective-permute-start(bf16[83,8,1]{0,2,1:T(2,128)(2,1)S(1)} %get-tuple-element.158), channel_id=1, source_target_pairs={{0,1},{1,2},{2,3},{3,0},{4,5},{5,6},{6,7},{7,4},{8,9},{9,10},{10,1... | collective-permute-start | bytes 3992 | tf_op jit(solution)/shard_map/ppermute | solution.py:16
  111.9 4.5 %collective-permute-start.9 = (bf16[83,8,1]{0,2,1:T(2,128)(2,1)S(1)}, bf16[83,8,1]{0,2,1:T(2,128)(2,1)S(1)}, u32[]{:S(2)}, u32[]{:S(2)}) collective-permute-start(bf16[83,8,1]{0,2,1:T(2,128)(2,1)S(1)} %get-tuple-element.159), channel_id=1, source_target_pairs={{1,0},{2,1},{3,2},{0,3},{5,4},{6,5},{7,6},{4,7},{9,8},{10,9},{11,1... | collective-permute-start | bytes 3992 | tf_op jit(solution)/shard_map/ppermute | solution.py:19
  116.4 5.5 %collective-permute-start.10 = (bf16[83,1,130]{0,2,1:T(8,128)(2,1)S(1)}, bf16[83,1,130]{0,2,1:T(8,128)(2,1)S(1)}, u32[]{:S(2)}, u32[]{:S(2)}) collective-permute-start(bf16[83,1,130]{0,2,1:T(8,128)(2,1)S(1)} %get-tuple-element.154), channel_id=1, source_target_pairs={{4,0},{8,4},{12,8},{5,1},{9,5},{13,9},{6,2},{10,6},{14,10},{7,3},{... | collective-permute-start | bytes 64748 | tf_op jit(solution)/shard_map/ppermute | solution.py:19
  117.7 5.0 %collective-permute-start.11 = (bf16[83,1,130]{0,2,1:T(8,128)(2,1)S(1)}, bf16[83,1,130]{0,2,1:T(8,128)(2,1)S(1)}, u32[]{:S(2)}, u32[]{:S(2)}) collective-permute-start(bf16[83,1,130]{0,2,1:T(8,128)(2,1)S(1)} %get-tuple-element.155), channel_id=1, source_target_pairs={{0,4},{4,8},{8,12},{1,5},{5,9},{9,13},{2,6},{6,10},{10,14},{3,7},{... | collective-permute-start | bytes 64748 | tf_op jit(solution)/shard_map/ppermute | solution.py:16
  127.2 10.4 %copy-start.20 = (bf16[192,1024]{1,0:T(8,128)(2,1)}, bf16[192,1024]{1,0:T(8,128)(2,1)S(1)}, u32[]{:S(2)}) copy-start(bf16[192,1024]{1,0:T(8,128)(2,1)S(1)} %get-tuple-element.123) | copy-start | bytes 1179652
  138.6 6.4 %slice-start = ((bf16[747,192]{1,0:T(8,128)(2,1)}), bf16[747,64]{1,0:T(8,128)(2,1)S(1)}, s32[]{:S(2)}) async-start(bf16[747,192]{1,0:T(8,128)(2,1)} %copy-done.22), calls=%async_computation.5 | async-start | bytes 385024 | tf_op jit(solution)/shard_map/slice | solution.py:88
  141.2 14.9 %collective-permute-start.12 = (bf16[192,8,1]{2,0,1:T(8,128)(2,1)}, bf16[192,8,1]{2,0,1:T(8,128)(2,1)S(1)}, u32[]{:S(2)}, u32[]{:S(2)}) collective-permute-start(bf16[192,8,1]{2,0,1:T(8,128)(2,1)} %get-tuple-element.136), channel_id=1, source_target_pairs={{0,1},{1,2},{2,3},{3,0},{4,5},{5,6},{6,7},{7,4},{8,9},{9,10},{10,1... | collective-permute-start | bytes 9224 | tf_op jit(solution)/shard_map/ppermute | solution.py:16
  145.0 11.0 %collective-permute-start.13 = (bf16[192,8,1]{2,0,1:T(8,128)(2,1)}, bf16[192,8,1]{2,0,1:T(8,128)(2,1)S(1)}, u32[]{:S(2)}, u32[]{:S(2)}) collective-permute-start(bf16[192,8,1]{2,0,1:T(8,128)(2,1)} %get-tuple-element.137), channel_id=1, source_target_pairs={{1,0},{2,1},{3,2},{0,3},{5,4},{6,5},{7,6},{4,7},{9,8},{10,9},{11,1... | collective-permute-start | bytes 9224 | tf_op jit(solution)/shard_map/ppermute | solution.py:19
  147.8 23.1 %all-to-all-start.2 = ((bf16[16,144,128]{2,1,0:T(8,128)(2,1)}), bf16[16,144,128]{2,1,0:T(8,128)(2,1)S(1)}, u32[]{:S(2)}, u32[]{:S(2)}) async-start(bf16[16,144,128]{2,1,0:T(8,128)(2,1)} %bitcast.79), calls=%async_computation.2 | async-start | bytes 1179648 | tf_op jit(solution)/shard_map/all_to_all | solution.py:98
  156.2 10.7 %collective-permute-start.14 = (bf16[192,1,130]{2,0,1:T(8,128)(2,1)S(1)}, bf16[192,1,130]{2,0,1:T(8,128)(2,1)S(1)}, u32[]{:S(2)}, u32[]{:S(2)}) collective-permute-start(bf16[192,1,130]{2,0,1:T(8,128)(2,1)S(1)} %get-tuple-element.105), channel_id=1, source_target_pairs={{4,0},{8,4},{12,8},{5,1},{9,5},{13,9},{6,2},{10,6},{14,10},{7,3},{... | collective-permute-start | bytes 149768 | tf_op jit(solution)/shard_map/ppermute | solution.py:19
  157.5 9.4 %collective-permute-start.15 = (bf16[192,1,130]{2,0,1:T(8,128)(2,1)S(1)}, bf16[192,1,130]{2,0,1:T(8,128)(2,1)S(1)}, u32[]{:S(2)}, u32[]{:S(2)}) collective-permute-start(bf16[192,1,130]{2,0,1:T(8,128)(2,1)S(1)} %get-tuple-element.104), channel_id=1, source_target_pairs={{0,4},{4,8},{8,12},{1,5},{5,9},{9,13},{2,6},{6,10},{10,14},{3,7},{... | collective-permute-start | bytes 149768 | tf_op jit(solution)/shard_map/ppermute | solution.py:16
  172.0 18.8 %all-to-all-start.3 = ((bf16[16,144,128]{2,1,0:T(8,128)(2,1)}), bf16[16,144,128]{2,1,0:T(8,128)(2,1)S(1)}, u32[]{:S(2)}, u32[]{:S(2)}) async-start(bf16[16,144,128]{2,1,0:T(8,128)(2,1)} %broadcast_in_dim.16), calls=%async_computation.3 | async-start | bytes 1179648 | tf_op jit(solution)/shard_map/all_to_all | solution.py:98
  177.6 24.5 %copy-start.25 = (f32[1,83,8,128]{3,1,2,0:T(8,128)S(1)}, f32[1,83,8,128]{3,1,2,0:T(8,128)}, u32[]{:S(2)}) copy-start(f32[1,83,8,128]{3,1,2,0:T(8,128)} %copy.195) | copy-start | bytes 1019908
  191.8 21.9 %all-to-all-start.4 = ((bf16[16,144,128]{2,1,0:T(8,128)(2,1)}), bf16[16,144,128]{2,1,0:T(8,128)(2,1)S(1)}, u32[]{:S(2)}, u32[]{:S(2)}) async-start(bf16[16,144,128]{2,1,0:T(8,128)(2,1)} %broadcast_in_dim.17), calls=%async_computation.4 | async-start | bytes 1179648 | tf_op jit(solution)/shard_map/all_to_all | solution.py:98
  (21 other events, 31.1 us)

commit v2 on v0

v2 whole, which is shorter than its diff:
```python
import functools
import math

import jax
import jax.numpy as jnp
from jax import lax
from jax.experimental import pallas as pl
from jax.experimental.pallas import tpu as pltpu
from jax.sharding import PartitionSpec as P

soft_eps = 0.01
norm_eps = 1e-05
C = 83
CP = 88
CI = 96
HID = 192
ROWS = 8
COLS = 128
RIM = 4
PITCH = COLS + 2 * RIM
TALL = ROWS + 2 * RIM
FLAT = TALL * PITCH
TILES = FLAT // 128
SPREAD = (2, 15)
HIDDEN = (3, 14)
OWN = (4, 13)
MEMBERS = 16
PLACES = 16
CHUNK = 72
PIECE = 144
f32 = jnp.float32
bf16 = jnp.bfloat16
GELU_A = math.sqrt(2.0 / math.pi)
GELU_B = 0.044715
VMEM_LIMIT = 60 * 1024 * 1024


def call(kernel, outs, scratch, *operands, smem=0):
    specs = [pl.BlockSpec(memory_space=pltpu.SMEM)] * smem
    specs += [pl.BlockSpec(memory_space=pltpu.VMEM)] * (len(operands) - smem)
    return pl.pallas_call(
        kernel,
        out_shape=[jax.ShapeDtypeStruct(shape, kind) for shape, kind in outs],
        in_specs=specs,
        out_specs=[pl.BlockSpec(memory_space=pltpu.VMEM)] * len(outs),
        scratch_shapes=[pltpu.VMEM(shape, kind) for shape, kind in scratch],
        compiler_params=pltpu.CompilerParams(vmem_limit_bytes=VMEM_LIMIT),
    )(*operands)


def step_of(offset):
    return (offset // 3 - 1) * PITCH + offset % 3 - 1


def tile(index):
    return pl.ds(128 * index, 128)


def lanes_of(height):
    return lax.broadcasted_iota(jnp.int32, (height, 128), 1)


def rows_kernel(emb_ref, pert_ref, target_ref, own_ref, up_ref, down_ref, latent, truth):
    latent[...] = emb_ref[...].astype(f32) + pert_ref[...].astype(f32)
    truth[...] = target_ref[...].astype(f32)
    rest = jnp.zeros((CP - C, 128), f32)
    for r in range(ROWS):
        for base, source, sent in ((0, latent, RIM), (ROWS, truth, RIM // 2)):
            row = jnp.concatenate([source[pl.ds(r, C, stride=ROWS), :], rest], axis=0)
            own_ref[base + r] = row
            place = 0 if base == 0 else RIM
            if r < sent:
                up_ref[place + r] = row
            if r >= ROWS - sent:
                down_ref[place + r - (ROWS - sent)] = row


def latent_row(own_ref, top_ref, bottom_ref, row):
    if row < RIM:
        return top_ref[row]
    if row < RIM + ROWS:
        return own_ref[row - RIM]
    return bottom_ref[row - RIM - ROWS]


def truth_row(own_ref, top_ref, bottom_ref, row):
    half = RIM // 2
    if row < half:
        return top_ref[RIM + row]
    if row < half + ROWS:
        return own_ref[ROWS + row - half]
    return bottom_ref[RIM + row - half - ROWS]


def columns_kernel(own_ref, top_ref, bottom_ref, left_ref, right_ref):
    lane = lanes_of(CP)
    left = jnp.zeros((CP, 128), f32)
    right = jnp.zeros((CP, 128), f32)
    plan = [(latent_row, row, RIM * row, RIM) for row in range(TALL)]
    plan += [
        (truth_row, row, RIM * TALL + RIM // 2 * row, RIM // 2) for row in range(ROWS + RIM)
    ]
    for source, row, start, width in plan:
        values = source(own_ref, top_ref, bottom_ref, row)
        here = (lane >= start) & (lane < start + width)
        left = jnp.where(here, pltpu.roll(values, start % 128, 1), left)
        right = jnp.where(here, pltpu.roll(values, (start + width) % 128, 1), right)
    left_ref[...] = left
    right_ref[...] = right


def flat_tiles(pieces, first, last):
    lane = lanes_of(CP)
    rolled = {}
    for index in range(first, last):
        result = jnp.zeros((CP, 128), f32)
        for number, (values, lane_from, flat_to, width) in enumerate(pieces):
            low, high = max(flat_to - 128 * index, 0), min(flat_to + width - 128 * index, 128)
            if low >= high:
                continue
            if number not in rolled:
                shift = (flat_to - lane_from) % 128
                rolled[number] = pltpu.roll(values(), shift, 1) if shift else values()
            result = jnp.where((lane >= low) & (lane < high), rolled[number], result)
        yield index, result


def forward_kernel(
    own_ref, top_ref, bottom_ref, left_ref, right_ref, gain_ref, valid_ref, mine_ref, w1_ref, w2_ref,
    forecast_ref, truth_ref, pre_ref, hidden_ref, window_ref, latent_ref,
    latent, normed, window, hidden, partial,
):
    pieces, truths = [], []
    for row in range(TALL):
        pieces.append((functools.partial(latent_row, own_ref, top_ref, bottom_ref, row), 0, PITCH * row + RIM, COLS))
        pieces.append((lambda: left_ref[...], RIM * row, PITCH * row, RIM))
        pieces.append((lambda: right_ref[...], RIM * row, PITCH * row + RIM + COLS, RIM))
    half = RIM // 2
    for row in range(ROWS + RIM):
        flat, lane = PITCH * (row + half) + RIM, RIM * TALL + half * row
        truths.append((functools.partial(truth_row, own_ref, top_ref, bottom_ref, row), 0, flat, COLS))
        truths.append((lambda: left_ref[...], lane, flat - half, half))
        truths.append((lambda: right_ref[...], lane, flat + COLS, half))
    real = lax.broadcasted_iota(jnp.int32, (CP, 128), 0) < C
    gain = gain_ref[...]
    normed[CP:CI, :] = jnp.zeros((CI - CP, FLAT), f32)
    for index, values in flat_tiles(pieces, 0, TILES):
        latent[:, tile(index)] = values
        average = jnp.sum(values, axis=0, keepdims=True) * (1.0 / C)
        centered = jnp.where(real, values - average, 0.0)
        variance = jnp.sum(centered * centered, axis=0, keepdims=True) * (1.0 / C)
        scaled = centered * lax.rsqrt(variance + norm_eps) * gain
        normed[0:CP, tile(index)] = scaled * valid_ref[:, tile(index)]
    for index, values in flat_tiles(truths, *SPREAD):
        truth_ref[pl.ds(CP * (index - SPREAD[0]), CP), :] = values
    truth_ref[pl.ds(CP * (SPREAD[1] - SPREAD[0]), 8), :] = jnp.zeros((8, 128), f32)
    latent_ref[...] = latent[:, 128 * OWN[0] : 128 * OWN[1]]

    for group in range(CI // 16):
        values = normed[16 * group : 16 * group + 16, :]
        for offset in range(9):
            shift = -step_of(offset) % FLAT
            moved = pltpu.roll(values, shift, 1) if shift else values
            window[CI * offset + 16 * group : CI * offset + 16 * group + 16, :] = moved.astype(bf16)
    window_ref[...] = window[:, 128 * OWN[0] : 128 * OWN[1]]

    for first, last in ((0, 3), (3, 7), (7, 11), (11, 14), (14, 17)):
        span = slice(128 * first, 128 * last)
        pre = jnp.dot(w1_ref[...], window[:, span], preferred_element_type=f32)
        if first >= HIDDEN[0] and last <= HIDDEN[1]:
            pre_ref[:, 128 * (first - HIDDEN[0]) : 128 * (last - HIDDEN[0])] = pre
        curve = jnp.tanh(GELU_A * (pre + GELU_B * (pre * pre * pre)))
        hidden[:, span] = (0.5 * pre * (1.0 + curve) * valid_ref[:, span]).astype(bf16)
        partial[:, span] = jnp.dot(w2_ref[...], hidden[:, span], preferred_element_type=f32)
    hidden_ref[...] = (hidden[:, 128 * OWN[0] : 128 * OWN[1]].astype(f32) * mine_ref[...]).astype(bf16)

    for group in range(CP // 8):
        total = None
        for offset in range(9):
            start = CP * offset + 8 * group
            shift = -step_of(offset) % FLAT
            values = partial[start : start + 8, :]
            moved = pltpu.roll(values, shift, 1) if shift else values
            total = moved if total is None else total + moved
        for index in range(*SPREAD):
            start = CP * (index - SPREAD[0]) + 8 * group
            forecast_ref[start : start + 8, :] = (
                total[:, 128 * index : 128 * index + 128] + latent[8 * group : 8 * group + 8, tile(index)]
            )
    forecast_ref[pl.ds(CP * (SPREAD[1] - SPREAD[0]), 8), :] = jnp.zeros((8, 128), f32)


def soft_slope(values):
    return values * lax.rsqrt(values * values + soft_eps)


def score_kernel(member_ref, forecast_ref, truth_ref, grad_ref, grads):
    base = member_ref[0] * CHUNK

    def body(step, carry):
        span = pl.ds(pl.multiple_of(8 * step, 8), 8)
        truth = truth_ref[pl.ds(pl.multiple_of(base + 8 * step, 8), 8), :]
        values = [forecast_ref[m, span, :] for m in range(MEMBERS)]
        totals = [jnp.zeros((8, 128), f32)] * MEMBERS
        for first in range(MEMBERS):
            for second in range(first):
                slope = soft_slope(values[first] - values[second])
                totals[first] = totals[first] + slope
                totals[second] = totals[second] - slope
        for m in range(MEMBERS):
            grads[m, span, :] = soft_slope(values[m] - truth) - totals[m] * (1.0 / (MEMBERS - 1))
        return carry

    lax.fori_loop(0, CHUNK // 8, body, 0)
    grad_ref[...] = grads[...].astype(bf16)


def backward_kernel(
    grad_ref, pre_ref, hidden_ref, window_ref, latent_ref, gain_ref, valid_ref, mine_ref, w2_ref, w1_ref,
    states_ref, weights_ref,
    chunks, grad, window, grad_pre, partial, shifted, result, packed,
):
    for m in range(MEMBERS):
        chunks[CHUNK * m : CHUNK * m + CHUNK, :] = grad_ref[m].astype(f32)
    edge = 128 * SPREAD[0]
    grad[:, 0:edge] = jnp.zeros((CI, edge), f32)
    grad[:, 128 * SPREAD[1] :] = jnp.zeros((CI, FLAT - 128 * SPREAD[1]), f32)
    grad[CP:CI, :] = jnp.zeros((CI - CP, FLAT), f32)
    for index in range(*SPREAD):
        values = chunks[CP * (index - SPREAD[0]) : CP * (index - SPREAD[0]) + CP, :]
        grad[0:CP, tile(index)] = values * valid_ref[:, tile(index)]
    low, high = 128 * HIDDEN[0], 128 * HIDDEN[1]
    for group in range(CI // 16):
        values = grad[16 * group : 16 * group + 16, :]
        for offset in range(9):
            shift = step_of(offset) % FLAT
            moved = pltpu.roll(values, shift, 1) if shift else values
            window[CI * offset + 16 * group : CI * offset + 16 * group + 16, :] = moved[:, low:high].astype(bf16)
    inner = slice(128 * (OWN[0] - HIDDEN[0]), 128 * (OWN[1] - HIDDEN[0]))
    across = (((1,), (1,)), ((), ()))
    grad_out = lax.dot_general(window[:, inner], hidden_ref[...], across, preferred_element_type=f32)
    for k in range(9):
        values = grad_out[CI * k : CI * k + C, :]
        packed[C * (9 + k) : C * (10 + k), :] = values[:, 0:128]
        packed[C * (18 + k) : C * (19 + k), 64:128] = values[:, 128:192]
    for first, last in ((0, 4), (4, 8), (8, 11)):
        span = slice(128 * first, 128 * last)
        grad_hidden = jnp.dot(w2_ref[...], window[:, span], preferred_element_type=f32)
        pre = pre_ref[:, span]
        square = pre * pre
        curve = jnp.tanh(GELU_A * (pre + GELU_B * (square * pre)))
        slope = 0.5 * (1.0 + curve) + 0.5 * pre * (1.0 - curve * curve) * (GELU_A * (1.0 + 3.0 * GELU_B * square))
        live = valid_ref[:, low + 128 * first : low + 128 * last]
        grad_pre[:, span] = (grad_hidden * slope * live).astype(bf16)
        partial[:, span] = jnp.dot(w1_ref[...], grad_pre[:, span], preferred_element_type=f32)
    own_pre = (grad_pre[:, inner].astype(f32) * mine_ref[...]).astype(bf16)
    grad_in = lax.dot_general(window_ref[...], own_pre, across, preferred_element_type=f32)
    for k in range(9):
        values = grad_in[CI * k : CI * k + C, :]
        packed[C * k : C * (k + 1), :] = values[:, 0:128]
        packed[C * (18 + k) : C * (19 + k), 0:64] = values[:, 128:192]
    packed[27 * C :, :] = jnp.zeros((PLACES * PIECE - 27 * C, 128), f32)
    for place in range(PLACES):
        weights_ref[place] = packed[PIECE * place : PIECE * place + PIECE, :].astype(bf16)

    span = high - low
    for group in range(CP // 8):
        total = None
        for offset in range(9):
            start = CP * offset + 8 * group
            shift = step_of(offset) % span
            values = partial[start : start + 8, :]
            moved = pltpu.roll(values, shift, 1) if shift else values
            total = moved if total is None else total + moved
        shifted[8 * group : 8 * group + 8, :] = total[:, inner]
    real = lax.broadcasted_iota(jnp.int32, (CP, 128), 0) < C
    gain = gain_ref[...]
    for index in range(OWN[1] - OWN[0]):
        values = latent_ref[:, tile(index)]
        average = jnp.sum(values, axis=0, keepdims=True) * (1.0 / C)
        centered = jnp.where(real, values - average, 0.0)
        variance = jnp.sum(centered * centered, axis=0, keepdims=True) * (1.0 / C)
        scale = lax.rsqrt(variance + norm_eps)
        unit = centered * scale
        pull = shifted[:, tile(index)] * gain
        mean_pull = jnp.sum(pull, axis=0, keepdims=True) * (1.0 / C)
        mean_both = jnp.sum(pull * unit, axis=0, keepdims=True) * (1.0 / C)
        shifted[:, tile(index)] = (
            grad[0:CP, tile(index + OWN[0])] + scale * (pull - mean_pull - unit * mean_both)
        )
    lane = lanes_of(CP)
    for row in range(ROWS):
        start = PITCH * (row + RIM) + RIM - 128 * OWN[0]
        index, off = divmod(start, 128)
        values = shifted[:, tile(index)]
        if off:
            near = pltpu.roll(values, 128 - off, 1)
            far = pltpu.roll(shifted[:, tile(index + 1)], 128 - off, 1)
            values = jnp.where(lane < 128 - off, near, far)
        result[pl.ds(row, C, stride=ROWS), :] = values[0:C]
    states_ref[...] = result[...].astype(bf16)


def total_kernel(parts_ref, copies_ref):
    total = parts_ref[0].astype(f32)
    for index in range(1, parts_ref.shape[0]):
        total = total + parts_ref[index].astype(f32)
    total = total.astype(bf16)
    for index in range(copies_ref.shape[0]):
        copies_ref[index] = total


def weights_kernel(parts_ref, grad_in_ref, grad_out_ref, packed):
    scale = 1.0 / math.sqrt(MEMBERS * 32 * 512)
    for place in range(PLACES):
        packed[PIECE * place : PIECE * place + PIECE, :] = parts_ref[place].astype(f32) * scale
    for k in range(9):
        first = packed[C * k : C * (k + 1), :]
        second = packed[C * (9 + k) : C * (10 + k), :]
        shared = packed[C * (18 + k) : C * (19 + k), :]
        grad_out_ref[k, :, 0:128] = second
        grad_out_ref[k, :, 128:192] = shared[:, 64:128]
        grad_in_ref[k, 0:128, :] = first.T
        grad_in_ref[k, 128:192, :] = shared[:, 0:64].T


def neighbours(axis, periodic):
    count = lax.axis_size(axis)
    forward = [(i, i + 1) for i in range(count - 1)]
    if periodic:
        forward.append((count - 1, 0))
    return forward, [(target, source) for source, target in forward]


def swap(values, axes):
    return lax.all_to_all(values, axes, split_axis=0, concat_axis=0, tiled=True)


def on_device(
    embeddings,
    entry_perturbation,
    target,
    feature_scale_factor,
    first_stencil_kernel,
    second_stencil_kernel,
):
    def rows(values):
        return values.reshape(C * ROWS, COLS)

    def padded(weight, dim, size):
        pads = [(0, 0)] * 3
        pads[dim] = (0, size - weight.shape[dim])
        return jnp.pad(weight, pads)

    own, up, down = call(
        rows_kernel,
        [((2 * ROWS, CP, 128), f32), ((RIM + RIM // 2, CP, 128), f32), ((RIM + RIM // 2, CP, 128), f32)],
        [((C * ROWS, COLS), f32)] * 2,
        rows(embeddings), rows(entry_perturbation), rows(target),
    )
    forward, backward = neighbours("lat", False)
    top = lax.ppermute(down, "lat", forward)
    bottom = lax.ppermute(up, "lat", backward)
    to_left, to_right = call(
        columns_kernel, [((CP, 128), f32)] * 2, [], own, top, bottom
    )
    forward, backward = neighbours("lon", True)
    left = lax.ppermute(to_right, "lon", forward)
    right = lax.ppermute(to_left, "lon", backward)

    gain = jnp.broadcast_to(jnp.pad(feature_scale_factor, (0, CP - C))[:, None], (CP, 128))
    place = jnp.arange(FLAT, dtype=jnp.int32)
    row, column = place // PITCH - RIM, place % PITCH - RIM
    line = row + ROWS * lax.axis_index("lat")
    valid = ((line >= 0) & (line < ROWS * lax.axis_size("lat"))).astype(f32)[None]
    mine = ((row >= 0) & (row < ROWS) & (column >= 0) & (column < COLS)).astype(f32)[None]
    mine = mine[:, 128 * OWN[0] : 128 * OWN[1]]
    w1_stack = padded(first_stencil_kernel, 2, CI).transpose(1, 0, 2).reshape(HID, 9 * CI)
    w2_stack = padded(second_stencil_kernel, 1, CP).reshape(9 * CP, HID)
    w2_turned = padded(second_stencil_kernel, 1, CI).transpose(2, 0, 1).reshape(HID, 9 * CI)
    w1_turned = padded(first_stencil_kernel.transpose(0, 2, 1), 1, CP).reshape(9 * CP, HID)

    own_lanes = 128 * (OWN[1] - OWN[0])
    hidden_lanes = 128 * (HIDDEN[1] - HIDDEN[0])
    forecast, truth, pre, hidden, window, latent = call(
        forward_kernel,
        [
            ((MEMBERS * CHUNK, 128), f32),
            ((MEMBERS * CHUNK, 128), f32),
            ((HID, hidden_lanes), f32),
            ((HID, own_lanes), bf16),
            ((9 * CI, own_lanes), bf16),
            ((CP, own_lanes), f32),
        ],
        [
            ((CP, FLAT), f32),
            ((CI, FLAT), f32),
            ((9 * CI, FLAT), bf16),
            ((HID, FLAT), bf16),
            ((9 * CP, FLAT), f32),
        ],
        own, top, bottom, left, right, gain, valid, mine, w1_stack, w2_stack,
    )
    spread = swap(forecast.reshape(MEMBERS, CHUNK, 128), "member")
    member = lax.axis_index("member").astype(jnp.int32)[None]
    (grads,) = call(
        score_kernel,
        [((MEMBERS, CHUNK, 128), bf16)],
        [((MEMBERS, CHUNK, 128), f32)],
        member, spread, truth, smem=1,
    )
    grads = swap(grads, "member")
    states, weights = call(
        backward_kernel,
        [((C * ROWS, COLS), bf16), ((PLACES, PIECE, 128), bf16)],
        [
            ((MEMBERS * CHUNK, 128), f32),
            ((CI, FLAT), f32),
            ((9 * CI, hidden_lanes), bf16),
            ((HID, hidden_lanes), bf16),
            ((9 * CP, hidden_lanes), f32),
            ((CP, own_lanes), f32),
            ((C * ROWS, COLS), f32),
            ((PLACES * PIECE, 128), f32),
        ],
        grads, pre, hidden, window, latent, gain, valid, mine, w2_turned, w1_turned,
    )
    piece = (PIECE, 128)
    (copies,) = call(total_kernel, [((MEMBERS,) + piece, bf16)], [], swap(weights, ("lat", "lon")))
    (copies,) = call(total_kernel, [((PLACES,) + piece, bf16)], [], swap(copies, "member"))
    grad_in, grad_out = call(
        weights_kernel,
        [((9, HID, C), f32), ((9, C, HID), f32)],
        [((PLACES * PIECE, 128), f32)],
        swap(copies, ("lat", "lon")),
    )
    return (states.reshape(embeddings.shape), grad_in, grad_out)


def solution(mesh):
    placed = (
        P("member", None, "lat", "lon"),
        P("member", None, "lat", "lon"),
        P(None, "lat", "lon"),
        P(),
        P(),
        P(),
    )
    return jax.shard_map(
        on_device,
        mesh=mesh,
        in_specs=placed,
        out_specs=(P("member", None, "lat", "lon"), P(), P()),
        check_vma=False,
    )
```

time: 422 us -> 162 us (0.38)
  waiting for transfers between devices: 277 us -> 33.7 us
  blocking collectives: 19.2 us -> 62.2 us
  Pallas kernels: 0 us -> 30.5 us
  matrix products: 25.5 us -> 0 us
  starting transfers between devices: 46.3 us -> 23.5 us
  other arithmetic: 17.4 us -> 1.3 us
  between operations: 15.1 us -> 0.75 us
  local copies, waits for them, and re-layouts: 18.2 us -> 9.1 us
    psum x1 -> x0, waiting for transfers between devices: 233 us -> none  [on_device(): grad_in, grad_out = lax.psum((grad_in, grad_out), ('member', 'lat', 'lon'))]
    all_to_all x1 -> x3, blocking collectives: 19.2 us -> 62.2 us  [swap(): return lax.all_to_all(values, axes, split_axis=0, concat_axis=0, tiled=True)]
    pallas_call x0 -> x8, Pallas kernels: none -> 30.5 us  [call(): pl.pallas_call(kernel, out_shape=[jax.ShapeDtypeStruct(shape, kind) for s...]
    ppermute x16 -> x4, starting transfers between devices: 37.1 us -> 10 us  [the longest x1 4.66 us: on_device(): left = lax.ppermute(to_right, 'lon', forward)]
    dot_general x54 -> x0, matrix products: 25.5 us -> none  [the longest x18 14.6 us: weight_grad(): jnp.dot(flat_grad, window_cells(padded, offset // 3, offset % 3, block_he...]
    ppermute x16 -> x4, waiting for transfers between devices: 33.4 us -> 9.81 us  [the longest x1 3.7 us: on_device(): bottom = lax.ppermute(up, 'lat', backward)]
    all_to_all x1 -> x2, waiting for transfers between devices: 10.7 us -> 23.9 us  [swap(): return lax.all_to_all(values, axes, split_axis=0, concat_axis=0, tiled=True)]
    unnamed x87 -> x19, local copies, waits for them, and re-layouts: 11.3 us -> 4.72 us
  transfers between devices with their start and end apart: 18 -> 6, of which waited for: 15 -> 5; matrix products, arithmetic and copies ran while one was open for 3% -> 3% of each run, Pallas kernels for 0% -> 0%
where the time goes in v2:
time: 162 us; the launch traced here: 161 us
  blocking collectives  62.2 us (38%)
  waiting for transfers between devices  33.7 us (21%)
  Pallas kernels  30.5 us (19%)
  starting transfers between devices  23.5 us (15%)
  local copies, waits for them, and re-layouts  9.1 us (6%)
    all_to_all x3, blocking collectives, swap(): return lax.all_to_all(values, axes, split_axis=0, concat_axis=0, tiled=True)  62.2 us
    pallas_call x8, Pallas kernels, call(): pl.pallas_call(kernel, out_shape=[jax.ShapeDtypeStruct(shape, kind) for s...  30.5 us
    all_to_all x2, waiting for transfers between devices, swap(): return lax.all_to_all(values, axes, split_axis=0, concat_axis=0, tiled=True)  23.9 us
    all_to_all x2, starting transfers between devices, swap(): return lax.all_to_all(values, axes, split_axis=0, concat_axis=0, tiled=True)  13.5 us
    unnamed x19, local copies, waits for them, and re-layouts  4.72 us
    ppermute x1, starting transfers between devices, on_device(): left = lax.ppermute(to_right, 'lon', forward)  4.66 us
    ppermute x1, starting transfers between devices, on_device(): top = lax.ppermute(down, 'lat', forward)  4.08 us
    ppermute x1, waiting for transfers between devices, on_device(): bottom = lax.ppermute(up, 'lat', backward)  3.7 us
  transfers between devices with their start and end apart: 6, of which 5 were waited for; matrix products, arithmetic and copies ran while one was open for 3% of the time, Pallas kernels for 0%

profile of v2, /device:TPU:1, one launch (start us, length us, event | category | flops | bytes accessed | tf_op | source)
XLA Modules:
  0.0 161.1 jit_solution(11207667263562910303)
XLA Ops:
  0.7 2.3 %shard_map.85 = (f32[16,88,128]{2,1,0:T(8,128)}, f32[6,88,128]{2,1,0:T(8,128)}, f32[6,88,128]{2,1,0:T(8,128)}) custom-call(bf16[664,128]{1,0:T(8,128)(2,1)} %bitcast.21, bf16[664,128]{1,0:T(8,128)(2,1)} %bitcast.22, bf16[664,128]{1,0:T(8,128)(2,1)} %bitcast.23), custom_call_target="tpu_custom_call" | custom-call | tf_op jit(solution)/shard_map/pallas_call | solution.py:41
  2.9 4.1 %collective-permute-start = (f32[6,88,128]{2,1,0:T(8,128)}, f32[6,88,128]{2,1,0:T(8,128)S(1)}, u32[]{:S(2)}, u32[]{:S(2)}) collective-permute-start(f32[6,88,128]{2,1,0:T(8,128)} %get-tuple-element.19), channel_id=1, source_target_pairs={{0,4},{4,8},{8,12},{1,5},{5,9},{9,13},{2,6},{6,10},{10,14},{3,7},{... | collective-permute-start | bytes 811016 | tf_op jit(solution)/shard_map/ppermute | solution.py:362
  7.0 1.3 collective-permute-start.1
  8.4 0.6 and_convert_fusion.1.mine_ref
  9.0 3.4 %collective-permute-done.top_ref = f32[6,88,128]{2,1,0:T(8,128)S(1)} collective-permute-done((f32[6,88,128]{2,1,0:T(8,128)}, f32[6,88,128]{2,1,0:T(8,128)S(1)}, u32[]{:S(2)}, u32[]{:S(2)}) %collective-permute-start) | collective-permute-done | bytes 270368 | tf_op jit(solution)/shard_map/ppermute | solution.py:362
  12.5 3.7 %collective-permute-done.1.bottom_ref = f32[6,88,128]{2,1,0:T(8,128)S(1)} collective-permute-done((f32[6,88,128]{2,1,0:T(8,128)}, f32[6,88,128]{2,1,0:T(8,128)S(1)}, u32[]{:S(2)}, u32[]{:S(2)}) %collective-permute-start.1) | collective-permute-done | bytes 270368 | tf_op jit(solution)/shard_map/ppermute | solution.py:363
  16.2 0.7 copy-done.5
  16.9 2.6 %shard_map.86 = (f32[88,128]{1,0:T(8,128)}, f32[88,128]{1,0:T(8,128)}) custom-call(f32[16,88,128]{2,1,0:T(8,128)} %get-tuple-element.18.own_ref, f32[6,88,128]{2,1,0:T(8,128)} %copy-done.4, f32[6,88,128]{2,1,0:T(8,128)} %copy-done.5), custom_call_target="tpu_custom_call" | custom-call | tf_op jit(solution)/shard_map/pallas_call | solution.py:41
  19.5 4.7 %collective-permute-start.2 = (f32[88,128]{1,0:T(8,128)}, f32[88,128]{1,0:T(8,128)S(1)}, u32[]{:S(2)}, u32[]{:S(2)}) collective-permute-start(f32[88,128]{1,0:T(8,128)} %get-tuple-element.21), channel_id=1, source_target_pairs={{0,1},{1,2},{2,3},{3,0},{4,5},{5,6},{6,7},{7,4},{8,9},{9,10},{10,1... | collective-permute-start | bytes 135176 | tf_op jit(solution)/shard_map/ppermute | solution.py:368
  24.1 0.6 and_convert_fusion.valid_ref
  24.9 0.9 copy.12.w1_ref
  25.8 0.8 pad.21
  26.7 2.7 %collective-permute-done.3.right_ref = f32[88,128]{1,0:T(8,128)S(1)} collective-permute-done((f32[88,128]{1,0:T(8,128)}, f32[88,128]{1,0:T(8,128)S(1)}, u32[]{:S(2)}, u32[]{:S(2)}) %collective-permute-start.3) | collective-permute-done | bytes 45088 | tf_op jit(solution)/shard_map/ppermute | solution.py:369
  29.3 0.7 broadcast_in_dim.5.gain_ref
  30.0 8.3 %shard_map.87 = (f32[1152,128]{1,0:T(8,128)}, f32[1152,128]{1,0:T(8,128)}, f32[192,1408]{1,0:T(8,128)}, bf16[192,1152]{1,0:T(8,128)(2,1)}, bf16[864,1152]{1,0:T(8,128)(2,1)}, /*index=5*/f32[88,1152]{1,0:T(8,128)}) custom-call(f32[16,88,128]{2,1,0:T(8,128)} %get-tuple-element.18.own_ref, f32[6,88,128]{2,1,0:T(8,128)} %copy-done.4, f32[6,88,128]{2,1,0:T(8,128)} %copy-done.5, ...), custom_call_target="tpu_custom_call" | custom-call | tf_op jit(solution)/shard_map/pallas_call | solution.py:41
  38.3 8.4 %all-to-all-start = ((f32[16,72,128]{2,1,0:T(8,128)}), f32[16,72,128]{2,1,0:T(8,128)S(1)}, u32[]{:S(2)}, u32[]{:S(2)}) async-start(f32[16,72,128]{2,1,0:T(8,128)} %bitcast.20), calls=%async_computation | async-start | bytes 1179648 | tf_op jit(solution)/shard_map/all_to_all | solution.py:336
  46.7 16.2 %all-to-all-done.forecast_ref = f32[16,72,128]{2,1,0:T(8,128)S(1)} async-done(((f32[16,72,128]{2,1,0:T(8,128)}), f32[16,72,128]{2,1,0:T(8,128)S(1)}, u32[]{:S(2)}, u32[]{:S(2)}) %all-to-all-start) | async-done | bytes 589856 | tf_op jit(solution)/shard_map/all_to_all | solution.py:336
  62.9 0.8 copy-done
  63.8 3.2 %shard_map.88 = bf16[16,72,128]{2,1,0:T(8,128)(2,1)} custom-call(s32[1]{0:T(128)} %bitcast.member_ref, f32[16,72,128]{2,1,0:T(8,128)} %copy-done, f32[1152,128]{1,0:T(8,128)} %get-tuple-element.24.truth_ref), custom_call_target="tpu_custom_call" | custom-call | tf_op jit(solution)/shard_map/pallas_call | solution.py:41
  66.9 5.1 %all-to-all-start.1 = ((bf16[16,72,128]{2,1,0:T(8,128)(2,1)}), bf16[16,72,128]{2,1,0:T(8,128)(2,1)S(1)}, u32[]{:S(2)}, u32[]{:S(2)}) async-start(bf16[16,72,128]{2,1,0:T(8,128)(2,1)} %shard_map.88), calls=%async_computation.1 | async-start | bytes 589824 | tf_op jit(solution)/shard_map/all_to_all | solution.py:336
  72.1 0.9 copy.13.w2_ref
  73.0 0.8 pad.23
  73.8 7.7 %all-to-all-done.1.grad_ref = bf16[16,72,128]{2,1,0:T(8,128)(2,1)S(1)} async-done(((bf16[16,72,128]{2,1,0:T(8,128)(2,1)}), bf16[16,72,128]{2,1,0:T(8,128)(2,1)S(1)}, u32[]{:S(2)}, u32[]{:S(2)}) %all-to-all-start.1) | async-done | bytes 294944 | tf_op jit(solution)/shard_map/all_to_all | solution.py:336
  81.5 0.7 copy-done.3
  82.3 7.6 %shard_map.89 = (bf16[664,128]{1,0:T(8,128)(2,1)}, bf16[16,144,128]{2,1,0:T(8,128)(2,1)}) custom-call(bf16[16,72,128]{2,1,0:T(8,128)(2,1)} %copy-done.3, f32[192,1408]{1,0:T(8,128)} %get-tuple-element.25.pre_ref, bf16[192,1152]{1,0:T(8,128)(2,1)} %get-tuple-element.26.hidden_ref, bf16[864,1152]{1,0:T(8,128)(2,1)} %get-tuple-element.27.window_ref, ...), custom_call_target="tpu_custom_call" | custom-call | tf_op jit(solution)/shard_map/pallas_call | solution.py:41
  89.8 21.0 %all_to_all.25.parts_ref = bf16[16,144,128]{2,1,0:T(8,128)(2,1)} all-to-all(bf16[16,144,128]{2,1,0:T(8,128)(2,1)} %get-tuple-element.30), channel_id=1, replica_groups=mesh['member'=16,'lat'=4,'lon'=4] {'lat','lon'}, dimensions={0} | all-to-all | bytes 1179648 | tf_op jit(solution)/shard_map/all_to_all | solution.py:336
  110.8 2.0 %shard_map.90 = bf16[16,144,128]{2,1,0:T(8,128)(2,1)} custom-call(bf16[16,144,128]{2,1,0:T(8,128)(2,1)} %all_to_all.25.parts_ref), custom_call_target="tpu_custom_call" | custom-call | tf_op jit(solution)/shard_map/pallas_call | solution.py:41
  112.8 21.6 %all_to_all.26.parts_ref = bf16[16,144,128]{2,1,0:T(8,128)(2,1)} all-to-all(bf16[16,144,128]{2,1,0:T(8,128)(2,1)} %shard_map.90), channel_id=1, replica_groups=mesh['member'=16,'lat'=4,'lon'=4] {'member'}, dimensions={0} | all-to-all | bytes 1179648 | tf_op jit(solution)/shard_map/all_to_all | solution.py:336
  134.4 2.0 %shard_map.91 = bf16[16,144,128]{2,1,0:T(8,128)(2,1)} custom-call(bf16[16,144,128]{2,1,0:T(8,128)(2,1)} %all_to_all.26.parts_ref), custom_call_target="tpu_custom_call" | custom-call | tf_op jit(solution)/shard_map/pallas_call | solution.py:41
  136.4 19.6 %all_to_all.27.parts_ref = bf16[16,144,128]{2,1,0:T(8,128)(2,1)} all-to-all(bf16[16,144,128]{2,1,0:T(8,128)(2,1)} %shard_map.91), channel_id=1, replica_groups=mesh['member'=16,'lat'=4,'lon'=4] {'lat','lon'}, dimensions={0} | all-to-all | bytes 1179648 | tf_op jit(solution)/shard_map/all_to_all | solution.py:336
  156.0 2.6 %shard_map.92 = (f32[9,192,83]{2,1,0:T(8,128)}, f32[9,83,192]{2,1,0:T(8,128)}) custom-call(bf16[16,144,128]{2,1,0:T(8,128)(2,1)} %all_to_all.27.parts_ref), custom_call_target="tpu_custom_call" | custom-call | tf_op jit(solution)/shard_map/pallas_call | solution.py:41
  158.6 2.4 %copy.14 = f32[9,192,83]{1,2,0:T(8,128)} copy(f32[9,192,83]{2,1,0:T(8,128)} %get-tuple-element.37) | data formatting | bytes 1147392
  (22 shorter events, 0.2 us)
Async XLA Ops:
  0.6 24.1 %copy-start.2 = (bf16[9,192,83]{1,2,0:T(8,128)(2,1)S(1)}, bf16[9,192,83]{1,2,0:T(8,128)(2,1)}, u32[]{:S(2)}) copy-start(bf16[9,192,83]{1,2,0:T(8,128)(2,1)} %param.10) | copy-start | bytes 860548
  0.6 25.2 %copy-start.1 = (bf16[9,83,192]{2,1,0:T(8,128)(2,1)S(1)}, bf16[9,83,192]{2,1,0:T(8,128)(2,1)}, u32[]{:S(2)}) copy-start(bf16[9,83,192]{2,1,0:T(8,128)(2,1)} %param.11) | copy-start | bytes 860548
  2.9 23.7 %copy-start.8 = (f32[83]{0:T(128)S(1)}, f32[83]{0:T(128)}, u32[]{:S(2)}) copy-start(f32[83]{0:T(128)} %param.9) | copy-start | bytes 1000
  2.9 9.5 %collective-permute-start = (f32[6,88,128]{2,1,0:T(8,128)}, f32[6,88,128]{2,1,0:T(8,128)S(1)}, u32[]{:S(2)}, u32[]{:S(2)}) collective-permute-start(f32[6,88,128]{2,1,0:T(8,128)} %get-tuple-element.19), channel_id=1, source_target_pairs={{0,4},{4,8},{8,12},{1,5},{5,9},{9,13},{2,6},{6,10},{10,14},{3,7},{... | collective-permute-start | bytes 811016 | tf_op jit(solution)/shard_map/ppermute | solution.py:362
  7.0 9.1 %collective-permute-start.1 = (f32[6,88,128]{2,1,0:T(8,128)}, f32[6,88,128]{2,1,0:T(8,128)S(1)}, u32[]{:S(2)}, u32[]{:S(2)}) collective-permute-start(f32[6,88,128]{2,1,0:T(8,128)} %get-tuple-element.20), channel_id=1, source_target_pairs={{4,0},{8,4},{12,8},{5,1},{9,5},{13,9},{6,2},{10,6},{14,10},{7,3},{... | collective-permute-start | bytes 811016 | tf_op jit(solution)/shard_map/ppermute | solution.py:363
  12.5 3.7 %copy-start.4 = (f32[6,88,128]{2,1,0:T(8,128)}, f32[6,88,128]{2,1,0:T(8,128)S(1)}, u32[]{:S(2)}) copy-start(f32[6,88,128]{2,1,0:T(8,128)S(1)} %collective-permute-done.top_ref) | copy-start | bytes 811012
  16.2 0.7 copy-start.5
  19.5 7.2 %collective-permute-start.2 = (f32[88,128]{1,0:T(8,128)}, f32[88,128]{1,0:T(8,128)S(1)}, u32[]{:S(2)}, u32[]{:S(2)}) collective-permute-start(f32[88,128]{1,0:T(8,128)} %get-tuple-element.21), channel_id=1, source_target_pairs={{0,1},{1,2},{2,3},{3,0},{4,5},{5,6},{6,7},{7,4},{8,9},{9,10},{10,1... | collective-permute-start | bytes 135176 | tf_op jit(solution)/shard_map/ppermute | solution.py:368
  24.1 5.2 %collective-permute-start.3 = (f32[88,128]{1,0:T(8,128)}, f32[88,128]{1,0:T(8,128)S(1)}, u32[]{:S(2)}, u32[]{:S(2)}) collective-permute-start(f32[88,128]{1,0:T(8,128)} %get-tuple-element.22), channel_id=1, source_target_pairs={{1,0},{2,1},{3,2},{0,3},{5,4},{6,5},{7,6},{4,7},{9,8},{10,9},{11,1... | collective-permute-start | bytes 135176 | tf_op jit(solution)/shard_map/ppermute | solution.py:369
  26.6 3.4 %copy-start.6 = (f32[88,128]{1,0:T(8,128)}, f32[88,128]{1,0:T(8,128)S(1)}, u32[]{:S(2)}) copy-start(f32[88,128]{1,0:T(8,128)S(1)} %collective-permute-done.2.left_ref) | copy-start | bytes 135172
  29.3 0.7 copy-start.7
  38.3 24.6 %all-to-all-start = ((f32[16,72,128]{2,1,0:T(8,128)}), f32[16,72,128]{2,1,0:T(8,128)S(1)}, u32[]{:S(2)}, u32[]{:S(2)}) async-start(f32[16,72,128]{2,1,0:T(8,128)} %bitcast.20), calls=%async_computation | async-start | bytes 1179648 | tf_op jit(solution)/shard_map/all_to_all | solution.py:336
  62.9 0.8 copy-start
  66.9 14.6 %all-to-all-start.1 = ((bf16[16,72,128]{2,1,0:T(8,128)(2,1)}), bf16[16,72,128]{2,1,0:T(8,128)(2,1)S(1)}, u32[]{:S(2)}, u32[]{:S(2)}) async-start(bf16[16,72,128]{2,1,0:T(8,128)(2,1)} %shard_map.88), calls=%async_computation.1 | async-start | bytes 589824 | tf_op jit(solution)/shard_map/all_to_all | solution.py:336
  81.5 0.7 copy-start.3

commit v3 on v2

--- a/solution.py
+++ b/solution.py
@@ -25,17 +25,16 @@
 HIDDEN = (3, 14)
 OWN = (4, 13)
 MEMBERS = 16
-PLACES = 16
+GROUPS = 64
 CHUNK = 72
-PIECE = 144
+PIECE = 40
 f32 = jnp.float32
 bf16 = jnp.bfloat16
 GELU_A = math.sqrt(2.0 / math.pi)
 GELU_B = 0.044715
-VMEM_LIMIT = 60 * 1024 * 1024
-
-
-def call(kernel, outs, scratch, *operands, smem=0):
+
+
+def call(kernel, limit, outs, scratch, *operands, smem=0):
     specs = [pl.BlockSpec(memory_space=pltpu.SMEM)] * smem
     specs += [pl.BlockSpec(memory_space=pltpu.VMEM)] * (len(operands) - smem)
     return pl.pallas_call(
@@ -44,7 +43,7 @@
         in_specs=specs,
         out_specs=[pl.BlockSpec(memory_space=pltpu.VMEM)] * len(outs),
         scratch_shapes=[pltpu.VMEM(shape, kind) for shape, kind in scratch],
-        compiler_params=pltpu.CompilerParams(vmem_limit_bytes=VMEM_LIMIT),
+        compiler_params=pltpu.CompilerParams(vmem_limit_bytes=limit << 20),
     )(*operands)
 
 
@@ -126,9 +125,9 @@
 
 
 def forward_kernel(
-    own_ref, top_ref, bottom_ref, left_ref, right_ref, gain_ref, valid_ref, mine_ref, w1_ref, w2_ref,
+    member_ref, own_ref, top_ref, bottom_ref, left_ref, right_ref, gain_ref, valid_ref, mine_ref, w1_ref, w2_ref,
     forecast_ref, truth_ref, pre_ref, hidden_ref, window_ref, latent_ref,
-    latent, normed, window, hidden, partial,
+    latent, normed, window, hidden, partial, truth,
 ):
     pieces, truths = [], []
     for row in range(TALL):
@@ -152,8 +151,9 @@
         scaled = centered * lax.rsqrt(variance + norm_eps) * gain
         normed[0:CP, tile(index)] = scaled * valid_ref[:, tile(index)]
     for index, values in flat_tiles(truths, *SPREAD):
-        truth_ref[pl.ds(CP * (index - SPREAD[0]), CP), :] = values
-    truth_ref[pl.ds(CP * (SPREAD[1] - SPREAD[0]), 8), :] = jnp.zeros((8, 128), f32)
+        truth[pl.ds(CP * (index - SPREAD[0]), CP), :] = values
+    truth[pl.ds(CP * (SPREAD[1] - SPREAD[0]), 8), :] = jnp.zeros((8, 128), f32)
+    truth_ref[...] = truth[pl.ds(pl.multiple_of(member_ref[0] * CHUNK, 8), CHUNK), :]
     latent_ref[...] = latent[:, 128 * OWN[0] : 128 * OWN[1]]
 
     for group in range(CI // 16):
@@ -194,12 +194,10 @@
     return values * lax.rsqrt(values * values + soft_eps)
 
 
-def score_kernel(member_ref, forecast_ref, truth_ref, grad_ref, grads):
-    base = member_ref[0] * CHUNK
-
+def score_kernel(forecast_ref, truth_ref, grad_ref, grads):
     def body(step, carry):
         span = pl.ds(pl.multiple_of(8 * step, 8), 8)
-        truth = truth_ref[pl.ds(pl.multiple_of(base + 8 * step, 8), 8), :]
+        truth = truth_ref[span, :]
         values = [forecast_ref[m, span, :] for m in range(MEMBERS)]
         totals = [jnp.zeros((8, 128), f32)] * MEMBERS
         for first in range(MEMBERS):
@@ -259,8 +257,8 @@
         values = grad_in[CI * k : CI * k + C, :]
         packed[C * k : C * (k + 1), :] = values[:, 0:128]
         packed[C * (18 + k) : C * (19 + k), 0:64] = values[:, 128:192]
-    packed[27 * C :, :] = jnp.zeros((PLACES * PIECE - 27 * C, 128), f32)
-    for place in range(PLACES):
+    packed[27 * C :, :] = jnp.zeros((GROUPS * PIECE - 27 * C, 128), f32)
+    for place in range(GROUPS):
         weights_ref[place] = packed[PIECE * place : PIECE * place + PIECE, :].astype(bf16)
 
     span = high - low
@@ -312,7 +310,7 @@
 
 def weights_kernel(parts_ref, grad_in_ref, grad_out_ref, packed):
     scale = 1.0 / math.sqrt(MEMBERS * 32 * 512)
-    for place in range(PLACES):
+    for place in range(GROUPS):
         packed[PIECE * place : PIECE * place + PIECE, :] = parts_ref[place].astype(f32) * scale
     for k in range(9):
         first = packed[C * k : C * (k + 1), :]
@@ -320,8 +318,8 @@
         shared = packed[C * (18 + k) : C * (19 + k), :]
         grad_out_ref[k, :, 0:128] = second
         grad_out_ref[k, :, 128:192] = shared[:, 64:128]
-        grad_in_ref[k, 0:128, :] = first.T
-        grad_in_ref[k, 128:192, :] = shared[:, 0:64].T
+        grad_in_ref[k, :, 0:128] = first
+        grad_in_ref[k, :, 128:192] = shared[:, 0:64]
 
 
 def neighbours(axis, periodic):
@@ -354,6 +352,7 @@
 
     own, up, down = call(
         rows_kernel,
+        6,
         [((2 * ROWS, CP, 128), f32), ((RIM + RIM // 2, CP, 128), f32), ((RIM + RIM // 2, CP, 128), f32)],
         [((C * ROWS, COLS), f32)] * 2,
         rows(embeddings), rows(entry_perturbation), rows(target),
@@ -362,7 +361,7 @@
     top = lax.ppermute(down, "lat", forward)
     bottom = lax.ppermute(up, "lat", backward)
     to_left, to_right = call(
-        columns_kernel, [((CP, 128), f32)] * 2, [], own, top, bottom
+        columns_kernel, 6, [((CP, 128), f32)] * 2, [], own, top, bottom
     )
     forward, backward = neighbours("lon", True)
     left = lax.ppermute(to_right, "lon", forward)
@@ -380,13 +379,15 @@
     w2_turned = padded(second_stencil_kernel, 1, CI).transpose(2, 0, 1).reshape(HID, 9 * CI)
     w1_turned = padded(first_stencil_kernel.transpose(0, 2, 1), 1, CP).reshape(9 * CP, HID)
 
+    member = lax.axis_index("member").astype(jnp.int32)[None]
     own_lanes = 128 * (OWN[1] - OWN[0])
     hidden_lanes = 128 * (HIDDEN[1] - HIDDEN[0])
     forecast, truth, pre, hidden, window, latent = call(
         forward_kernel,
+        26,
         [
             ((MEMBERS * CHUNK, 128), f32),
-            ((MEMBERS * CHUNK, 128), f32),
+            ((CHUNK, 128), f32),
             ((HID, hidden_lanes), f32),
             ((HID, own_lanes), bf16),
             ((9 * CI, own_lanes), bf16),
@@ -398,21 +399,23 @@
             ((9 * CI, FLAT), bf16),
             ((HID, FLAT), bf16),
             ((9 * CP, FLAT), f32),
+            ((MEMBERS * CHUNK, 128), f32),
         ],
-        own, top, bottom, left, right, gain, valid, mine, w1_stack, w2_stack,
+        member, own, top, bottom, left, right, gain, valid, mine, w1_stack, w2_stack, smem=1,
     )
     spread = swap(forecast.reshape(MEMBERS, CHUNK, 128), "member")
-    member = lax.axis_index("member").astype(jnp.int32)[None]
     (grads,) = call(
         score_kernel,
+        6,
         [((MEMBERS, CHUNK, 128), bf16)],
         [((MEMBERS, CHUNK, 128), f32)],
-        member, spread, truth, smem=1,
+        spread, truth,
     )
     grads = swap(grads, "member")
     states, weights = call(
         backward_kernel,
-        [((C * ROWS, COLS), bf16), ((PLACES, PIECE, 128), bf16)],
+        24,
+        [((C * ROWS, COLS), bf16), ((GROUPS, PIECE, 128), bf16)],
         [
             ((MEMBERS * CHUNK, 128), f32),
             ((CI, FLAT), f32),
@@ -421,19 +424,22 @@
             ((9 * CP, hidden_lanes), f32),
             ((CP, own_lanes), f32),
             ((C * ROWS, COLS), f32),
-            ((PLACES * PIECE, 128), f32),
+            ((GROUPS * PIECE, 128), f32),
         ],
         grads, pre, hidden, window, latent, gain, valid, mine, w2_turned, w1_turned,
     )
+    across, along = ("member", "lat"), "lon"
     piece = (PIECE, 128)
-    (copies,) = call(total_kernel, [((MEMBERS,) + piece, bf16)], [], swap(weights, ("lat", "lon")))
-    (copies,) = call(total_kernel, [((PLACES,) + piece, bf16)], [], swap(copies, "member"))
+    (copies,) = call(total_kernel, 6, [((4,) + piece, bf16)], [], swap(weights, across))
+    (copies,) = call(total_kernel, 6, [((GROUPS,) + piece, bf16)], [], swap(copies, along))
     grad_in, grad_out = call(
         weights_kernel,
-        [((9, HID, C), f32), ((9, C, HID), f32)],
-        [((PLACES * PIECE, 128), f32)],
-        swap(copies, ("lat", "lon")),
-    )
+        8,
+        [((9, C, HID), f32), ((9, C, HID), f32)],
+        [((GROUPS * PIECE, 128), f32)],
+        swap(copies, across),
+    )
+    grad_in = grad_in.transpose(0, 2, 1)
     return (states.reshape(embeddings.shape), grad_in, grad_out)
 
 

time: 162 us -> 148 us (0.914)
  blocking collectives: 62.2 us -> 87.2 us
  Pallas kernels: 30.5 us -> 13.8 us
  waiting for transfers between devices: 33.7 us -> 19.8 us
  starting transfers between devices: 23.5 us -> 13.8 us
    all_to_all x3 -> x4, blocking collectives: 62.2 us -> 87.2 us  [swap(): return lax.all_to_all(values, axes, split_axis=0, concat_axis=0, tiled=True)]
    pallas_call x8, Pallas kernels: 30.5 us -> 13.8 us  [call(): pl.pallas_call(kernel, out_shape=[jax.ShapeDtypeStruct(shape, kind) for s...]
    all_to_all x2 -> x1, waiting for transfers between devices: 23.9 us -> 7.76 us  [swap(): return lax.all_to_all(values, axes, split_axis=0, concat_axis=0, tiled=True)]
    all_to_all x2 -> x1, starting transfers between devices: 13.5 us -> 3.72 us  [swap(): return lax.all_to_all(values, axes, split_axis=0, concat_axis=0, tiled=True)]
    unnamed x19 -> x34, local copies, waits for them, and re-layouts: 4.72 us -> 6.96 us
  transfers between devices with their start and end apart: 6 -> 5, of which waited for: 5 -> 5; matrix products, arithmetic and copies ran while one was open for 3% -> 2% of each run, Pallas kernels for 0% -> 0%
where the time goes in v3:
time: 148 us; the launch traced here: 146 us
  blocking collectives  87.2 us (59%)
  waiting for transfers between devices  19.8 us (13%)
  Pallas kernels  13.8 us (9%)
  starting transfers between devices  13.8 us (9%)
  local copies, waits for them, and re-layouts  10.5 us (7%)
    all_to_all x4, blocking collectives, swap(): return lax.all_to_all(values, axes, split_axis=0, concat_axis=0, tiled=True)  87.2 us
    pallas_call x8, Pallas kernels, call(): pl.pallas_call(kernel, out_shape=[jax.ShapeDtypeStruct(shape, kind) for s...  13.8 us
    all_to_all x1, waiting for transfers between devices, swap(): return lax.all_to_all(values, axes, split_axis=0, concat_axis=0, tiled=True)  7.76 us
    unnamed x34, local copies, waits for them, and re-layouts  6.96 us
    ppermute x1, starting transfers between devices, on_device(): left = lax.ppermute(to_right, 'lon', forward)  4.74 us
    ppermute x1, starting transfers between devices, on_device(): top = lax.ppermute(down, 'lat', forward)  4.09 us
    ppermute x1, waiting for transfers between devices, on_device(): right = lax.ppermute(to_left, 'lon', backward)  3.84 us
    ppermute x1, waiting for transfers between devices, on_device(): bottom = lax.ppermute(up, 'lat', backward)  3.81 us
  transfers between devices with their start and end apart: 5, of which 5 were waited for; matrix products, arithmetic and copies ran while one was open for 2% of the time, Pallas kernels for 0%

profile of v3, /device:TPU:1, one launch (start us, length us, event | category | flops | bytes accessed | tf_op | source)
XLA Modules:
  0.0 146.1 jit_solution(15440614199994168472)
XLA Ops:
  0.6 0.9 copy-done.8
  1.6 0.9 copy-done.9
  2.5 0.9 copy-done.10
  3.4 0.2 shard_map.85
  3.6 4.1 %collective-permute-start = (f32[6,88,128]{2,1,0:T(8,128)S(1)}, f32[6,88,128]{2,1,0:T(8,128)S(1)}, u32[]{:S(2)}, u32[]{:S(2)}) collective-permute-start(f32[6,88,128]{2,1,0:T(8,128)S(1)} %get-tuple-element.19), channel_id=1, source_target_pairs={{0,4},{4,8},{8,12},{1,5},{5,9},{9,13},{2,6},{6,10},{10,14},{3,7},{... | collective-permute-start | bytes 811016 | tf_op jit(solution)/shard_map/ppermute | solution.py:361
  7.7 1.3 collective-permute-start.1
  9.1 3.7 %collective-permute-done.top_ref = f32[6,88,128]{2,1,0:T(8,128)S(1)} collective-permute-done((f32[6,88,128]{2,1,0:T(8,128)S(1)}, f32[6,88,128]{2,1,0:T(8,128)S(1)}, u32[]{:S(2)}, u32[]{:S(2)}) %collective-permute-start) | collective-permute-done | bytes 270368 | tf_op jit(solution)/shard_map/ppermute | solution.py:361
  12.8 3.8 %collective-permute-done.1.bottom_ref = f32[6,88,128]{2,1,0:T(8,128)S(1)} collective-permute-done((f32[6,88,128]{2,1,0:T(8,128)S(1)}, f32[6,88,128]{2,1,0:T(8,128)S(1)}, u32[]{:S(2)}, u32[]{:S(2)}) %collective-permute-start.1) | collective-permute-done | bytes 270368 | tf_op jit(solution)/shard_map/ppermute | solution.py:362
  16.6 0.7 shard_map.86
  17.4 4.7 %collective-permute-start.2 = (f32[88,128]{1,0:T(8,128)S(1)}, f32[88,128]{1,0:T(8,128)S(1)}, u32[]{:S(2)}, u32[]{:S(2)}) collective-permute-start(f32[88,128]{1,0:T(8,128)S(1)} %get-tuple-element.21), channel_id=1, source_target_pairs={{0,1},{1,2},{2,3},{3,0},{4,5},{5,6},{6,7},{7,4},{8,9},{9,10},{10,1... | collective-permute-start | bytes 135176 | tf_op jit(solution)/shard_map/ppermute | solution.py:367
  22.1 0.1 pad.20
  22.2 0.2 copy.11.w1_ref
  22.6 0.7 collective-permute-done.2.left_ref
  23.2 3.8 %collective-permute-done.3.right_ref = f32[88,128]{1,0:T(8,128)S(1)} collective-permute-done((f32[88,128]{1,0:T(8,128)S(1)}, f32[88,128]{1,0:T(8,128)S(1)}, u32[]{:S(2)}, u32[]{:S(2)}) %collective-permute-start.3) | collective-permute-done | bytes 45088 | tf_op jit(solution)/shard_map/ppermute | solution.py:368
  27.2 1.0 copy-done.1
  28.1 5.0 %shard_map.87 = (f32[1152,128]{1,0:T(8,128)S(1)}, f32[72,128]{1,0:T(8,128)S(1)}, f32[192,1408]{1,0:T(8,128)S(1)}, bf16[192,1152]{1,0:T(8,128)(2,1)S(1)}, bf16[86...) custom-call(s32[1]{0:T(128)} %bitcast.member_ref, f32[16,88,128]{2,1,0:T(8,128)S(1)} %get-tuple-element.18.own_ref, ...), custom_call_target="tpu_custom_call" | custom-call | tf_op jit(solution)/shard_map/pallas_call | solution.py:40
  33.1 1.0 copy-done.2
  34.1 26.5 %all_to_all.25.forecast_ref = f32[16,72,128]{2,1,0:T(8,128)S(1)} all-to-all(f32[16,72,128]{2,1,0:T(8,128)S(1)} %bitcast.18), channel_id=1, replica_groups=mesh['member'=16,'lat'=4,'lon'=4] {'member'}, dimensions={0} | all-to-all | bytes 1179648 | tf_op jit(solution)/shard_map/all_to_all | solution.py:334
  60.6 2.0 %shard_map.88 = bf16[16,72,128]{2,1,0:T(8,128)(2,1)} custom-call(f32[16,72,128]{2,1,0:T(8,128)S(1)} %all_to_all.25.forecast_ref, f32[72,128]{1,0:T(8,128)S(1)} %get-tuple-element.24.truth_ref), custom_call_target="tpu_custom_call" | custom-call | tf_op jit(solution)/shard_map/pallas_call | solution.py:40
  62.6 3.7 %all-to-all-start.1 = ((bf16[16,72,128]{2,1,0:T(8,128)(2,1)}), bf16[16,72,128]{2,1,0:T(8,128)(2,1)S(1)}, u32[]{:S(2)}, u32[]{:S(2)}) async-start(bf16[16,72,128]{2,1,0:T(8,128)(2,1)} %shard_map.88), calls=%async_computation.1 | async-start | bytes 589824 | tf_op jit(solution)/shard_map/all_to_all | solution.py:334
  66.3 0.8 pad.22
  67.1 1.2 copy.12.w2_ref
  68.4 1.1 pad.23
  69.4 7.8 %all-to-all-done.1.grad_ref = bf16[16,72,128]{2,1,0:T(8,128)(2,1)S(1)} async-done(((bf16[16,72,128]{2,1,0:T(8,128)(2,1)}), bf16[16,72,128]{2,1,0:T(8,128)(2,1)S(1)}, u32[]{:S(2)}, u32[]{:S(2)}) %all-to-all-start.1) | async-done | bytes 294944 | tf_op jit(solution)/shard_map/all_to_all | solution.py:334
  77.2 1.2 copy-done.3
  78.4 1.0 copy-done.7
  79.4 4.4 %shard_map.89 = (bf16[664,128]{1,0:T(8,128)(2,1)}, bf16[64,40,128]{2,1,0:T(8,128)(2,1)S(1)}) custom-call(bf16[16,72,128]{2,1,0:T(8,128)(2,1)S(1)} %all-to-all-done.1.grad_ref, f32[192,1408]{1,0:T(8,128)S(1)} %copy-done.3, bf16[192,1152]{1,0:T(8,128)(2,1)S(1)} %copy-done.5, bf16[864,1152]{1,0:T(8,128)(2,1)S(1)} %get-tuple-element.27.window_ref, ...), custom_call_target="tpu_custom_call" | custom-call | tf_op jit(solution)/shard_map/pallas_call | solution.py:40
  83.9 26.2 %all_to_all.26.parts_ref = bf16[64,40,128]{2,1,0:T(8,128)(2,1)S(1)} all-to-all(bf16[64,40,128]{2,1,0:T(8,128)(2,1)S(1)} %get-tuple-element.30), channel_id=1, replica_groups=mesh['member'=16,'lat'=4,'lon'=4] {'member','lat'}, dimensions={0} | all-to-all | bytes 1310720 | tf_op jit(solution)/shard_map/all_to_all | solution.py:334
  110.1 0.1 shard_map.90
  110.2 10.1 %all_to_all.27.parts_ref = bf16[4,40,128]{2,1,0:T(8,128)(2,1)S(1)} all-to-all(bf16[4,40,128]{2,1,0:T(8,128)(2,1)S(1)} %shard_map.90), channel_id=1, replica_groups=mesh['member'=16,'lat'=4,'lon'=4] {'lon'}, dimensions={0} | all-to-all | bytes 81920 | tf_op jit(solution)/shard_map/all_to_all | solution.py:334
  120.4 24.3 %all_to_all.28.parts_ref = bf16[64,40,128]{2,1,0:T(8,128)(2,1)S(1)} all-to-all(bf16[64,40,128]{2,1,0:T(8,128)(2,1)S(1)} %shard_map.91), channel_id=1, replica_groups=mesh['member'=16,'lat'=4,'lon'=4] {'member','lat'}, dimensions={0} | all-to-all | bytes 1310720 | tf_op jit(solution)/shard_map/all_to_all | solution.py:334
  144.8 1.4 shard_map.92
  (36 shorter events, 0.4 us)
Async XLA Ops:
  0.6 0.9 copy-start.8
  1.5 0.9 copy-start.9
  2.5 0.9 copy-start.10
  3.4 18.8 %copy-start.15 = (bf16[9,192,83]{1,2,0:T(8,128)(2,1)S(1)}, bf16[9,192,83]{1,2,0:T(8,128)(2,1)}, u32[]{:S(2)}) copy-start(bf16[9,192,83]{1,2,0:T(8,128)(2,1)} %param.10) | copy-start | bytes 860548
  3.4 19.1 %copy-start.13 = (bf16[9,83,192]{2,1,0:T(8,128)(2,1)S(1)}, bf16[9,83,192]{2,1,0:T(8,128)(2,1)}, u32[]{:S(2)}) copy-start(bf16[9,83,192]{2,1,0:T(8,128)(2,1)} %param.11) | copy-start | bytes 860548
  3.6 18.9 %copy-start.16 = (f32[83]{0:T(128)S(1)}, f32[83]{0:T(128)}, u32[]{:S(2)}) copy-start(f32[83]{0:T(128)} %param.9) | copy-start | bytes 1000
  3.6 9.2 %collective-permute-start = (f32[6,88,128]{2,1,0:T(8,128)S(1)}, f32[6,88,128]{2,1,0:T(8,128)S(1)}, u32[]{:S(2)}, u32[]{:S(2)}) collective-permute-start(f32[6,88,128]{2,1,0:T(8,128)S(1)} %get-tuple-element.19), channel_id=1, source_target_pairs={{0,4},{4,8},{8,12},{1,5},{5,9},{9,13},{2,6},{6,10},{10,14},{3,7},{... | collective-permute-start | bytes 811016 | tf_op jit(solution)/shard_map/ppermute | solution.py:361
  7.7 8.9 %collective-permute-start.1 = (f32[6,88,128]{2,1,0:T(8,128)S(1)}, f32[6,88,128]{2,1,0:T(8,128)S(1)}, u32[]{:S(2)}, u32[]{:S(2)}) collective-permute-start(f32[6,88,128]{2,1,0:T(8,128)S(1)} %get-tuple-element.20), channel_id=1, source_target_pairs={{4,0},{8,4},{12,8},{5,1},{9,5},{13,9},{6,2},{10,6},{14,10},{7,3},{... | collective-permute-start | bytes 811016 | tf_op jit(solution)/shard_map/ppermute | solution.py:362
  9.1 24.0 %copy-start.11 = (f32[1,1152]{1,0:T(1,128)}, f32[1,1152]{1,0:T(1,128)S(1)}, u32[]{:S(2)}) copy-start(f32[1,1152]{1,0:T(1,128)S(1)} %and_convert_fusion.1.mine_ref) | copy-start | bytes 13828
  16.6 10.5 %copy-start = (f32[6,88,128]{2,1,0:T(8,128)}, f32[6,88,128]{2,1,0:T(8,128)S(1)}, u32[]{:S(2)}) copy-start(f32[6,88,128]{2,1,0:T(8,128)S(1)} %collective-permute-done.1.bottom_ref) | copy-start | bytes 811012
  17.4 5.9 %collective-permute-start.2 = (f32[88,128]{1,0:T(8,128)S(1)}, f32[88,128]{1,0:T(8,128)S(1)}, u32[]{:S(2)}, u32[]{:S(2)}) collective-permute-start(f32[88,128]{1,0:T(8,128)S(1)} %get-tuple-element.21), channel_id=1, source_target_pairs={{0,1},{1,2},{2,3},{3,0},{4,5},{5,6},{6,7},{7,4},{8,9},{9,10},{10,1... | collective-permute-start | bytes 135176 | tf_op jit(solution)/shard_map/ppermute | solution.py:367
  22.1 5.0 %collective-permute-start.3 = (f32[88,128]{1,0:T(8,128)S(1)}, f32[88,128]{1,0:T(8,128)S(1)}, u32[]{:S(2)}, u32[]{:S(2)}) collective-permute-start(f32[88,128]{1,0:T(8,128)S(1)} %get-tuple-element.22), channel_id=1, source_target_pairs={{1,0},{2,1},{3,2},{0,3},{5,4},{6,5},{7,6},{4,7},{9,8},{10,9},{11,1... | collective-permute-start | bytes 135176 | tf_op jit(solution)/shard_map/ppermute | solution.py:368
  27.1 1.0 copy-start.1
  33.1 1.0 copy-start.2
  34.1 26.5 %copy-start.4 = (bf16[192,1152]{1,0:T(8,128)(2,1)}, bf16[192,1152]{1,0:T(8,128)(2,1)S(1)}, u32[]{:S(2)}) copy-start(bf16[192,1152]{1,0:T(8,128)(2,1)S(1)} %get-tuple-element.26.hidden_ref) | copy-start | bytes 1327108
  34.1 26.5 %copy-start.6 = (f32[88,1152]{1,0:T(8,128)}, f32[88,1152]{1,0:T(8,128)S(1)}, u32[]{:S(2)}) copy-start(f32[88,1152]{1,0:T(8,128)S(1)} %get-tuple-element.28.latent_ref) | copy-start | bytes 1216516
  34.1 32.2 %copy-start.14 = (bf16[9,83,192]{2,1,0:T(8,128)(2,1)S(1)}, bf16[9,83,192]{2,1,0:T(8,128)(2,1)}, u32[]{:S(2)}) copy-start(bf16[9,83,192]{2,1,0:T(8,128)(2,1)} %param.11) | copy-start | bytes 860548
  60.6 16.6 %copy-start.12 = (f32[1,1152]{1,0:T(1,128)S(1)}, f32[1,1152]{1,0:T(1,128)}, u32[]{:S(2)}) copy-start(f32[1,1152]{1,0:T(1,128)} %copy-done.11) | copy-start | bytes 13828
  60.6 16.6 %copy-start.5 = (bf16[192,1152]{1,0:T(8,128)(2,1)S(1)}, bf16[192,1152]{1,0:T(8,128)(2,1)}, u32[]{:S(2)}) copy-start(bf16[192,1152]{1,0:T(8,128)(2,1)} %copy-done.4) | copy-start | bytes 1327108
  62.6 14.6 %all-to-all-start.1 = ((bf16[16,72,128]{2,1,0:T(8,128)(2,1)}), bf16[16,72,128]{2,1,0:T(8,128)(2,1)S(1)}, u32[]{:S(2)}, u32[]{:S(2)}) async-start(bf16[16,72,128]{2,1,0:T(8,128)(2,1)} %shard_map.88), calls=%async_computation.1 | async-start | bytes 589824 | tf_op jit(solution)/shard_map/all_to_all | solution.py:334
  77.2 1.2 copy-start.3
  78.4 1.0 copy-start.7

commit v4 on v3

--- a/solution.py
+++ b/solution.py
@@ -25,28 +25,58 @@
 HIDDEN = (3, 14)
 OWN = (4, 13)
 MEMBERS = 16
-GROUPS = 64
+GROUPS = 32
+RING = 8
 CHUNK = 72
-PIECE = 40
+PIECE = 72
+HALF = RIM // 2
 f32 = jnp.float32
 bf16 = jnp.bfloat16
 GELU_A = math.sqrt(2.0 / math.pi)
 GELU_B = 0.044715
 
 
-def call(kernel, limit, outs, scratch, *operands, smem=0):
+def call(kernel, limit, outs, scratch, *operands, smem=0, far=(), copies=0):
+    near = pl.BlockSpec(memory_space=pltpu.VMEM)
+    away = pl.BlockSpec(memory_space=pltpu.HBM)
     specs = [pl.BlockSpec(memory_space=pltpu.SMEM)] * smem
-    specs += [pl.BlockSpec(memory_space=pltpu.VMEM)] * (len(operands) - smem)
+    specs += [away if i in far else near for i in range(smem, len(operands))]
+    kinds = [kind[0] if isinstance(kind, tuple) else kind for _, kind in outs]
+    kept = [pltpu.VMEM(shape, kind) for shape, kind in scratch]
     return pl.pallas_call(
         kernel,
-        out_shape=[jax.ShapeDtypeStruct(shape, kind) for shape, kind in outs],
+        out_shape=[jax.ShapeDtypeStruct(shape, kind) for (shape, _), kind in zip(outs, kinds)],
         in_specs=specs,
-        out_specs=[pl.BlockSpec(memory_space=pltpu.VMEM)] * len(outs),
-        scratch_shapes=[pltpu.VMEM(shape, kind) for shape, kind in scratch],
+        out_specs=[away if isinstance(kind, tuple) else near for _, kind in outs],
+        scratch_shapes=kept + ([pltpu.SemaphoreType.DMA((copies,))] if copies else []),
         compiler_params=pltpu.CompilerParams(vmem_limit_bytes=limit << 20),
     )(*operands)
 
 
+def started(*pairs, semaphores):
+    moves = [
+        pltpu.make_async_copy(source, target, semaphores.at[i]) for i, (source, target) in enumerate(pairs)
+    ]
+    for move in moves:
+        move.start()
+    return moves
+
+
+def gain_column(gain_ref):
+    row = lax.broadcasted_iota(jnp.int32, (CP, C), 0)
+    lane = lax.broadcasted_iota(jnp.int32, (CP, C), 1)
+    spread = jnp.where(row == lane, jnp.broadcast_to(gain_ref[...], (CP, C)), 0.0)
+    return jnp.sum(spread, axis=1, keepdims=True)
+
+
+def centred(values):
+    real = lax.broadcasted_iota(jnp.int32, (CP, 128), 0) < C
+    average = jnp.sum(values, axis=0, keepdims=True) * (1.0 / C)
+    centered = jnp.where(real, values - average, 0.0)
+    variance = jnp.sum(centered * centered, axis=0, keepdims=True) * (1.0 / C)
+    return centered, lax.rsqrt(variance + norm_eps)
+
+
 def step_of(offset):
     return (offset // 3 - 1) * PITCH + offset % 3 - 1
 
@@ -59,36 +89,58 @@
     return lax.broadcasted_iota(jnp.int32, (height, 128), 1)
 
 
-def rows_kernel(emb_ref, pert_ref, target_ref, own_ref, up_ref, down_ref, latent, truth):
-    latent[...] = emb_ref[...].astype(f32) + pert_ref[...].astype(f32)
-    truth[...] = target_ref[...].astype(f32)
+def rows_kernel(
+    emb_ref, pert_ref, target_ref, gain_ref, own_ref, up_ref, down_ref, emb, pert, target, first, second, truth, semaphores,
+):
+    moves = started((emb_ref, emb), (pert_ref, pert), (target_ref, target), semaphores=semaphores)
+    for move, source, wide in zip(moves, (emb, pert, target), (first, second, truth)):
+        move.wait()
+        wide[...] = source[...].astype(f32).reshape(C * ROWS, COLS)
     rest = jnp.zeros((CP - C, 128), f32)
+    gain = gain_column(gain_ref)
+
+    def row_of(source, r):
+        return jnp.concatenate([source[pl.ds(r, C, stride=ROWS), :], rest], axis=0)
+
     for r in range(ROWS):
-        for base, source, sent in ((0, latent, RIM), (ROWS, truth, RIM // 2)):
-            row = jnp.concatenate([source[pl.ds(r, C, stride=ROWS), :], rest], axis=0)
-            own_ref[base + r] = row
-            place = 0 if base == 0 else RIM
-            if r < sent:
-                up_ref[place + r] = row
-            if r >= ROWS - sent:
-                down_ref[place + r - (ROWS - sent)] = row
+        parts = row_of(first, r), row_of(second, r)
+        goal = row_of(truth, r)
+        latent = parts[0] + parts[1]
+        own_ref[r] = latent
+        own_ref[ROWS + r] = goal
+        sent, place = (up_ref, r) if r < RIM else (down_ref, ROWS - 1 - r)
+        if place < HALF:
+            near = r if r < RIM else r - (ROWS - HALF)
+            sent[near] = parts[0].astype(bf16)
+            sent[HALF + near] = parts[1].astype(bf16)
+            sent[3 * HALF + near] = goal.astype(bf16)
+        else:
+            centered, scale = centred(latent)
+            outer = r - HALF if r < RIM else r - RIM
+            sent[2 * HALF + outer] = (centered * scale * gain).astype(bf16)
 
 
 def latent_row(own_ref, top_ref, bottom_ref, row):
+    def near(rim_ref, r):
+        return rim_ref[r].astype(f32) + rim_ref[HALF + r].astype(f32)
+
+    if row < HALF:
+        return top_ref[2 * HALF + row].astype(f32)
     if row < RIM:
-        return top_ref[row]
+        return near(top_ref, row - HALF)
     if row < RIM + ROWS:
         return own_ref[row - RIM]
-    return bottom_ref[row - RIM - ROWS]
+    if row < RIM + ROWS + HALF:
+        return near(bottom_ref, row - RIM - ROWS)
+    return bottom_ref[2 * HALF + row - RIM - ROWS - HALF].astype(f32)
 
 
 def truth_row(own_ref, top_ref, bottom_ref, row):
-    half = RIM // 2
-    if row < half:
-        return top_ref[RIM + row]
-    if row < half + ROWS:
-        return own_ref[ROWS + row - half]
-    return bottom_ref[RIM + row - half - ROWS]
+    if row < HALF:
+        return top_ref[3 * HALF + row].astype(f32)
+    if row < HALF + ROWS:
+        return own_ref[ROWS + row - HALF]
+    return bottom_ref[3 * HALF + row - HALF - ROWS].astype(f32)
 
 
 def columns_kernel(own_ref, top_ref, bottom_ref, left_ref, right_ref):
@@ -127,34 +179,40 @@
 def forward_kernel(
     member_ref, own_ref, top_ref, bottom_ref, left_ref, right_ref, gain_ref, valid_ref, mine_ref, w1_ref, w2_ref,
     forecast_ref, truth_ref, pre_ref, hidden_ref, window_ref, latent_ref,
-    latent, normed, window, hidden, partial, truth,
+    latent, normed, window, hidden, partial, truth, pre_kept, hidden_kept, semaphores,
 ):
     pieces, truths = [], []
     for row in range(TALL):
         pieces.append((functools.partial(latent_row, own_ref, top_ref, bottom_ref, row), 0, PITCH * row + RIM, COLS))
         pieces.append((lambda: left_ref[...], RIM * row, PITCH * row, RIM))
         pieces.append((lambda: right_ref[...], RIM * row, PITCH * row + RIM + COLS, RIM))
-    half = RIM // 2
+    half = HALF
     for row in range(ROWS + RIM):
         flat, lane = PITCH * (row + half) + RIM, RIM * TALL + half * row
         truths.append((functools.partial(truth_row, own_ref, top_ref, bottom_ref, row), 0, flat, COLS))
         truths.append((lambda: left_ref[...], lane, flat - half, half))
         truths.append((lambda: right_ref[...], lane, flat + COLS, half))
-    real = lax.broadcasted_iota(jnp.int32, (CP, 128), 0) < C
-    gain = gain_ref[...]
+    gain = gain_column(gain_ref)
+    lane = lanes_of(CP)
+    inner_low, inner_high = PITCH * HALF, PITCH * (TALL - HALF)
     normed[CP:CI, :] = jnp.zeros((CI - CP, FLAT), f32)
     for index, values in flat_tiles(pieces, 0, TILES):
         latent[:, tile(index)] = values
-        average = jnp.sum(values, axis=0, keepdims=True) * (1.0 / C)
-        centered = jnp.where(real, values - average, 0.0)
-        variance = jnp.sum(centered * centered, axis=0, keepdims=True) * (1.0 / C)
-        scaled = centered * lax.rsqrt(variance + norm_eps) * gain
-        normed[0:CP, tile(index)] = scaled * valid_ref[:, tile(index)]
+        start = 128 * index
+        if start < inner_high and start + 128 > inner_low:
+            centered, scale = centred(values)
+            scaled = centered * scale * gain
+            if start < inner_low or start + 128 > inner_high:
+                inside = (lane >= inner_low - start) & (lane < inner_high - start)
+                scaled = jnp.where(inside, scaled, values)
+            values = scaled
+        normed[0:CP, tile(index)] = values * valid_ref[:, tile(index)]
+    own = pl.ds(128 * OWN[0], 128 * (OWN[1] - OWN[0]))
+    moves = started((latent.at[:, own], latent_ref), semaphores=semaphores)
     for index, values in flat_tiles(truths, *SPREAD):
         truth[pl.ds(CP * (index - SPREAD[0]), CP), :] = values
     truth[pl.ds(CP * (SPREAD[1] - SPREAD[0]), 8), :] = jnp.zeros((8, 128), f32)
     truth_ref[...] = truth[pl.ds(pl.multiple_of(member_ref[0] * CHUNK, 8), CHUNK), :]
-    latent_ref[...] = latent[:, 128 * OWN[0] : 128 * OWN[1]]
 
     for group in range(CI // 16):
         values = normed[16 * group : 16 * group + 16, :]
@@ -162,17 +220,18 @@
             shift = -step_of(offset) % FLAT
             moved = pltpu.roll(values, shift, 1) if shift else values
             window[CI * offset + 16 * group : CI * offset + 16 * group + 16, :] = moved.astype(bf16)
-    window_ref[...] = window[:, 128 * OWN[0] : 128 * OWN[1]]
+    moves += started((window.at[:, own], window_ref), semaphores=semaphores.at[1:2])
 
     for first, last in ((0, 3), (3, 7), (7, 11), (11, 14), (14, 17)):
         span = slice(128 * first, 128 * last)
         pre = jnp.dot(w1_ref[...], window[:, span], preferred_element_type=f32)
         if first >= HIDDEN[0] and last <= HIDDEN[1]:
-            pre_ref[:, 128 * (first - HIDDEN[0]) : 128 * (last - HIDDEN[0])] = pre
+            pre_kept[:, 128 * (first - HIDDEN[0]) : 128 * (last - HIDDEN[0])] = pre
         curve = jnp.tanh(GELU_A * (pre + GELU_B * (pre * pre * pre)))
         hidden[:, span] = (0.5 * pre * (1.0 + curve) * valid_ref[:, span]).astype(bf16)
         partial[:, span] = jnp.dot(w2_ref[...], hidden[:, span], preferred_element_type=f32)
-    hidden_ref[...] = (hidden[:, 128 * OWN[0] : 128 * OWN[1]].astype(f32) * mine_ref[...]).astype(bf16)
+    hidden_kept[...] = (hidden[:, 128 * OWN[0] : 128 * OWN[1]].astype(f32) * mine_ref[...]).astype(bf16)
+    moves += started((pre_kept, pre_ref), (hidden_kept, hidden_ref), semaphores=semaphores.at[2:4])
 
     for group in range(CP // 8):
         total = None
@@ -188,6 +247,8 @@
                 total[:, 128 * index : 128 * index + 128] + latent[8 * group : 8 * group + 8, tile(index)]
             )
     forecast_ref[pl.ds(CP * (SPREAD[1] - SPREAD[0]), 8), :] = jnp.zeros((8, 128), f32)
+    for move in moves:
+        move.wait()
 
 
 def soft_slope(values):
@@ -214,10 +275,11 @@
 
 
 def backward_kernel(
-    grad_ref, pre_ref, hidden_ref, window_ref, latent_ref, gain_ref, valid_ref, mine_ref, w2_ref, w1_ref,
-    states_ref, weights_ref,
-    chunks, grad, window, grad_pre, partial, shifted, result, packed,
+    grad_ref, pre_far, hidden_far, window_far, valid_ref, mine_ref, w2_ref,
+    grad_pre_ref, own_grad_ref, weights_ref,
+    pre_ref, hidden_ref, window_ref, chunks, grad, window, grad_pre, packed, semaphores,
 ):
+    moves = started((hidden_far, hidden_ref), (pre_far, pre_ref), (window_far, window_ref), semaphores=semaphores)
     for m in range(MEMBERS):
         chunks[CHUNK * m : CHUNK * m + CHUNK, :] = grad_ref[m].astype(f32)
     edge = 128 * SPREAD[0]
@@ -234,13 +296,17 @@
             shift = step_of(offset) % FLAT
             moved = pltpu.roll(values, shift, 1) if shift else values
             window[CI * offset + 16 * group : CI * offset + 16 * group + 16, :] = moved[:, low:high].astype(bf16)
+    own = pl.ds(128 * OWN[0], 128 * (OWN[1] - OWN[0]))
+    later = started((grad.at[0:CP, own], own_grad_ref), semaphores=semaphores.at[3:4])
     inner = slice(128 * (OWN[0] - HIDDEN[0]), 128 * (OWN[1] - HIDDEN[0]))
+    moves[0].wait()
     across = (((1,), (1,)), ((), ()))
     grad_out = lax.dot_general(window[:, inner], hidden_ref[...], across, preferred_element_type=f32)
     for k in range(9):
         values = grad_out[CI * k : CI * k + C, :]
         packed[C * (9 + k) : C * (10 + k), :] = values[:, 0:128]
         packed[C * (18 + k) : C * (19 + k), 64:128] = values[:, 128:192]
+    moves[1].wait()
     for first, last in ((0, 4), (4, 8), (8, 11)):
         span = slice(128 * first, 128 * last)
         grad_hidden = jnp.dot(w2_ref[...], window[:, span], preferred_element_type=f32)
@@ -250,8 +316,9 @@
         slope = 0.5 * (1.0 + curve) + 0.5 * pre * (1.0 - curve * curve) * (GELU_A * (1.0 + 3.0 * GELU_B * square))
         live = valid_ref[:, low + 128 * first : low + 128 * last]
         grad_pre[:, span] = (grad_hidden * slope * live).astype(bf16)
-        partial[:, span] = jnp.dot(w1_ref[...], grad_pre[:, span], preferred_element_type=f32)
+    later += started((grad_pre, grad_pre_ref), semaphores=semaphores.at[4:5])
     own_pre = (grad_pre[:, inner].astype(f32) * mine_ref[...]).astype(bf16)
+    moves[2].wait()
     grad_in = lax.dot_general(window_ref[...], own_pre, across, preferred_element_type=f32)
     for k in range(9):
         values = grad_in[CI * k : CI * k + C, :]
@@ -260,8 +327,22 @@
     packed[27 * C :, :] = jnp.zeros((GROUPS * PIECE - 27 * C, 128), f32)
     for place in range(GROUPS):
         weights_ref[place] = packed[PIECE * place : PIECE * place + PIECE, :].astype(bf16)
-
-    span = high - low
+    for move in later:
+        move.wait()
+
+
+def states_kernel(
+    grad_pre_far, grad_far, latent_far, gain_ref, w1_ref,
+    states_ref,
+    grad_pre, grad, latent, partial, shifted, result, semaphores,
+):
+    moves = started((grad_pre_far, grad_pre), (latent_far, latent), (grad_far, grad), semaphores=semaphores)
+    span = 128 * (HIDDEN[1] - HIDDEN[0])
+    inner = slice(128 * (OWN[0] - HIDDEN[0]), 128 * (OWN[1] - HIDDEN[0]))
+    moves[0].wait()
+    for first in range(0, span, 512):
+        some = slice(first, min(first + 512, span))
+        partial[:, some] = jnp.dot(w1_ref[...], grad_pre[:, some], preferred_element_type=f32)
     for group in range(CP // 8):
         total = None
         for offset in range(9):
@@ -271,21 +352,16 @@
             moved = pltpu.roll(values, shift, 1) if shift else values
             total = moved if total is None else total + moved
         shifted[8 * group : 8 * group + 8, :] = total[:, inner]
-    real = lax.broadcasted_iota(jnp.int32, (CP, 128), 0) < C
-    gain = gain_ref[...]
+    gain = gain_column(gain_ref)
+    for move in moves[1:]:
+        move.wait()
     for index in range(OWN[1] - OWN[0]):
-        values = latent_ref[:, tile(index)]
-        average = jnp.sum(values, axis=0, keepdims=True) * (1.0 / C)
-        centered = jnp.where(real, values - average, 0.0)
-        variance = jnp.sum(centered * centered, axis=0, keepdims=True) * (1.0 / C)
-        scale = lax.rsqrt(variance + norm_eps)
+        centered, scale = centred(latent[:, tile(index)])
         unit = centered * scale
         pull = shifted[:, tile(index)] * gain
         mean_pull = jnp.sum(pull, axis=0, keepdims=True) * (1.0 / C)
         mean_both = jnp.sum(pull * unit, axis=0, keepdims=True) * (1.0 / C)
-        shifted[:, tile(index)] = (
-            grad[0:CP, tile(index + OWN[0])] + scale * (pull - mean_pull - unit * mean_both)
-        )
+        shifted[:, tile(index)] = grad[:, tile(index)] + scale * (pull - mean_pull - unit * mean_both)
     lane = lanes_of(CP)
     for row in range(ROWS):
         start = PITCH * (row + RIM) + RIM - 128 * OWN[0]
@@ -342,20 +418,22 @@
     first_stencil_kernel,
     second_stencil_kernel,
 ):
-    def rows(values):
-        return values.reshape(C * ROWS, COLS)
-
     def padded(weight, dim, size):
         pads = [(0, 0)] * 3
         pads[dim] = (0, size - weight.shape[dim])
         return jnp.pad(weight, pads)
 
+    member_axes, plane = ("half", "ring"), ("half", "lat", "lon")
+    gain = feature_scale_factor[None]
+    block = (C, ROWS, COLS)
+    rim = ((4 * HALF, CP, 128), bf16)
     own, up, down = call(
         rows_kernel,
         6,
-        [((2 * ROWS, CP, 128), f32), ((RIM + RIM // 2, CP, 128), f32), ((RIM + RIM // 2, CP, 128), f32)],
-        [((C * ROWS, COLS), f32)] * 2,
-        rows(embeddings), rows(entry_perturbation), rows(target),
+        [((2 * ROWS, CP, 128), f32), rim, rim],
+        [(block, bf16)] * 3 + [((C * ROWS, COLS), f32)] * 3,
+        embeddings.reshape(block), entry_perturbation.reshape(block), target, gain,
+        far=(0, 1, 2), copies=3,
     )
     forward, backward = neighbours("lat", False)
     top = lax.ppermute(down, "lat", forward)
@@ -367,7 +445,6 @@
     left = lax.ppermute(to_right, "lon", forward)
     right = lax.ppermute(to_left, "lon", backward)
 
-    gain = jnp.broadcast_to(jnp.pad(feature_scale_factor, (0, CP - C))[:, None], (CP, 128))
     place = jnp.arange(FLAT, dtype=jnp.int32)
     row, column = place // PITCH - RIM, place % PITCH - RIM
     line = row + ROWS * lax.axis_index("lat")
@@ -379,7 +456,7 @@
     w2_turned = padded(second_stencil_kernel, 1, CI).transpose(2, 0, 1).reshape(HID, 9 * CI)
     w1_turned = padded(first_stencil_kernel.transpose(0, 2, 1), 1, CP).reshape(9 * CP, HID)
 
-    member = lax.axis_index("member").astype(jnp.int32)[None]
+    member = lax.axis_index(member_axes).astype(jnp.int32)[None]
     own_lanes = 128 * (OWN[1] - OWN[0])
     hidden_lanes = 128 * (HIDDEN[1] - HIDDEN[0])
     forecast, truth, pre, hidden, window, latent = call(
@@ -388,10 +465,10 @@
         [
             ((MEMBERS * CHUNK, 128), f32),
             ((CHUNK, 128), f32),
-            ((HID, hidden_lanes), f32),
-            ((HID, own_lanes), bf16),
-            ((9 * CI, own_lanes), bf16),
-            ((CP, own_lanes), f32),
+            ((HID, hidden_lanes), (f32,)),
+            ((HID, own_lanes), (bf16,)),
+            ((9 * CI, own_lanes), (bf16,)),
+            ((CP, own_lanes), (f32,)),
         ],
         [
             ((CP, FLAT), f32),
@@ -400,10 +477,13 @@
             ((HID, FLAT), bf16),
             ((9 * CP, FLAT), f32),
             ((MEMBERS * CHUNK, 128), f32),
+            ((HID, hidden_lanes), f32),
+            ((HID, own_lanes), bf16),
         ],
-        member, own, top, bottom, left, right, gain, valid, mine, w1_stack, w2_stack, smem=1,
-    )
-    spread = swap(forecast.reshape(MEMBERS, CHUNK, 128), "member")
+        member, own, top, bottom, left, right, gain, valid, mine, w1_stack, w2_stack,
+        smem=1, copies=4,
+    )
+    spread = swap(forecast.reshape(MEMBERS, CHUNK, 128), member_axes)
     (grads,) = call(
         score_kernel,
         6,
@@ -411,51 +491,66 @@
         [((MEMBERS, CHUNK, 128), f32)],
         spread, truth,
     )
-    grads = swap(grads, "member")
-    states, weights = call(
+    grads = swap(grads, member_axes)
+    grad_pre, own_grad, weights = call(
         backward_kernel,
-        24,
-        [((C * ROWS, COLS), bf16), ((GROUPS, PIECE, 128), bf16)],
+        22,
         [
+            ((HID, hidden_lanes), (bf16,)),
+            ((CP, own_lanes), (f32,)),
+            ((GROUPS, PIECE, 128), bf16),
+        ],
+        [
+            ((HID, hidden_lanes), f32),
+            ((HID, own_lanes), bf16),
+            ((9 * CI, own_lanes), bf16),
             ((MEMBERS * CHUNK, 128), f32),
             ((CI, FLAT), f32),
             ((9 * CI, hidden_lanes), bf16),
             ((HID, hidden_lanes), bf16),
+            ((GROUPS * PIECE, 128), f32),
+        ],
+        grads, pre, hidden, window, valid, mine, w2_turned,
+        far=(1, 2, 3), copies=5,
+    )
+    parts = swap(weights, plane)
+    (states,) = call(
+        states_kernel,
+        14,
+        [((C * ROWS, COLS), bf16)],
+        [
+            ((HID, hidden_lanes), bf16),
+            ((CP, own_lanes), f32),
+            ((CP, own_lanes), f32),
             ((9 * CP, hidden_lanes), f32),
             ((CP, own_lanes), f32),
             ((C * ROWS, COLS), f32),
-            ((GROUPS * PIECE, 128), f32),
         ],
-        grads, pre, hidden, window, latent, gain, valid, mine, w2_turned, w1_turned,
-    )
-    across, along = ("member", "lat"), "lon"
+        grad_pre, own_grad, latent, gain, w1_turned,
+        far=(0, 1, 2), copies=3,
+    )
     piece = (PIECE, 128)
-    (copies,) = call(total_kernel, 6, [((4,) + piece, bf16)], [], swap(weights, across))
-    (copies,) = call(total_kernel, 6, [((GROUPS,) + piece, bf16)], [], swap(copies, along))
+    (copies,) = call(total_kernel, 6, [((RING,) + piece, bf16)], [], parts)
+    (copies,) = call(total_kernel, 6, [((GROUPS,) + piece, bf16)], [], swap(copies, "ring"))
     grad_in, grad_out = call(
         weights_kernel,
         8,
         [((9, C, HID), f32), ((9, C, HID), f32)],
         [((GROUPS * PIECE, 128), f32)],
-        swap(copies, across),
+        swap(copies, plane),
     )
     grad_in = grad_in.transpose(0, 2, 1)
     return (states.reshape(embeddings.shape), grad_in, grad_out)
 
 
 def solution(mesh):
-    placed = (
-        P("member", None, "lat", "lon"),
-        P("member", None, "lat", "lon"),
-        P(None, "lat", "lon"),
-        P(),
-        P(),
-        P(),
-    )
+    places = mesh.devices.reshape(MEMBERS // RING, RING, *mesh.devices.shape[1:])
+    fine = jax.sharding.Mesh(places, ("half", "ring", "lat", "lon"))
+    whole = P(("half", "ring"), None, "lat", "lon")
     return jax.shard_map(
         on_device,
-        mesh=mesh,
-        in_specs=placed,
-        out_specs=(P("member", None, "lat", "lon"), P(), P()),
+        mesh=fine,
+        in_specs=(whole, whole, P(None, "lat", "lon"), P(), P(), P()),
+        out_specs=(whole, P(), P()),
         check_vma=False,
     )

time: 148 us -> 140 us (0.946)
  blocking collectives: 87.2 us -> 57 us
  waiting for transfers between devices: 19.8 us -> 28.1 us
  Pallas kernels: 13.8 us -> 21 us
  starting transfers between devices: 13.8 us -> 19.8 us
  local copies, waits for them, and re-layouts: 10.5 us -> 12.6 us
    all_to_all x4 -> x3, blocking collectives: 87.2 us -> 57 us  [swap(): return lax.all_to_all(values, axes, split_axis=0, concat_axis=0, tiled=True)]
    all_to_all x1 -> x2, waiting for transfers between devices: 7.76 us -> 18.9 us  [swap(): return lax.all_to_all(values, axes, split_axis=0, concat_axis=0, tiled=True)]
    pallas_call x8 -> x9, Pallas kernels: 13.8 us -> 21 us  [call(): pl.pallas_call(kernel, out_shape=[jax.ShapeDtypeStruct(shape, kind) for (...]
    all_to_all x1 -> x2, starting transfers between devices: 3.72 us -> 9.8 us  [swap(): return lax.all_to_all(values, axes, split_axis=0, concat_axis=0, tiled=True)]
    unnamed x34 -> x42, local copies, waits for them, and re-layouts: 6.96 us -> 9.91 us
    ppermute x1, waiting for transfers between devices: 3.69 us -> 1.78 us  [on_device(): top = lax.ppermute(down, 'lat', forward)]
  transfers between devices with their start and end apart: 5 -> 6, of which waited for: 5 -> 5; matrix products, arithmetic and copies ran while one was open for 2% -> 2% of each run, Pallas kernels for 0% -> 2%
where the time goes in v4:
time: 140 us; the launch traced here: 139 us
  blocking collectives  57 us (41%)
  waiting for transfers between devices  28.1 us (20%)
  Pallas kernels  21 us (15%)
  starting transfers between devices  19.8 us (14%)
  local copies, waits for them, and re-layouts  12.6 us (9%)
    all_to_all x3, blocking collectives, swap(): return lax.all_to_all(values, axes, split_axis=0, concat_axis=0, tiled=True)  57 us
    pallas_call x9, Pallas kernels, call(): pl.pallas_call(kernel, out_shape=[jax.ShapeDtypeStruct(shape, kind) for (...  21 us
    all_to_all x2, waiting for transfers between devices, swap(): return lax.all_to_all(values, axes, split_axis=0, concat_axis=0, tiled=True)  18.9 us
    unnamed x42, local copies, waits for them, and re-layouts  9.91 us
    all_to_all x2, starting transfers between devices, swap(): return lax.all_to_all(values, axes, split_axis=0, concat_axis=0, tiled=True)  9.8 us
    ppermute x1, starting transfers between devices, on_device(): left = lax.ppermute(to_right, 'lon', forward)  4.74 us
    ppermute x1, starting transfers between devices, on_device(): top = lax.ppermute(down, 'lat', forward)  3.96 us
    ppermute x1, waiting for transfers between devices, on_device(): bottom = lax.ppermute(up, 'lat', backward)  3.8 us
  transfers between devices with their start and end apart: 6, of which 5 were waited for; matrix products, arithmetic and copies ran while one was open for 2% of the time, Pallas kernels for 2%

profile of v4, /device:TPU:1, one launch (start us, length us, event | category | flops | bytes accessed | tf_op | source)
XLA Modules:
  0.0 139.5 jit_solution(6414971554053301528)
XLA Ops:
  0.6 0.9 copy-done.12
  1.6 0.9 copy-done.13
  2.5 0.9 copy-done.14
  3.4 0.7 copy-done.17
  4.0 1.0 shard_map.85
  5.0 4.0 %collective-permute-start = (bf16[8,88,128]{2,1,0:T(8,128)(2,1)S(1)}, bf16[8,88,128]{2,1,0:T(8,128)(2,1)S(1)}, u32[]{:S(2)}, u32[]{:S(2)}) collective-permute-start(bf16[8,88,128]{2,1,0:T(8,128)(2,1)S(1)} %get-tuple-element.20), channel_id=1, source_target_pairs={{0,4},{4,8},{8,12},{1,5},{5,9},{9,13},{2,6},{6,10},{10,14},{3,7},{... | collective-permute-start | bytes 540680 | tf_op jit(solution)/shard_map/ppermute | solution.py:439
  9.0 1.3 collective-permute-start.1
  10.4 1.8 %collective-permute-done.top_ref = bf16[8,88,128]{2,1,0:T(8,128)(2,1)S(1)} collective-permute-done((bf16[8,88,128]{2,1,0:T(8,128)(2,1)S(1)}, bf16[8,88,128]{2,1,0:T(8,128)(2,1)S(1)}, u32[]{:S(2)}, u32[]{:S(2)}) %collective-permute-start) | collective-permute-done | bytes 180256 | tf_op jit(solution)/shard_map/ppermute | solution.py:439
  12.2 3.8 %collective-permute-done.1.bottom_ref = bf16[8,88,128]{2,1,0:T(8,128)(2,1)S(1)} collective-permute-done((bf16[8,88,128]{2,1,0:T(8,128)(2,1)S(1)}, bf16[8,88,128]{2,1,0:T(8,128)(2,1)S(1)}, u32[]{:S(2)}, u32[]{:S(2)}) %collective-permute-start.1) | collective-permute-done | bytes 180256 | tf_op jit(solution)/shard_map/ppermute | solution.py:440
  16.6 4.7 %collective-permute-start.2 = (f32[88,128]{1,0:T(8,128)S(1)}, f32[88,128]{1,0:T(8,128)S(1)}, u32[]{:S(2)}, u32[]{:S(2)}) collective-permute-start(f32[88,128]{1,0:T(8,128)S(1)} %get-tuple-element.22), channel_id=1, source_target_pairs={{0,1},{1,2},{2,3},{3,0},{4,5},{5,6},{6,7},{7,4},{8,9},{9,10},{10,1... | collective-permute-start | bytes 135176 | tf_op jit(solution)/shard_map/ppermute | solution.py:445
  21.4 1.1 pad.15
  22.8 3.5 %collective-permute-done.3.right_ref = f32[88,128]{1,0:T(8,128)S(1)} collective-permute-done((f32[88,128]{1,0:T(8,128)S(1)}, f32[88,128]{1,0:T(8,128)S(1)}, u32[]{:S(2)}, u32[]{:S(2)}) %collective-permute-start.3) | collective-permute-done | bytes 45088 | tf_op jit(solution)/shard_map/ppermute | solution.py:446
  27.0 0.9 copy-done.3
  27.9 0.9 copy-done.5
  28.8 0.8 copy-done.16
  29.6 7.2 %shard_map.87 = (f32[1152,128]{1,0:T(8,128)S(1)}, f32[72,128]{1,0:T(8,128)S(1)}, f32[192,1408]{1,0:T(8,128)S(1)}, bf16[192,1152]{1,0:T(8,128)(2,1)S(1)}, bf16[86...) custom-call(s32[1]{0:T(128)} %bitcast.member_ref, f32[16,88,128]{2,1,0:T(8,128)S(1)} %get-tuple-element.19.own_ref, ...), custom_call_target="tpu_custom_call" | custom-call | tf_op jit(solution)/shard_map/pallas_call | solution.py:46
  36.8 1.0 copy-done
  37.8 26.4 %all_to_all.25.forecast_ref = f32[16,72,128]{2,1,0:T(8,128)S(1)} all-to-all(f32[16,72,128]{2,1,0:T(8,128)S(1)} %bitcast.18), channel_id=1, replica_groups=mesh['half'=2,'ring'=8,'lat'=4,'lon'=4] {'half','ring'}, dimensions={0} | all-to-all | bytes 1179648 | tf_op jit(solution)/shard_map/all_to_all | solution.py:410
  64.2 1.9 %shard_map.88 = bf16[16,72,128]{2,1,0:T(8,128)(2,1)} custom-call(f32[16,72,128]{2,1,0:T(8,128)S(1)} %all_to_all.25.forecast_ref, f32[72,128]{1,0:T(8,128)S(1)} %get-tuple-element.25.truth_ref), custom_call_target="tpu_custom_call" | custom-call | tf_op jit(solution)/shard_map/pallas_call | solution.py:46
  66.1 3.7 %all-to-all-start.1 = ((bf16[16,72,128]{2,1,0:T(8,128)(2,1)}), bf16[16,72,128]{2,1,0:T(8,128)(2,1)S(1)}, u32[]{:S(2)}, u32[]{:S(2)}) async-start(bf16[16,72,128]{2,1,0:T(8,128)(2,1)} %shard_map.88), calls=%async_computation.1 | async-start | bytes 589824 | tf_op jit(solution)/shard_map/all_to_all | solution.py:410
  69.8 1.1 pad.17
  71.1 9.6 %all-to-all-done.1.grad_ref = bf16[16,72,128]{2,1,0:T(8,128)(2,1)S(1)} async-done(((bf16[16,72,128]{2,1,0:T(8,128)(2,1)}), bf16[16,72,128]{2,1,0:T(8,128)(2,1)S(1)}, u32[]{:S(2)}, u32[]{:S(2)}) %all-to-all-start.1) | async-done | bytes 294944 | tf_op jit(solution)/shard_map/all_to_all | solution.py:410
  80.7 1.2 copy-done.1
  82.0 1.0 copy-done.7
  83.0 5.2 %shard_map.89 = (bf16[192,1408]{1,0:T(8,128)(2,1)S(1)}, f32[88,1152]{1,0:T(8,128)S(1)}, bf16[32,72,128]{2,1,0:T(8,128)(2,1)S(1)}) custom-call(bf16[16,72,128]{2,1,0:T(8,128)(2,1)S(1)} %all-to-all-done.1.grad_ref, f32[192,1408]{1,0:T(8,128)S(1)} %copy-done.1, bf16[192,1152]{1,0:T(8,128)(2,1)S(1)} %copy-done.7, ...), custom_call_target="tpu_custom_call" | custom-call | tf_op jit(solution)/shard_map/pallas_call | solution.py:46
  88.2 18.6 %all_to_all.26.parts_ref = bf16[32,72,128]{2,1,0:T(8,128)(2,1)S(1)} all-to-all(bf16[32,72,128]{2,1,0:T(8,128)(2,1)S(1)} %get-tuple-element.32), channel_id=1, replica_groups=mesh['half'=2,'ring'=8,'lat'=4,'lon'=4] {'half','lat','lon'}, dimensions={0} | all-to-all | bytes 1179648 | tf_op jit(solution)/shard_map/all_to_all | solution.py:410
  106.9 12.0 %all_to_all.27.parts_ref = bf16[8,72,128]{2,1,0:T(8,128)(2,1)S(1)} all-to-all(bf16[8,72,128]{2,1,0:T(8,128)(2,1)S(1)} %shard_map.91), channel_id=1, replica_groups=mesh['half'=2,'ring'=8,'lat'=4,'lon'=4] {'ring'}, dimensions={0} | all-to-all | bytes 294912 | tf_op jit(solution)/shard_map/all_to_all | solution.py:410
  118.9 0.9 shard_map.92
  119.7 6.1 %all-to-all-start.4 = ((bf16[32,72,128]{2,1,0:T(8,128)(2,1)}), bf16[32,72,128]{2,1,0:T(8,128)(2,1)S(1)}, u32[]{:S(2)}, u32[]{:S(2)}) async-start(bf16[32,72,128]{2,1,0:T(8,128)(2,1)} %shard_map.92), calls=%async_computation.4 | async-start | bytes 1179648 | tf_op jit(solution)/shard_map/all_to_all | solution.py:410
  125.9 2.8 %shard_map.90 = bf16[664,128]{1,0:T(8,128)(2,1)} custom-call(bf16[192,1408]{1,0:T(8,128)(2,1)S(1)} %get-tuple-element.29.grad_pre_far, f32[88,1152]{1,0:T(8,128)S(1)} %copy-done.11, f32[88,1152]{1,0:T(8,128)S(1)} %copy-done.9, f32[1,83]{1,0:T(1,128)S(1)} %bitcast.23, bf16[792,192]{1,0:T(8,128)(2,1)S(1)} %bitcast.16), custom_call_target="tpu_custom_call" | custom-call | tf_op jit(solution)/shard_map/pallas_call | solution.py:46
  128.8 9.3 %all-to-all-done.4.parts_ref = bf16[32,72,128]{2,1,0:T(8,128)(2,1)S(1)} async-done(((bf16[32,72,128]{2,1,0:T(8,128)(2,1)}), bf16[32,72,128]{2,1,0:T(8,128)(2,1)S(1)}, u32[]{:S(2)}, u32[]{:S(2)}) %all-to-all-start.4) | async-done | bytes 589856 | tf_op jit(solution)/shard_map/all_to_all | solution.py:410
  138.1 1.4 shard_map.93
  (44 shorter events, 2.1 us)
Async XLA Ops:
  0.6 0.9 copy-start.12
  1.6 0.9 copy-start.13
  2.5 0.9 copy-start.14
  3.4 0.7 copy-start.17
  4.0 18.7 %copy-start.19 = (bf16[9,83,192]{2,1,0:T(8,128)(2,1)S(1)}, bf16[9,83,192]{2,1,0:T(8,128)(2,1)}, u32[]{:S(2)}) copy-start(bf16[9,83,192]{2,1,0:T(8,128)(2,1)} %param.11) | copy-start | bytes 860548
  4.0 22.9 %copy-start.18 = (f32[83]{0:T(128)S(1)}, f32[83]{0:T(128)}, u32[]{:S(2)}) copy-start(f32[83]{0:T(128)} %param.9) | copy-start | bytes 1000
  5.0 7.2 %collective-permute-start = (bf16[8,88,128]{2,1,0:T(8,128)(2,1)S(1)}, bf16[8,88,128]{2,1,0:T(8,128)(2,1)S(1)}, u32[]{:S(2)}, u32[]{:S(2)}) collective-permute-start(bf16[8,88,128]{2,1,0:T(8,128)(2,1)S(1)} %get-tuple-element.20), channel_id=1, source_target_pairs={{0,4},{4,8},{8,12},{1,5},{5,9},{9,13},{2,6},{6,10},{10,14},{3,7},{... | collective-permute-start | bytes 540680 | tf_op jit(solution)/shard_map/ppermute | solution.py:439
  9.0 7.0 %collective-permute-start.1 = (bf16[8,88,128]{2,1,0:T(8,128)(2,1)S(1)}, bf16[8,88,128]{2,1,0:T(8,128)(2,1)S(1)}, u32[]{:S(2)}, u32[]{:S(2)}) collective-permute-start(bf16[8,88,128]{2,1,0:T(8,128)(2,1)S(1)} %get-tuple-element.21), channel_id=1, source_target_pairs={{4,0},{8,4},{12,8},{5,1},{9,5},{13,9},{6,2},{10,6},{14,10},{7,3},{... | collective-permute-start | bytes 540680 | tf_op jit(solution)/shard_map/ppermute | solution.py:440
  12.2 14.8 %copy-start.2 = (bf16[8,88,128]{2,1,0:T(8,128)(2,1)}, bf16[8,88,128]{2,1,0:T(8,128)(2,1)S(1)}, u32[]{:S(2)}) copy-start(bf16[8,88,128]{2,1,0:T(8,128)(2,1)S(1)} %collective-permute-done.top_ref) | copy-start | bytes 540676
  16.0 11.0 %copy-start.4 = (bf16[8,88,128]{2,1,0:T(8,128)(2,1)}, bf16[8,88,128]{2,1,0:T(8,128)(2,1)S(1)}, u32[]{:S(2)}) copy-start(bf16[8,88,128]{2,1,0:T(8,128)(2,1)S(1)} %collective-permute-done.1.bottom_ref) | copy-start | bytes 540676
  16.6 6.2 %collective-permute-start.2 = (f32[88,128]{1,0:T(8,128)S(1)}, f32[88,128]{1,0:T(8,128)S(1)}, u32[]{:S(2)}, u32[]{:S(2)}) collective-permute-start(f32[88,128]{1,0:T(8,128)S(1)} %get-tuple-element.22), channel_id=1, source_target_pairs={{0,1},{1,2},{2,3},{3,0},{4,5},{5,6},{6,7},{7,4},{8,9},{9,10},{10,1... | collective-permute-start | bytes 135176 | tf_op jit(solution)/shard_map/ppermute | solution.py:445
  21.4 5.0 %collective-permute-start.3 = (f32[88,128]{1,0:T(8,128)S(1)}, f32[88,128]{1,0:T(8,128)S(1)}, u32[]{:S(2)}, u32[]{:S(2)}) collective-permute-start(f32[88,128]{1,0:T(8,128)S(1)} %get-tuple-element.23), channel_id=1, source_target_pairs={{1,0},{2,1},{3,2},{0,3},{5,4},{6,5},{7,6},{4,7},{9,8},{10,9},{11,1... | collective-permute-start | bytes 135176 | tf_op jit(solution)/shard_map/ppermute | solution.py:446
  26.3 0.6 copy-start.15
  27.0 0.9 copy-start.3
  27.9 0.9 copy-start.5
  28.8 0.8 copy-start.16
  36.8 1.0 copy-start
  37.8 26.4 %copy-start.6 = (bf16[192,1152]{1,0:T(8,128)(2,1)}, bf16[192,1152]{1,0:T(8,128)(2,1)S(1)}, u32[]{:S(2)}) copy-start(bf16[192,1152]{1,0:T(8,128)(2,1)S(1)} %get-tuple-element.27.hidden_far) | copy-start | bytes 1327108
  37.8 26.4 %copy-start.8 = (f32[88,1152]{1,0:T(8,128)}, f32[88,1152]{1,0:T(8,128)S(1)}, u32[]{:S(2)}) copy-start(f32[88,1152]{1,0:T(8,128)S(1)} %get-tuple-element.31.latent_far) | copy-start | bytes 1216516
  66.1 14.6 %all-to-all-start.1 = ((bf16[16,72,128]{2,1,0:T(8,128)(2,1)}), bf16[16,72,128]{2,1,0:T(8,128)(2,1)S(1)}, u32[]{:S(2)}, u32[]{:S(2)}) async-start(bf16[16,72,128]{2,1,0:T(8,128)(2,1)} %shard_map.88), calls=%async_computation.1 | async-start | bytes 589824 | tf_op jit(solution)/shard_map/all_to_all | solution.py:410
  80.7 1.2 copy-start.1
  82.0 1.0 copy-start.7
  88.2 30.7 %copy-start.10 = (f32[88,1152]{1,0:T(8,128)}, f32[88,1152]{1,0:T(8,128)S(1)}, u32[]{:S(2)}) copy-start(f32[88,1152]{1,0:T(8,128)S(1)} %get-tuple-element.30.grad_far) | copy-start | bytes 1216516
  88.2 37.7 %copy-start.20 = (bf16[9,192,83]{1,2,0:T(8,128)(2,1)S(1)}, bf16[9,192,83]{1,2,0:T(8,128)(2,1)}, u32[]{:S(2)}) copy-start(bf16[9,192,83]{1,2,0:T(8,128)(2,1)} %param.10) | copy-start | bytes 860548
  106.8 19.2 %copy-start.9 = (f32[88,1152]{1,0:T(8,128)S(1)}, f32[88,1152]{1,0:T(8,128)}, u32[]{:S(2)}) copy-start(f32[88,1152]{1,0:T(8,128)} %copy-done.8) | copy-start | bytes 1216516
  119.7 6.2 %copy-start.11 = (f32[88,1152]{1,0:T(8,128)S(1)}, f32[88,1152]{1,0:T(8,128)}, u32[]{:S(2)}) copy-start(f32[88,1152]{1,0:T(8,128)} %copy-done.10) | copy-start | bytes 1216516
  119.7 18.4 %all-to-all-start.4 = ((bf16[32,72,128]{2,1,0:T(8,128)(2,1)}), bf16[32,72,128]{2,1,0:T(8,128)(2,1)S(1)}, u32[]{:S(2)}, u32[]{:S(2)}) async-start(bf16[32,72,128]{2,1,0:T(8,128)(2,1)} %shard_map.92), calls=%async_computation.4 | async-start | bytes 1179648 | tf_op jit(solution)/shard_map/all_to_all | solution.py:410

commit v5 on v4

--- a/solution.py
+++ b/solution.py
@@ -36,16 +36,24 @@
 GELU_B = 0.044715
 
 
-def call(kernel, limit, outs, scratch, *operands, smem=0, far=(), copies=0):
+def call(kernel, limit, outs, scratch, *operands, smem=0, far=(), close=(), home=(), copies=0):
     near = pl.BlockSpec(memory_space=pltpu.VMEM)
     away = pl.BlockSpec(memory_space=pltpu.HBM)
     specs = [pl.BlockSpec(memory_space=pltpu.SMEM)] * smem
     specs += [away if i in far else near for i in range(smem, len(operands))]
     kinds = [kind[0] if isinstance(kind, tuple) else kind for _, kind in outs]
+    placed = {i: pltpu.VMEM for i in close} | {i: pltpu.HBM for i in (*far, *home)}
+    operands = [
+        pltpu.with_memory_space_constraint(operand, placed[i]) if i in placed else operand
+        for i, operand in enumerate(operands)
+    ]
     kept = [pltpu.VMEM(shape, kind) for shape, kind in scratch]
     return pl.pallas_call(
         kernel,
-        out_shape=[jax.ShapeDtypeStruct(shape, kind) for (shape, _), kind in zip(outs, kinds)],
+        out_shape=[
+            (pltpu.HBM if isinstance(given, tuple) else jax.ShapeDtypeStruct)(shape, kind)
+            for (shape, given), kind in zip(outs, kinds)
+        ],
         in_specs=specs,
         out_specs=[away if isinstance(kind, tuple) else near for _, kind in outs],
         scratch_shapes=kept + ([pltpu.SemaphoreType.DMA((copies,))] if copies else []),
@@ -222,16 +230,18 @@
             window[CI * offset + 16 * group : CI * offset + 16 * group + 16, :] = moved.astype(bf16)
     moves += started((window.at[:, own], window_ref), semaphores=semaphores.at[1:2])
 
-    for first, last in ((0, 3), (3, 7), (7, 11), (11, 14), (14, 17)):
+    for number, (first, last) in enumerate(((0, 3), (3, 7), (7, 11), (11, 14), (14, 17))):
         span = slice(128 * first, 128 * last)
         pre = jnp.dot(w1_ref[...], window[:, span], preferred_element_type=f32)
         if first >= HIDDEN[0] and last <= HIDDEN[1]:
-            pre_kept[:, 128 * (first - HIDDEN[0]) : 128 * (last - HIDDEN[0])] = pre
+            kept = pl.ds(128 * (first - HIDDEN[0]), 128 * (last - first))
+            pre_kept[:, kept] = pre
+            moves += started((pre_kept.at[:, kept], pre_ref.at[:, kept]), semaphores=semaphores.at[number + 2 : number + 3])
         curve = jnp.tanh(GELU_A * (pre + GELU_B * (pre * pre * pre)))
         hidden[:, span] = (0.5 * pre * (1.0 + curve) * valid_ref[:, span]).astype(bf16)
         partial[:, span] = jnp.dot(w2_ref[...], hidden[:, span], preferred_element_type=f32)
     hidden_kept[...] = (hidden[:, 128 * OWN[0] : 128 * OWN[1]].astype(f32) * mine_ref[...]).astype(bf16)
-    moves += started((pre_kept, pre_ref), (hidden_kept, hidden_ref), semaphores=semaphores.at[2:4])
+    moves += started((hidden_kept, hidden_ref), semaphores=semaphores.at[2:3])
 
     for group in range(CP // 8):
         total = None
@@ -433,13 +443,13 @@
         [((2 * ROWS, CP, 128), f32), rim, rim],
         [(block, bf16)] * 3 + [((C * ROWS, COLS), f32)] * 3,
         embeddings.reshape(block), entry_perturbation.reshape(block), target, gain,
-        far=(0, 1, 2), copies=3,
+        far=(0, 1, 2), home=(3,), copies=3,
     )
     forward, backward = neighbours("lat", False)
     top = lax.ppermute(down, "lat", forward)
     bottom = lax.ppermute(up, "lat", backward)
     to_left, to_right = call(
-        columns_kernel, 6, [((CP, 128), f32)] * 2, [], own, top, bottom
+        columns_kernel, 6, [((CP, 128), f32)] * 2, [], own, top, bottom, close=(0, 1, 2)
     )
     forward, backward = neighbours("lon", True)
     left = lax.ppermute(to_right, "lon", forward)
@@ -481,7 +491,7 @@
             ((HID, own_lanes), bf16),
         ],
         member, own, top, bottom, left, right, gain, valid, mine, w1_stack, w2_stack,
-        smem=1, copies=4,
+        smem=1, close=(1, 2, 3, 4, 5), copies=6,
     )
     spread = swap(forecast.reshape(MEMBERS, CHUNK, 128), member_axes)
     (grads,) = call(

time: 140 us -> 130 us (0.929)
  local copies, waits for them, and re-layouts: 12.6 us -> 1.74 us
    unnamed x42 -> x6, local copies, waits for them, and re-layouts: 9.91 us -> 0.01 us
  transfers between devices with their start and end apart: 6 -> 6, of which waited for: 5 -> 5; matrix products, arithmetic and copies ran while one was open for 2% -> 1% of each run, Pallas kernels for 2% -> 3%
where the time goes in v5:
time: 130 us; the launch traced here: 129 us
  blocking collectives  56.9 us (44%)
  waiting for transfers between devices  28.6 us (22%)
  Pallas kernels  21.3 us (16%)
  starting transfers between devices  19.5 us (15%)
  local copies, waits for them, and re-layouts  1.74 us (1%)
    all_to_all x3, blocking collectives, swap(): return lax.all_to_all(values, axes, split_axis=0, concat_axis=0, tiled=True)  56.9 us
    pallas_call x9, Pallas kernels, call(): pl.pallas_call(kernel, out_shape=[(pltpu.HBM if isinstance(given, tuple)...  21.3 us
    all_to_all x2, waiting for transfers between devices, swap(): return lax.all_to_all(values, axes, split_axis=0, concat_axis=0, tiled=True)  19.5 us
    all_to_all x2, starting transfers between devices, swap(): return lax.all_to_all(values, axes, split_axis=0, concat_axis=0, tiled=True)  9.49 us
    ppermute x1, starting transfers between devices, on_device(): left = lax.ppermute(to_right, 'lon', forward)  4.74 us
    ppermute x1, starting transfers between devices, on_device(): top = lax.ppermute(down, 'lat', forward)  3.96 us
    ppermute x1, waiting for transfers between devices, on_device(): bottom = lax.ppermute(up, 'lat', backward)  3.8 us
    ppermute x1, waiting for transfers between devices, on_device(): right = lax.ppermute(to_left, 'lon', backward)  3.53 us
  transfers between devices with their start and end apart: 6, of which 5 were waited for; matrix products, arithmetic and copies ran while one was open for 1% of the time, Pallas kernels for 3%

profile of v5, /device:TPU:1, one launch (start us, length us, event | category | flops | bytes accessed | tf_op | source)
XLA Modules:
  0.0 129.0 jit_solution(12011742269175224298)
XLA Ops:
  0.6 0.0 copy-start.1
  0.7 2.1 %shard_map.85 = (f32[16,88,128]{2,1,0:T(8,128)S(1)}, bf16[8,88,128]{2,1,0:T(8,128)(2,1)S(1)}, bf16[8,88,128]{2,1,0:T(8,128)(2,1)S(1)}) custom-call(bf16[83,8,128]{2,1,0:T(8,128)(2,1)} %bitcast.26, bf16[83,8,128]{2,1,0:T(8,128)(2,1)} %bitcast.27, bf16[83,8,128]{2,1,0:T(8,128)(2,1)} %target_ref.1, f32[1,83]{1,0:T(1,128)} %bitcast.19), custom_call_target="tpu_custom_call" | custom-call | tf_op jit(solution)/shard_map/pallas_call | solution.py:51
  2.7 4.0 %collective-permute-start = (bf16[8,88,128]{2,1,0:T(8,128)(2,1)S(1)}, bf16[8,88,128]{2,1,0:T(8,128)(2,1)S(1)}, u32[]{:S(2)}, u32[]{:S(2)}) collective-permute-start(bf16[8,88,128]{2,1,0:T(8,128)(2,1)S(1)} %get-tuple-element.20), channel_id=1, source_target_pairs={{0,4},{4,8},{8,12},{1,5},{5,9},{9,13},{2,6},{6,10},{10,14},{3,7},{... | collective-permute-start | bytes 540680 | tf_op jit(solution)/shard_map/ppermute | solution.py:449
  6.7 1.3 %collective-permute-start.1 = (bf16[8,88,128]{2,1,0:T(8,128)(2,1)S(1)}, bf16[8,88,128]{2,1,0:T(8,128)(2,1)S(1)}, u32[]{:S(2)}, u32[]{:S(2)}) collective-permute-start(bf16[8,88,128]{2,1,0:T(8,128)(2,1)S(1)} %get-tuple-element.21), channel_id=1, source_target_pairs={{4,0},{8,4},{12,8},{5,1},{9,5},{13,9},{6,2},{10,6},{14,10},{7,3},{... | collective-permute-start | bytes 540680 | tf_op jit(solution)/shard_map/ppermute | solution.py:450
  8.1 1.8 %collective-permute-done.top_ref = bf16[8,88,128]{2,1,0:T(8,128)(2,1)S(1)} collective-permute-done((bf16[8,88,128]{2,1,0:T(8,128)(2,1)S(1)}, bf16[8,88,128]{2,1,0:T(8,128)(2,1)S(1)}, u32[]{:S(2)}, u32[]{:S(2)}) %collective-permute-start) | collective-permute-done | bytes 180256 | tf_op jit(solution)/shard_map/ppermute | solution.py:449
  9.9 3.8 %collective-permute-done.1.bottom_ref = bf16[8,88,128]{2,1,0:T(8,128)(2,1)S(1)} collective-permute-done((bf16[8,88,128]{2,1,0:T(8,128)(2,1)S(1)}, bf16[8,88,128]{2,1,0:T(8,128)(2,1)S(1)}, u32[]{:S(2)}, u32[]{:S(2)}) %collective-permute-start.1) | collective-permute-done | bytes 180256 | tf_op jit(solution)/shard_map/ppermute | solution.py:450
  13.7 0.6 shard_map.86
  14.3 4.7 %collective-permute-start.2 = (f32[88,128]{1,0:T(8,128)S(1)}, f32[88,128]{1,0:T(8,128)S(1)}, u32[]{:S(2)}, u32[]{:S(2)}) collective-permute-start(f32[88,128]{1,0:T(8,128)S(1)} %get-tuple-element.22), channel_id=1, source_target_pairs={{0,1},{1,2},{2,3},{3,0},{4,5},{5,6},{6,7},{7,4},{8,9},{9,10},{10,1... | collective-permute-start | bytes 135176 | tf_op jit(solution)/shard_map/ppermute | solution.py:455
  19.1 0.0 collective-permute-start.3
  19.1 1.1 pad.15
  20.2 0.2 copy.11.w1_ref
  20.4 0.1 pad.16
  20.5 0.0 collective-permute-done.2.left_ref
  20.5 3.5 %collective-permute-done.3.right_ref = f32[88,128]{1,0:T(8,128)S(1)} collective-permute-done((f32[88,128]{1,0:T(8,128)S(1)}, f32[88,128]{1,0:T(8,128)S(1)}, u32[]{:S(2)}, u32[]{:S(2)}) %collective-permute-start.3) | collective-permute-done | bytes 45088 | tf_op jit(solution)/shard_map/ppermute | solution.py:456
  24.1 5.7 %shard_map.87 = (f32[1152,128]{1,0:T(8,128)S(1)}, f32[72,128]{1,0:T(8,128)S(1)}, f32[192,1408]{1,0:T(8,128)}, bf16[192,1152]{1,0:T(8,128)(2,1)}, bf16[864,1152]{1,0:T(8,128)(2,1)}, /*index=5*/f32[88,1152]{1,0:T(8,128)}) custom-call(s32[1]{0:T(128)} %bitcast.member_ref, f32[16,88,128]{2,1,0:T(8,128)S(1)} %get-tuple-element.19.own_ref, ...), custom_call_target="tpu_custom_call" | custom-call | tf_op jit(solution)/shard_map/pallas_call | solution.py:51
  29.7 26.4 %all_to_all.25.forecast_ref = f32[16,72,128]{2,1,0:T(8,128)S(1)} all-to-all(f32[16,72,128]{2,1,0:T(8,128)S(1)} %bitcast.18), channel_id=1, replica_groups=mesh['half'=2,'ring'=8,'lat'=4,'lon'=4] {'half','ring'}, dimensions={0} | all-to-all | bytes 1179648 | tf_op jit(solution)/shard_map/all_to_all | solution.py:420
  56.1 1.9 %shard_map.88 = bf16[16,72,128]{2,1,0:T(8,128)(2,1)} custom-call(f32[16,72,128]{2,1,0:T(8,128)S(1)} %all_to_all.25.forecast_ref, f32[72,128]{1,0:T(8,128)S(1)} %get-tuple-element.25.truth_ref), custom_call_target="tpu_custom_call" | custom-call | tf_op jit(solution)/shard_map/pallas_call | solution.py:51
  58.1 3.5 %all-to-all-start.1 = ((bf16[16,72,128]{2,1,0:T(8,128)(2,1)}), bf16[16,72,128]{2,1,0:T(8,128)(2,1)S(1)}, u32[]{:S(2)}, u32[]{:S(2)}) async-start(bf16[16,72,128]{2,1,0:T(8,128)(2,1)} %shard_map.88), calls=%async_computation.1 | async-start | bytes 589824 | tf_op jit(solution)/shard_map/all_to_all | solution.py:420
  61.6 0.1 pad.17
  61.7 0.2 copy.12.w2_ref
  61.9 10.7 %all-to-all-done.1.grad_ref = bf16[16,72,128]{2,1,0:T(8,128)(2,1)S(1)} async-done(((bf16[16,72,128]{2,1,0:T(8,128)(2,1)}), bf16[16,72,128]{2,1,0:T(8,128)(2,1)S(1)}, u32[]{:S(2)}, u32[]{:S(2)}) %all-to-all-start.1) | async-done | bytes 294944 | tf_op jit(solution)/shard_map/all_to_all | solution.py:420
  72.6 5.3 %shard_map.89 = (bf16[192,1408]{1,0:T(8,128)(2,1)}, f32[88,1152]{1,0:T(8,128)}, bf16[32,72,128]{2,1,0:T(8,128)(2,1)S(1)}) custom-call(bf16[16,72,128]{2,1,0:T(8,128)(2,1)S(1)} %all-to-all-done.1.grad_ref, f32[192,1408]{1,0:T(8,128)} %get-tuple-element.26.pre_far, bf16[192,1152]{1,0:T(8,128)(2,1)} %get-tuple-element.27.hidden_far, ...), custom_call_target="tpu_custom_call" | custom-call | tf_op jit(solution)/shard_map/pallas_call | solution.py:51
  77.9 0.0 copy-start.2
  77.9 18.6 %all_to_all.26.parts_ref = bf16[32,72,128]{2,1,0:T(8,128)(2,1)S(1)} all-to-all(bf16[32,72,128]{2,1,0:T(8,128)(2,1)S(1)} %get-tuple-element.32), channel_id=1, replica_groups=mesh['half'=2,'ring'=8,'lat'=4,'lon'=4] {'half','lat','lon'}, dimensions={0} | all-to-all | bytes 1179648 | tf_op jit(solution)/shard_map/all_to_all | solution.py:420
  96.6 0.1 shard_map.91
  96.7 11.9 %all_to_all.27.parts_ref = bf16[8,72,128]{2,1,0:T(8,128)(2,1)S(1)} all-to-all(bf16[8,72,128]{2,1,0:T(8,128)(2,1)S(1)} %shard_map.91), channel_id=1, replica_groups=mesh['half'=2,'ring'=8,'lat'=4,'lon'=4] {'ring'}, dimensions={0} | all-to-all | bytes 294912 | tf_op jit(solution)/shard_map/all_to_all | solution.py:420
  108.5 0.9 shard_map.92
  109.4 6.0 %all-to-all-start.4 = ((bf16[32,72,128]{2,1,0:T(8,128)(2,1)}), bf16[32,72,128]{2,1,0:T(8,128)(2,1)S(1)}, u32[]{:S(2)}, u32[]{:S(2)}) async-start(bf16[32,72,128]{2,1,0:T(8,128)(2,1)} %shard_map.92), calls=%async_computation.4 | async-start | bytes 1179648 | tf_op jit(solution)/shard_map/all_to_all | solution.py:420
  115.4 0.1 pad.18
  115.5 3.4 %shard_map.90 = bf16[664,128]{1,0:T(8,128)(2,1)} custom-call(bf16[192,1408]{1,0:T(8,128)(2,1)} %get-tuple-element.29.grad_pre_far, f32[88,1152]{1,0:T(8,128)} %get-tuple-element.30.grad_far, f32[88,1152]{1,0:T(8,128)} %get-tuple-element.31.latent_far, f32[1,83]{1,0:T(1,128)S(1)} %bitcast.21, bf16[792,192]{1,0:T(8,128)(2,1)S(1)} %bitcast.16), custom_call_target="tpu_custom_call" | custom-call | tf_op jit(solution)/shard_map/pallas_call | solution.py:51
  118.9 8.8 %all-to-all-done.4.parts_ref = bf16[32,72,128]{2,1,0:T(8,128)(2,1)S(1)} async-done(((bf16[32,72,128]{2,1,0:T(8,128)(2,1)}), bf16[32,72,128]{2,1,0:T(8,128)(2,1)S(1)}, u32[]{:S(2)}, u32[]{:S(2)}) %all-to-all-start.4) | async-done | bytes 589856 | tf_op jit(solution)/shard_map/all_to_all | solution.py:420
  127.6 1.4 %shard_map.93 = (f32[9,83,192]{2,1,0:T(8,128)}, f32[9,83,192]{2,1,0:T(8,128)}) custom-call(bf16[32,72,128]{2,1,0:T(8,128)(2,1)S(1)} %all-to-all-done.4.parts_ref), custom_call_target="tpu_custom_call" | custom-call | tf_op jit(solution)/shard_map/pallas_call | solution.py:51
  (8 shorter events, 0.1 us)
Async XLA Ops:
  0.6 19.8 %copy-start.1 = (bf16[9,83,192]{2,1,0:T(8,128)(2,1)S(1)}, bf16[9,83,192]{2,1,0:T(8,128)(2,1)}, u32[]{:S(2)}) copy-start(bf16[9,83,192]{2,1,0:T(8,128)(2,1)} %param.11) | copy-start | bytes 860548
  0.6 23.4 %copy-start = (f32[83]{0:T(128)S(1)}, f32[83]{0:T(128)}, u32[]{:S(2)}) copy-start(f32[83]{0:T(128)} %param.9) | copy-start | bytes 1000
  2.7 7.2 %collective-permute-start = (bf16[8,88,128]{2,1,0:T(8,128)(2,1)S(1)}, bf16[8,88,128]{2,1,0:T(8,128)(2,1)S(1)}, u32[]{:S(2)}, u32[]{:S(2)}) collective-permute-start(bf16[8,88,128]{2,1,0:T(8,128)(2,1)S(1)} %get-tuple-element.20), channel_id=1, source_target_pairs={{0,4},{4,8},{8,12},{1,5},{5,9},{9,13},{2,6},{6,10},{10,14},{3,7},{... | collective-permute-start | bytes 540680 | tf_op jit(solution)/shard_map/ppermute | solution.py:449
  6.7 7.0 %collective-permute-start.1 = (bf16[8,88,128]{2,1,0:T(8,128)(2,1)S(1)}, bf16[8,88,128]{2,1,0:T(8,128)(2,1)S(1)}, u32[]{:S(2)}, u32[]{:S(2)}) collective-permute-start(bf16[8,88,128]{2,1,0:T(8,128)(2,1)S(1)} %get-tuple-element.21), channel_id=1, source_target_pairs={{4,0},{8,4},{12,8},{5,1},{9,5},{13,9},{6,2},{10,6},{14,10},{7,3},{... | collective-permute-start | bytes 540680 | tf_op jit(solution)/shard_map/ppermute | solution.py:450
  14.3 6.2 %collective-permute-start.2 = (f32[88,128]{1,0:T(8,128)S(1)}, f32[88,128]{1,0:T(8,128)S(1)}, u32[]{:S(2)}, u32[]{:S(2)}) collective-permute-start(f32[88,128]{1,0:T(8,128)S(1)} %get-tuple-element.22), channel_id=1, source_target_pairs={{0,1},{1,2},{2,3},{3,0},{4,5},{5,6},{6,7},{7,4},{8,9},{9,10},{10,1... | collective-permute-start | bytes 135176 | tf_op jit(solution)/shard_map/ppermute | solution.py:455
  19.1 5.0 %collective-permute-start.3 = (f32[88,128]{1,0:T(8,128)S(1)}, f32[88,128]{1,0:T(8,128)S(1)}, u32[]{:S(2)}, u32[]{:S(2)}) collective-permute-start(f32[88,128]{1,0:T(8,128)S(1)} %get-tuple-element.23), channel_id=1, source_target_pairs={{1,0},{2,1},{3,2},{0,3},{5,4},{6,5},{7,6},{4,7},{9,8},{10,9},{11,1... | collective-permute-start | bytes 135176 | tf_op jit(solution)/shard_map/ppermute | solution.py:456
  58.1 14.6 %all-to-all-start.1 = ((bf16[16,72,128]{2,1,0:T(8,128)(2,1)}), bf16[16,72,128]{2,1,0:T(8,128)(2,1)S(1)}, u32[]{:S(2)}, u32[]{:S(2)}) async-start(bf16[16,72,128]{2,1,0:T(8,128)(2,1)} %shard_map.88), calls=%async_computation.1 | async-start | bytes 589824 | tf_op jit(solution)/shard_map/all_to_all | solution.py:420
  77.9 37.5 %copy-start.2 = (bf16[9,192,83]{1,2,0:T(8,128)(2,1)S(1)}, bf16[9,192,83]{1,2,0:T(8,128)(2,1)}, u32[]{:S(2)}) copy-start(bf16[9,192,83]{1,2,0:T(8,128)(2,1)} %param.10) | copy-start | bytes 860548
  109.4 18.2 %all-to-all-start.4 = ((bf16[32,72,128]{2,1,0:T(8,128)(2,1)}), bf16[32,72,128]{2,1,0:T(8,128)(2,1)S(1)}, u32[]{:S(2)}, u32[]{:S(2)}) async-start(bf16[32,72,128]{2,1,0:T(8,128)(2,1)} %shard_map.92), calls=%async_computation.4 | async-start | bytes 1179648 | tf_op jit(solution)/shard_map/all_to_all | solution.py:420

commit v6 on v5

--- a/solution.py
+++ b/solution.py
@@ -16,20 +16,21 @@
 HID = 192
 ROWS = 8
 COLS = 128
-RIM = 4
+NEAR = 1
+FAR = 2
+RIM = NEAR + FAR
 PITCH = COLS + 2 * RIM
 TALL = ROWS + 2 * RIM
-FLAT = TALL * PITCH
-TILES = FLAT // 128
-SPREAD = (2, 15)
-HIDDEN = (3, 14)
-OWN = (4, 13)
+TILES = -(-TALL * PITCH // 128)
+FLAT = 128 * TILES
+SPREAD = (2, 13)
+OWN = (3, 12)
+OWN_LANES = 128 * (OWN[1] - OWN[0])
 MEMBERS = 16
 GROUPS = 32
 RING = 8
-CHUNK = 72
+CHUNK = 64
 PIECE = 72
-HALF = RIM // 2
 f32 = jnp.float32
 bf16 = jnp.bfloat16
 GELU_A = math.sqrt(2.0 / math.pi)
@@ -116,39 +117,42 @@
         latent = parts[0] + parts[1]
         own_ref[r] = latent
         own_ref[ROWS + r] = goal
-        sent, place = (up_ref, r) if r < RIM else (down_ref, ROWS - 1 - r)
-        if place < HALF:
-            near = r if r < RIM else r - (ROWS - HALF)
-            sent[near] = parts[0].astype(bf16)
-            sent[HALF + near] = parts[1].astype(bf16)
-            sent[3 * HALF + near] = goal.astype(bf16)
+        if RIM <= r < ROWS - RIM:
+            continue
+        sent, first_row = (up_ref, 0) if r < RIM else (down_ref, ROWS - RIM)
+        if r < NEAR or r >= ROWS - NEAR:
+            index = r - first_row if r < RIM else r - (ROWS - NEAR)
+            sent[index] = parts[0].astype(bf16)
+            sent[NEAR + index] = parts[1].astype(bf16)
+            sent[2 * NEAR + FAR + index] = goal.astype(bf16)
         else:
             centered, scale = centred(latent)
-            outer = r - HALF if r < RIM else r - RIM
-            sent[2 * HALF + outer] = (centered * scale * gain).astype(bf16)
+            index = r - NEAR if r < RIM else r - first_row
+            sent[2 * NEAR + index] = (centered * scale * gain).astype(bf16)
 
 
 def latent_row(own_ref, top_ref, bottom_ref, row):
     def near(rim_ref, r):
-        return rim_ref[r].astype(f32) + rim_ref[HALF + r].astype(f32)
-
-    if row < HALF:
-        return top_ref[2 * HALF + row].astype(f32)
+        return rim_ref[r].astype(f32) + rim_ref[NEAR + r].astype(f32)
+
+    if row < FAR:
+        return top_ref[2 * NEAR + row].astype(f32)
     if row < RIM:
-        return near(top_ref, row - HALF)
+        return near(top_ref, row - FAR)
     if row < RIM + ROWS:
         return own_ref[row - RIM]
-    if row < RIM + ROWS + HALF:
+    if row < RIM + ROWS + NEAR:
         return near(bottom_ref, row - RIM - ROWS)
-    return bottom_ref[2 * HALF + row - RIM - ROWS - HALF].astype(f32)
+    return bottom_ref[2 * NEAR + row - RIM - ROWS - NEAR].astype(f32)
 
 
 def truth_row(own_ref, top_ref, bottom_ref, row):
-    if row < HALF:
-        return top_ref[3 * HALF + row].astype(f32)
-    if row < HALF + ROWS:
-        return own_ref[ROWS + row - HALF]
-    return bottom_ref[3 * HALF + row - HALF - ROWS].astype(f32)
+    base = 2 * NEAR + FAR
+    if row < NEAR:
+        return top_ref[base + row].astype(f32)
+    if row < NEAR + ROWS:
+        return own_ref[ROWS + row - NEAR]
+    return bottom_ref[base + row - NEAR - ROWS].astype(f32)
 
 
 def columns_kernel(own_ref, top_ref, bottom_ref, left_ref, right_ref):
@@ -157,7 +161,7 @@
     right = jnp.zeros((CP, 128), f32)
     plan = [(latent_row, row, RIM * row, RIM) for row in range(TALL)]
     plan += [
-        (truth_row, row, RIM * TALL + RIM // 2 * row, RIM // 2) for row in range(ROWS + RIM)
+        (truth_row, row, RIM * TALL + NEAR * row, NEAR) for row in range(ROWS + 2 * NEAR)
     ]
     for source, row, start, width in plan:
         values = source(own_ref, top_ref, bottom_ref, row)
@@ -168,11 +172,11 @@
     right_ref[...] = right
 
 
-def flat_tiles(pieces, first, last):
-    lane = lanes_of(CP)
+def flat_tiles(pieces, first, last, height=CP, base=None):
+    lane = lanes_of(height)
     rolled = {}
     for index in range(first, last):
-        result = jnp.zeros((CP, 128), f32)
+        result = jnp.zeros((height, 128), f32) if base is None else base(index)
         for number, (values, lane_from, flat_to, width) in enumerate(pieces):
             low, high = max(flat_to - 128 * index, 0), min(flat_to + width - 128 * index, 128)
             if low >= high:
@@ -194,15 +198,14 @@
         pieces.append((functools.partial(latent_row, own_ref, top_ref, bottom_ref, row), 0, PITCH * row + RIM, COLS))
         pieces.append((lambda: left_ref[...], RIM * row, PITCH * row, RIM))
         pieces.append((lambda: right_ref[...], RIM * row, PITCH * row + RIM + COLS, RIM))
-    half = HALF
-    for row in range(ROWS + RIM):
-        flat, lane = PITCH * (row + half) + RIM, RIM * TALL + half * row
+    for row in range(ROWS + 2 * NEAR):
+        flat, lane = PITCH * (row + FAR) + RIM, RIM * TALL + NEAR * row
         truths.append((functools.partial(truth_row, own_ref, top_ref, bottom_ref, row), 0, flat, COLS))
-        truths.append((lambda: left_ref[...], lane, flat - half, half))
-        truths.append((lambda: right_ref[...], lane, flat + COLS, half))
+        truths.append((lambda: left_ref[...], lane, flat - NEAR, NEAR))
+        truths.append((lambda: right_ref[...], lane, flat + COLS, NEAR))
     gain = gain_column(gain_ref)
     lane = lanes_of(CP)
-    inner_low, inner_high = PITCH * HALF, PITCH * (TALL - HALF)
+    inner_low, inner_high = PITCH * FAR, PITCH * (TALL - FAR)
     normed[CP:CI, :] = jnp.zeros((CI - CP, FLAT), f32)
     for index, values in flat_tiles(pieces, 0, TILES):
         latent[:, tile(index)] = values
@@ -219,7 +222,8 @@
     moves = started((latent.at[:, own], latent_ref), semaphores=semaphores)
     for index, values in flat_tiles(truths, *SPREAD):
         truth[pl.ds(CP * (index - SPREAD[0]), CP), :] = values
-    truth[pl.ds(CP * (SPREAD[1] - SPREAD[0]), 8), :] = jnp.zeros((8, 128), f32)
+    filled = CP * (SPREAD[1] - SPREAD[0])
+    truth[filled:, :] = jnp.zeros((MEMBERS * CHUNK - filled, 128), f32)
     truth_ref[...] = truth[pl.ds(pl.multiple_of(member_ref[0] * CHUNK, 8), CHUNK), :]
 
     for group in range(CI // 16):
@@ -230,13 +234,15 @@
             window[CI * offset + 16 * group : CI * offset + 16 * group + 16, :] = moved.astype(bf16)
     moves += started((window.at[:, own], window_ref), semaphores=semaphores.at[1:2])
 
-    for number, (first, last) in enumerate(((0, 3), (3, 7), (7, 11), (11, 14), (14, 17))):
+    for number, first in enumerate(range(0, TILES, 4)):
+        last = min(first + 4, TILES)
         span = slice(128 * first, 128 * last)
         pre = jnp.dot(w1_ref[...], window[:, span], preferred_element_type=f32)
-        if first >= HIDDEN[0] and last <= HIDDEN[1]:
-            kept = pl.ds(128 * (first - HIDDEN[0]), 128 * (last - first))
-            pre_kept[:, kept] = pre
-            moves += started((pre_kept.at[:, kept], pre_ref.at[:, kept]), semaphores=semaphores.at[number + 2 : number + 3])
+        low, high = max(first, OWN[0]), min(last, OWN[1])
+        if low < high:
+            kept = pl.ds(128 * (low - OWN[0]), 128 * (high - low))
+            pre_kept[:, kept] = pre[:, 128 * (low - first) : 128 * (high - first)]
+            moves += started((pre_kept.at[:, kept], pre_ref.at[:, kept]), semaphores=semaphores.at[number + 3 : number + 4])
         curve = jnp.tanh(GELU_A * (pre + GELU_B * (pre * pre * pre)))
         hidden[:, span] = (0.5 * pre * (1.0 + curve) * valid_ref[:, span]).astype(bf16)
         partial[:, span] = jnp.dot(w2_ref[...], hidden[:, span], preferred_element_type=f32)
@@ -256,7 +262,7 @@
             forecast_ref[start : start + 8, :] = (
                 total[:, 128 * index : 128 * index + 128] + latent[8 * group : 8 * group + 8, tile(index)]
             )
-    forecast_ref[pl.ds(CP * (SPREAD[1] - SPREAD[0]), 8), :] = jnp.zeros((8, 128), f32)
+    forecast_ref[filled:, :] = jnp.zeros((MEMBERS * CHUNK - filled, 128), f32)
     for move in moves:
         move.wait()
 
@@ -284,9 +290,16 @@
     grad_ref[...] = grads[...].astype(bf16)
 
 
+def flat_row(values, row, first):
+    index, off = divmod(PITCH * (row + RIM) + RIM, 128)
+    near = pltpu.roll(values(index - first), 128 - off, 1)
+    far = pltpu.roll(values(index + 1 - first), 128 - off, 1)
+    return jnp.where(lanes_of(near.shape[0]) < 128 - off, near, far)
+
+
 def backward_kernel(
     grad_ref, pre_far, hidden_far, window_far, valid_ref, mine_ref, w2_ref,
-    grad_pre_ref, own_grad_ref, weights_ref,
+    grad_pre_ref, own_grad_ref, weights_ref, up_ref, down_ref, left_ref, right_ref,
     pre_ref, hidden_ref, window_ref, chunks, grad, window, grad_pre, packed, semaphores,
 ):
     moves = started((hidden_far, hidden_ref), (pre_far, pre_ref), (window_far, window_ref), semaphores=semaphores)
@@ -299,37 +312,34 @@
     for index in range(*SPREAD):
         values = chunks[CP * (index - SPREAD[0]) : CP * (index - SPREAD[0]) + CP, :]
         grad[0:CP, tile(index)] = values * valid_ref[:, tile(index)]
-    low, high = 128 * HIDDEN[0], 128 * HIDDEN[1]
+    low, high = 128 * OWN[0], 128 * OWN[1]
     for group in range(CI // 16):
         values = grad[16 * group : 16 * group + 16, :]
         for offset in range(9):
             shift = step_of(offset) % FLAT
             moved = pltpu.roll(values, shift, 1) if shift else values
             window[CI * offset + 16 * group : CI * offset + 16 * group + 16, :] = moved[:, low:high].astype(bf16)
-    own = pl.ds(128 * OWN[0], 128 * (OWN[1] - OWN[0]))
+    own = pl.ds(low, high - low)
     later = started((grad.at[0:CP, own], own_grad_ref), semaphores=semaphores.at[3:4])
-    inner = slice(128 * (OWN[0] - HIDDEN[0]), 128 * (OWN[1] - HIDDEN[0]))
     moves[0].wait()
     across = (((1,), (1,)), ((), ()))
-    grad_out = lax.dot_general(window[:, inner], hidden_ref[...], across, preferred_element_type=f32)
+    grad_out = lax.dot_general(window[...], hidden_ref[...], across, preferred_element_type=f32)
     for k in range(9):
         values = grad_out[CI * k : CI * k + C, :]
         packed[C * (9 + k) : C * (10 + k), :] = values[:, 0:128]
         packed[C * (18 + k) : C * (19 + k), 64:128] = values[:, 128:192]
     moves[1].wait()
-    for first, last in ((0, 4), (4, 8), (8, 11)):
-        span = slice(128 * first, 128 * last)
+    for first in range(0, high - low, 512):
+        span = slice(first, min(first + 512, high - low))
         grad_hidden = jnp.dot(w2_ref[...], window[:, span], preferred_element_type=f32)
         pre = pre_ref[:, span]
         square = pre * pre
         curve = jnp.tanh(GELU_A * (pre + GELU_B * (square * pre)))
         slope = 0.5 * (1.0 + curve) + 0.5 * pre * (1.0 - curve * curve) * (GELU_A * (1.0 + 3.0 * GELU_B * square))
-        live = valid_ref[:, low + 128 * first : low + 128 * last]
-        grad_pre[:, span] = (grad_hidden * slope * live).astype(bf16)
+        grad_pre[:, span] = (grad_hidden * slope * mine_ref[:, span]).astype(bf16)
     later += started((grad_pre, grad_pre_ref), semaphores=semaphores.at[4:5])
-    own_pre = (grad_pre[:, inner].astype(f32) * mine_ref[...]).astype(bf16)
     moves[2].wait()
-    grad_in = lax.dot_general(window_ref[...], own_pre, across, preferred_element_type=f32)
+    grad_in = lax.dot_general(window_ref[...], grad_pre[...], across, preferred_element_type=f32)
     for k in range(9):
         values = grad_in[CI * k : CI * k + C, :]
         packed[C * k : C * (k + 1), :] = values[:, 0:128]
@@ -337,19 +347,57 @@
     packed[27 * C :, :] = jnp.zeros((GROUPS * PIECE - 27 * C, 128), f32)
     for place in range(GROUPS):
         weights_ref[place] = packed[PIECE * place : PIECE * place + PIECE, :].astype(bf16)
+    lane = lanes_of(HID)
+    left, right = jnp.zeros((HID, 128), f32), jnp.zeros((HID, 128), f32)
+    for row in range(ROWS):
+        values = flat_row(lambda index: grad_pre[:, tile(index)].astype(f32), row, OWN[0])
+        if row == 0:
+            up_ref[...] = values.astype(bf16)
+        if row == ROWS - 1:
+            down_ref[...] = values.astype(bf16)
+        left = jnp.where(lane == row + 1, pltpu.roll(values, row + 1, 1), left)
+        right = jnp.where(lane == row + 1, pltpu.roll(values, row + 2, 1), right)
+    left_ref[...] = left.astype(bf16)
+    right_ref[...] = right.astype(bf16)
     for move in later:
         move.wait()
 
 
+def corners_kernel(top_ref, bottom_ref, left_ref, right_ref, to_left_ref, to_right_ref):
+    lane = lanes_of(HID)
+    top, bottom = top_ref[...].astype(f32), bottom_ref[...].astype(f32)
+    for step, columns_ref, sent_ref in ((0, left_ref, to_left_ref), (1, right_ref, to_right_ref)):
+        values = columns_ref[...].astype(f32)
+        values = jnp.where(lane == 0, pltpu.roll(top, step, 1) if step else top, values)
+        values = jnp.where(lane == ROWS + 1, pltpu.roll(bottom, ROWS + 1 + step, 1), values)
+        sent_ref[...] = values.astype(bf16)
+
+
 def states_kernel(
-    grad_pre_far, grad_far, latent_far, gain_ref, w1_ref,
+    grad_pre_far, grad_far, latent_far, gain_ref, w1_ref, top_ref, bottom_ref, left_ref, right_ref,
     states_ref,
-    grad_pre, grad, latent, partial, shifted, result, semaphores,
+    own_pre, grad, latent, grad_pre, partial, shifted, result, semaphores,
 ):
-    moves = started((grad_pre_far, grad_pre), (latent_far, latent), (grad_far, grad), semaphores=semaphores)
-    span = 128 * (HIDDEN[1] - HIDDEN[0])
-    inner = slice(128 * (OWN[0] - HIDDEN[0]), 128 * (OWN[1] - HIDDEN[0]))
+    moves = started((grad_pre_far, own_pre), (latent_far, latent), (grad_far, grad), semaphores=semaphores)
+    span = 128 * (SPREAD[1] - SPREAD[0])
+    inner = slice(128 * (OWN[0] - SPREAD[0]), 128 * (OWN[1] - SPREAD[0]))
     moves[0].wait()
+
+    def base(index):
+        if OWN[0] <= index < OWN[1]:
+            return own_pre[:, tile(index - OWN[0])].astype(f32)
+        return jnp.zeros((HID, 128), f32)
+
+    pieces = [
+        (lambda: top_ref[...].astype(f32), 0, PITCH * (RIM - 1) + RIM, COLS),
+        (lambda: bottom_ref[...].astype(f32), 0, PITCH * (RIM + ROWS) + RIM, COLS),
+    ]
+    for row in range(ROWS + 2):
+        flat = PITCH * (row + RIM - 1) + RIM
+        pieces.append((lambda: left_ref[...].astype(f32), row, flat - 1, 1))
+        pieces.append((lambda: right_ref[...].astype(f32), row, flat + COLS, 1))
+    for index, values in flat_tiles(pieces, *SPREAD, HID, base):
+        grad_pre[:, tile(index - SPREAD[0])] = values.astype(bf16)
     for first in range(0, span, 512):
         some = slice(first, min(first + 512, span))
         partial[:, some] = jnp.dot(w1_ref[...], grad_pre[:, some], preferred_element_type=f32)
@@ -372,15 +420,8 @@
         mean_pull = jnp.sum(pull, axis=0, keepdims=True) * (1.0 / C)
         mean_both = jnp.sum(pull * unit, axis=0, keepdims=True) * (1.0 / C)
         shifted[:, tile(index)] = grad[:, tile(index)] + scale * (pull - mean_pull - unit * mean_both)
-    lane = lanes_of(CP)
     for row in range(ROWS):
-        start = PITCH * (row + RIM) + RIM - 128 * OWN[0]
-        index, off = divmod(start, 128)
-        values = shifted[:, tile(index)]
-        if off:
-            near = pltpu.roll(values, 128 - off, 1)
-            far = pltpu.roll(shifted[:, tile(index + 1)], 128 - off, 1)
-            values = jnp.where(lane < 128 - off, near, far)
+        values = flat_row(lambda index: shifted[:, tile(index)], row, OWN[0])
         result[pl.ds(row, C, stride=ROWS), :] = values[0:C]
     states_ref[...] = result[...].astype(bf16)
 
@@ -436,7 +477,7 @@
     member_axes, plane = ("half", "ring"), ("half", "lat", "lon")
     gain = feature_scale_factor[None]
     block = (C, ROWS, COLS)
-    rim = ((4 * HALF, CP, 128), bf16)
+    rim = ((3 * NEAR + FAR, CP, 128), bf16)
     own, up, down = call(
         rows_kernel,
         6,
@@ -467,15 +508,15 @@
     w1_turned = padded(first_stencil_kernel.transpose(0, 2, 1), 1, CP).reshape(9 * CP, HID)
 
     member = lax.axis_index(member_axes).astype(jnp.int32)[None]
-    own_lanes = 128 * (OWN[1] - OWN[0])
-    hidden_lanes = 128 * (HIDDEN[1] - HIDDEN[0])
+    own_lanes = OWN_LANES
+    spread_lanes = 128 * (SPREAD[1] - SPREAD[0])
     forecast, truth, pre, hidden, window, latent = call(
         forward_kernel,
         26,
         [
             ((MEMBERS * CHUNK, 128), f32),
             ((CHUNK, 128), f32),
-            ((HID, hidden_lanes), (f32,)),
+            ((HID, own_lanes), (f32,)),
             ((HID, own_lanes), (bf16,)),
             ((9 * CI, own_lanes), (bf16,)),
             ((CP, own_lanes), (f32,)),
@@ -487,11 +528,11 @@
             ((HID, FLAT), bf16),
             ((9 * CP, FLAT), f32),
             ((MEMBERS * CHUNK, 128), f32),
-            ((HID, hidden_lanes), f32),
+            ((HID, own_lanes), f32),
             ((HID, own_lanes), bf16),
         ],
         member, own, top, bottom, left, right, gain, valid, mine, w1_stack, w2_stack,
-        smem=1, close=(1, 2, 3, 4, 5), copies=6,
+        smem=1, close=(1, 2, 3, 4, 5), copies=7,
     )
     spread = swap(forecast.reshape(MEMBERS, CHUNK, 128), member_axes)
     (grads,) = call(
@@ -502,41 +543,53 @@
         spread, truth,
     )
     grads = swap(grads, member_axes)
-    grad_pre, own_grad, weights = call(
+    strip = ((HID, 128), bf16)
+    grad_pre, own_grad, weights, up, down, to_left, to_right = call(
         backward_kernel,
         22,
         [
-            ((HID, hidden_lanes), (bf16,)),
+            ((HID, own_lanes), (bf16,)),
             ((CP, own_lanes), (f32,)),
             ((GROUPS, PIECE, 128), bf16),
+            strip, strip, strip, strip,
         ],
         [
-            ((HID, hidden_lanes), f32),
+            ((HID, own_lanes), f32),
             ((HID, own_lanes), bf16),
             ((9 * CI, own_lanes), bf16),
             ((MEMBERS * CHUNK, 128), f32),
             ((CI, FLAT), f32),
-            ((9 * CI, hidden_lanes), bf16),
-            ((HID, hidden_lanes), bf16),
+            ((9 * CI, own_lanes), bf16),
+            ((HID, own_lanes), bf16),
             ((GROUPS * PIECE, 128), f32),
         ],
         grads, pre, hidden, window, valid, mine, w2_turned,
         far=(1, 2, 3), copies=5,
     )
     parts = swap(weights, plane)
+    forward, backward = neighbours("lat", False)
+    top = lax.ppermute(down, "lat", forward)
+    bottom = lax.ppermute(up, "lat", backward)
+    to_left, to_right = call(
+        corners_kernel, 4, [strip, strip], [], top, bottom, to_left, to_right
+    )
+    forward, backward = neighbours("lon", True)
+    left = lax.ppermute(to_right, "lon", forward)
+    right = lax.ppermute(to_left, "lon", backward)
     (states,) = call(
         states_kernel,
-        14,
+        16,
         [((C * ROWS, COLS), bf16)],
         [
-            ((HID, hidden_lanes), bf16),
+            ((HID, own_lanes), bf16),
             ((CP, own_lanes), f32),
             ((CP, own_lanes), f32),
-            ((9 * CP, hidden_lanes), f32),
+            ((HID, spread_lanes), bf16),
+            ((9 * CP, spread_lanes), f32),
             ((CP, own_lanes), f32),
             ((C * ROWS, COLS), f32),
         ],
-        grad_pre, own_grad, latent, gain, w1_turned,
+        grad_pre, own_grad, latent, gain, w1_turned, top, bottom, left, right,
         far=(0, 1, 2), copies=3,
     )
     piece = (PIECE, 128)

time: 130 us -> 135 us (1.038)
  starting transfers between devices: 19.5 us -> 29.1 us
  waiting for transfers between devices: 28.6 us -> 26.2 us
  blocking collectives: 56.9 us -> 55.5 us
    all_to_all x2, waiting for transfers between devices: 19.5 us -> 8.61 us  [swap(): return lax.all_to_all(values, axes, split_axis=0, concat_axis=0, tiled=True)]
    ppermute x1 -> x2, waiting for transfers between devices: 3.53 us -> 7.38 us  [on_device(): right = lax.ppermute(to_left, 'lon', backward)]
    ppermute x1 -> x2, starting transfers between devices: 4.74 us -> 8.52 us  [on_device(): left = lax.ppermute(to_right, 'lon', forward)]
    ppermute x1 -> x2, starting transfers between devices: 3.96 us -> 7.26 us  [on_device(): top = lax.ppermute(down, 'lat', forward)]
    ppermute x1 -> x2, waiting for transfers between devices: 3.8 us -> 5.74 us  [on_device(): bottom = lax.ppermute(up, 'lat', backward)]
    ppermute x1 -> x2, waiting for transfers between devices: 1.78 us -> 3.38 us  [on_device(): top = lax.ppermute(down, 'lat', forward)]
    all_to_all x3, blocking collectives: 56.9 us -> 55.5 us  [swap(): return lax.all_to_all(values, axes, split_axis=0, concat_axis=0, tiled=True)]
    pallas_call x9 -> x10, Pallas kernels: 21.3 us -> 20.8 us  [call(): pl.pallas_call(kernel, out_shape=[(pltpu.HBM if isinstance(given, tuple)...]
  transfers between devices with their start and end apart: 6 -> 10, of which waited for: 5 -> 8; matrix products, arithmetic and copies ran while one was open for 1% -> 1% of each run, Pallas kernels for 3% -> 3%
where the time goes in v6:
time: 135 us; the launch traced here: 134 us
  blocking collectives  55.5 us (41%)
  starting transfers between devices  29.1 us (22%)
  waiting for transfers between devices  26.2 us (19%)
  Pallas kernels  20.8 us (15%)
  local copies, waits for them, and re-layouts  1.73 us (1%)
    all_to_all x3, blocking collectives, swap(): return lax.all_to_all(values, axes, split_axis=0, concat_axis=0, tiled=True)  55.5 us
    pallas_call x10, Pallas kernels, call(): pl.pallas_call(kernel, out_shape=[(pltpu.HBM if isinstance(given, tuple)...  20.8 us
    all_to_all x2, starting transfers between devices, swap(): return lax.all_to_all(values, axes, split_axis=0, concat_axis=0, tiled=True)  10.7 us
    all_to_all x2, waiting for transfers between devices, swap(): return lax.all_to_all(values, axes, split_axis=0, concat_axis=0, tiled=True)  8.61 us
    ppermute x2, starting transfers between devices, on_device(): left = lax.ppermute(to_right, 'lon', forward)  8.52 us
    ppermute x2, waiting for transfers between devices, on_device(): right = lax.ppermute(to_left, 'lon', backward)  7.38 us
    ppermute x2, starting transfers between devices, on_device(): top = lax.ppermute(down, 'lat', forward)  7.26 us
    ppermute x2, waiting for transfers between devices, on_device(): bottom = lax.ppermute(up, 'lat', backward)  5.74 us
  transfers between devices with their start and end apart: 10, of which 8 were waited for; matrix products, arithmetic and copies ran while one was open for 1% of the time, Pallas kernels for 3%

profile of v6, /device:TPU:1, one launch (start us, length us, event | category | flops | bytes accessed | tf_op | source)
XLA Modules:
  0.0 134.3 jit_solution(12839346770116251913)
XLA Ops:
  0.7 2.1 %shard_map.85 = (f32[16,88,128]{2,1,0:T(8,128)S(1)}, bf16[5,88,128]{2,1,0:T(8,128)(2,1)S(1)}, bf16[5,88,128]{2,1,0:T(8,128)(2,1)S(1)}) custom-call(bf16[83,8,128]{2,1,0:T(8,128)(2,1)} %bitcast.25, bf16[83,8,128]{2,1,0:T(8,128)(2,1)} %bitcast.26, bf16[83,8,128]{2,1,0:T(8,128)(2,1)} %target_ref.1, f32[1,83]{1,0:T(1,128)} %bitcast.19), custom_call_target="tpu_custom_call" | custom-call | tf_op jit(solution)/shard_map/pallas_call | solution.py:52
  2.8 4.0 %collective-permute-start = (bf16[5,88,128]{2,1,0:T(8,128)(2,1)S(1)}, bf16[5,88,128]{2,1,0:T(8,128)(2,1)S(1)}, u32[]{:S(2)}, u32[]{:S(2)}) collective-permute-start(bf16[5,88,128]{2,1,0:T(8,128)(2,1)S(1)} %get-tuple-element.26), channel_id=1, source_target_pairs={{0,4},{4,8},{8,12},{1,5},{5,9},{9,13},{2,6},{6,10},{10,14},{3,7},{... | collective-permute-start | bytes 337928 | tf_op jit(solution)/shard_map/ppermute | solution.py:490
  6.7 1.3 collective-permute-start.1
  8.1 0.3 collective-permute-done.top_ref
  8.5 3.8 %collective-permute-done.1.bottom_ref = bf16[5,88,128]{2,1,0:T(8,128)(2,1)S(1)} collective-permute-done((bf16[5,88,128]{2,1,0:T(8,128)(2,1)S(1)}, bf16[5,88,128]{2,1,0:T(8,128)(2,1)S(1)}, u32[]{:S(2)}, u32[]{:S(2)}) %collective-permute-start.1) | collective-permute-done | bytes 112672 | tf_op jit(solution)/shard_map/ppermute | solution.py:491
  12.2 0.6 shard_map.86
  12.8 5.0 %collective-permute-start.2 = (f32[88,128]{1,0:T(8,128)S(1)}, f32[88,128]{1,0:T(8,128)S(1)}, u32[]{:S(2)}, u32[]{:S(2)}) collective-permute-start(f32[88,128]{1,0:T(8,128)S(1)} %get-tuple-element.28), channel_id=1, source_target_pairs={{0,1},{1,2},{2,3},{3,0},{4,5},{5,6},{6,7},{7,4},{8,9},{9,10},{10,1... | collective-permute-start | bytes 135176 | tf_op jit(solution)/shard_map/ppermute | solution.py:496
  17.8 1.1 pad.15
  18.9 0.2 copy.11.w1_ref
  19.2 3.5 %collective-permute-done.3.right_ref = f32[88,128]{1,0:T(8,128)S(1)} collective-permute-done((f32[88,128]{1,0:T(8,128)S(1)}, f32[88,128]{1,0:T(8,128)S(1)}, u32[]{:S(2)}, u32[]{:S(2)}) %collective-permute-start.3) | collective-permute-done | bytes 45088 | tf_op jit(solution)/shard_map/ppermute | solution.py:497
  22.8 5.2 %shard_map.87 = (f32[1024,128]{1,0:T(8,128)S(1)}, f32[64,128]{1,0:T(8,128)S(1)}, f32[192,1152]{1,0:T(8,128)}, bf16[192,1152]{1,0:T(8,128)(2,1)}, bf16[864,1152]{1,0:T(8,128)(2,1)}, /*index=5*/f32[88,1152]{1,0:T(8,128)}) custom-call(s32[1]{0:T(128)} %bitcast.member_ref, f32[16,88,128]{2,1,0:T(8,128)S(1)} %get-tuple-element.25.own_ref, ...), custom_call_target="tpu_custom_call" | custom-call | tf_op jit(solution)/shard_map/pallas_call | solution.py:52
  27.9 22.8 %all_to_all.25.forecast_ref = f32[16,64,128]{2,1,0:T(8,128)S(1)} all-to-all(f32[16,64,128]{2,1,0:T(8,128)S(1)} %bitcast.18), channel_id=1, replica_groups=mesh['half'=2,'ring'=8,'lat'=4,'lon'=4] {'half','ring'}, dimensions={0} | all-to-all | bytes 1048576 | tf_op jit(solution)/shard_map/all_to_all | solution.py:461
  50.7 1.8 %shard_map.88 = bf16[16,64,128]{2,1,0:T(8,128)(2,1)} custom-call(f32[16,64,128]{2,1,0:T(8,128)S(1)} %all_to_all.25.forecast_ref, f32[64,128]{1,0:T(8,128)S(1)} %get-tuple-element.31.truth_ref), custom_call_target="tpu_custom_call" | custom-call | tf_op jit(solution)/shard_map/pallas_call | solution.py:52
  52.5 4.6 %all-to-all-start.1 = ((bf16[16,64,128]{2,1,0:T(8,128)(2,1)}), bf16[16,64,128]{2,1,0:T(8,128)(2,1)S(1)}, u32[]{:S(2)}, u32[]{:S(2)}) async-start(bf16[16,64,128]{2,1,0:T(8,128)(2,1)} %shard_map.88), calls=%async_computation.1 | async-start | bytes 524288 | tf_op jit(solution)/shard_map/all_to_all | solution.py:461
  57.1 0.2 copy.12.w2_ref
  57.3 8.6 %all-to-all-done.1.grad_ref = bf16[16,64,128]{2,1,0:T(8,128)(2,1)S(1)} async-done(((bf16[16,64,128]{2,1,0:T(8,128)(2,1)}), bf16[16,64,128]{2,1,0:T(8,128)(2,1)S(1)}, u32[]{:S(2)}, u32[]{:S(2)}) %all-to-all-start.1) | async-done | bytes 262176 | tf_op jit(solution)/shard_map/all_to_all | solution.py:461
  65.9 5.2 %shard_map.89 = (bf16[192,1152]{1,0:T(8,128)(2,1)}, f32[88,1152]{1,0:T(8,128)}, bf16[32,72,128]{2,1,0:T(8,128)(2,1)S(1)}, bf16[192,128]{1,0:T(8,128)(2,1)S(1)}, ...) custom-call(bf16[16,64,128]{2,1,0:T(8,128)(2,1)S(1)} %all-to-all-done.1.grad_ref, ...), custom_call_target="tpu_custom_call" | custom-call | tf_op jit(solution)/shard_map/pallas_call | solution.py:52
  71.1 21.1 %all_to_all.26.parts_ref = bf16[32,72,128]{2,1,0:T(8,128)(2,1)S(1)} all-to-all(bf16[32,72,128]{2,1,0:T(8,128)(2,1)S(1)} %get-tuple-element.44), channel_id=1, replica_groups=mesh['half'=2,'ring'=8,'lat'=4,'lon'=4] {'half','lat','lon'}, dimensions={0} | all-to-all | bytes 1179648 | tf_op jit(solution)/shard_map/all_to_all | solution.py:461
  92.2 0.1 shard_map.92
  92.3 11.7 %all_to_all.27.parts_ref = bf16[8,72,128]{2,1,0:T(8,128)(2,1)S(1)} all-to-all(bf16[8,72,128]{2,1,0:T(8,128)(2,1)S(1)} %shard_map.92), channel_id=1, replica_groups=mesh['half'=2,'ring'=8,'lat'=4,'lon'=4] {'ring'}, dimensions={0} | all-to-all | bytes 294912 | tf_op jit(solution)/shard_map/all_to_all | solution.py:461
  104.0 0.9 shard_map.93
  104.8 6.1 %all-to-all-start.4 = ((bf16[32,72,128]{2,1,0:T(8,128)(2,1)}), bf16[32,72,128]{2,1,0:T(8,128)(2,1)S(1)}, u32[]{:S(2)}, u32[]{:S(2)}) async-start(bf16[32,72,128]{2,1,0:T(8,128)(2,1)} %shard_map.93), calls=%async_computation.4 | async-start | bytes 1179648 | tf_op jit(solution)/shard_map/all_to_all | solution.py:461
  111.0 3.3 %collective-permute-start.4 = (bf16[192,128]{1,0:T(8,128)(2,1)S(1)}, bf16[192,128]{1,0:T(8,128)(2,1)S(1)}, u32[]{:S(2)}, u32[]{:S(2)}) collective-permute-start(bf16[192,128]{1,0:T(8,128)(2,1)S(1)} %get-tuple-element.38), channel_id=1, source_target_pairs={{0,4},{4,8},{8,12},{1,5},{5,9},{9,13},{2,6},{6,10},{10,14},{3,7},{... | collective-permute-start | bytes 147464 | tf_op jit(solution)/shard_map/ppermute | solution.py:571
  114.3 1.3 collective-permute-start.5
  115.6 3.0 %collective-permute-done.4.top_ref = bf16[192,128]{1,0:T(8,128)(2,1)S(1)} collective-permute-done((bf16[192,128]{1,0:T(8,128)(2,1)S(1)}, bf16[192,128]{1,0:T(8,128)(2,1)S(1)}, u32[]{:S(2)}, u32[]{:S(2)}) %collective-permute-start.4) | collective-permute-done | bytes 49184 | tf_op jit(solution)/shard_map/ppermute | solution.py:571
  118.6 2.0 %collective-permute-done.5.bottom_ref = bf16[192,128]{1,0:T(8,128)(2,1)S(1)} collective-permute-done((bf16[192,128]{1,0:T(8,128)(2,1)S(1)}, bf16[192,128]{1,0:T(8,128)(2,1)S(1)}, u32[]{:S(2)}, u32[]{:S(2)}) %collective-permute-start.5) | collective-permute-done | bytes 49184 | tf_op jit(solution)/shard_map/ppermute | solution.py:572
  120.6 0.1 shard_map.90
  120.7 3.5 %collective-permute-start.6 = (bf16[192,128]{1,0:T(8,128)(2,1)S(1)}, bf16[192,128]{1,0:T(8,128)(2,1)S(1)}, u32[]{:S(2)}, u32[]{:S(2)}) collective-permute-start(bf16[192,128]{1,0:T(8,128)(2,1)S(1)} %get-tuple-element.42), channel_id=1, source_target_pairs={{0,1},{1,2},{2,3},{3,0},{4,5},{5,6},{6,7},{7,4},{8,9},{9,10},{10,1... | collective-permute-start | bytes 147464 | tf_op jit(solution)/shard_map/ppermute | solution.py:577
  124.3 1.1 collective-permute-done.6.left_ref
  125.4 3.8 %collective-permute-done.7.right_ref = bf16[192,128]{1,0:T(8,128)(2,1)S(1)} collective-permute-done((bf16[192,128]{1,0:T(8,128)(2,1)S(1)}, bf16[192,128]{1,0:T(8,128)(2,1)S(1)}, u32[]{:S(2)}, u32[]{:S(2)}) %collective-permute-start.7) | collective-permute-done | bytes 49184 | tf_op jit(solution)/shard_map/ppermute | solution.py:578
  129.3 3.6 %shard_map.91 = bf16[664,128]{1,0:T(8,128)(2,1)} custom-call(bf16[192,1152]{1,0:T(8,128)(2,1)} %get-tuple-element.35.grad_pre_far, f32[88,1152]{1,0:T(8,128)} %get-tuple-element.36.grad_far, f32[88,1152]{1,0:T(8,128)} %get-tuple-element.37.latent_far, f32[1,83]{1,0:T(1,128)S(1)} %bitcast.21, bf16[792,192]{1,0:T(8,128)(2,1)S(1)} %bitcast.17, ...), custom_call_target="tpu_custom_call" | custom-call | tf_op jit(solution)/shard_map/pallas_call | solution.py:52
  132.9 1.4 %shard_map.94 = (f32[9,83,192]{2,1,0:T(8,128)}, f32[9,83,192]{2,1,0:T(8,128)}) custom-call(bf16[32,72,128]{2,1,0:T(8,128)(2,1)S(1)} %all-to-all-done.4.parts_ref), custom_call_target="tpu_custom_call" | custom-call | tf_op jit(solution)/shard_map/pallas_call | solution.py:52
  (17 shorter events, 0.4 us)
Async XLA Ops:
  0.6 18.5 %copy-start.1 = (bf16[9,83,192]{2,1,0:T(8,128)(2,1)S(1)}, bf16[9,83,192]{2,1,0:T(8,128)(2,1)}, u32[]{:S(2)}) copy-start(bf16[9,83,192]{2,1,0:T(8,128)(2,1)} %param.11) | copy-start | bytes 860548
  0.6 22.1 %copy-start = (f32[83]{0:T(128)S(1)}, f32[83]{0:T(128)}, u32[]{:S(2)}) copy-start(f32[83]{0:T(128)} %param.9) | copy-start | bytes 1000
  2.8 5.7 %collective-permute-start = (bf16[5,88,128]{2,1,0:T(8,128)(2,1)S(1)}, bf16[5,88,128]{2,1,0:T(8,128)(2,1)S(1)}, u32[]{:S(2)}, u32[]{:S(2)}) collective-permute-start(bf16[5,88,128]{2,1,0:T(8,128)(2,1)S(1)} %get-tuple-element.26), channel_id=1, source_target_pairs={{0,4},{4,8},{8,12},{1,5},{5,9},{9,13},{2,6},{6,10},{10,14},{3,7},{... | collective-permute-start | bytes 337928 | tf_op jit(solution)/shard_map/ppermute | solution.py:490
  6.7 5.5 %collective-permute-start.1 = (bf16[5,88,128]{2,1,0:T(8,128)(2,1)S(1)}, bf16[5,88,128]{2,1,0:T(8,128)(2,1)S(1)}, u32[]{:S(2)}, u32[]{:S(2)}) collective-permute-start(bf16[5,88,128]{2,1,0:T(8,128)(2,1)S(1)} %get-tuple-element.27), channel_id=1, source_target_pairs={{4,0},{8,4},{12,8},{5,1},{9,5},{13,9},{6,2},{10,6},{14,10},{7,3},{... | collective-permute-start | bytes 337928 | tf_op jit(solution)/shard_map/ppermute | solution.py:491
  12.8 6.4 %collective-permute-start.2 = (f32[88,128]{1,0:T(8,128)S(1)}, f32[88,128]{1,0:T(8,128)S(1)}, u32[]{:S(2)}, u32[]{:S(2)}) collective-permute-start(f32[88,128]{1,0:T(8,128)S(1)} %get-tuple-element.28), channel_id=1, source_target_pairs={{0,1},{1,2},{2,3},{3,0},{4,5},{5,6},{6,7},{7,4},{8,9},{9,10},{10,1... | collective-permute-start | bytes 135176 | tf_op jit(solution)/shard_map/ppermute | solution.py:496
  17.8 5.0 %collective-permute-start.3 = (f32[88,128]{1,0:T(8,128)S(1)}, f32[88,128]{1,0:T(8,128)S(1)}, u32[]{:S(2)}, u32[]{:S(2)}) collective-permute-start(f32[88,128]{1,0:T(8,128)S(1)} %get-tuple-element.29), channel_id=1, source_target_pairs={{1,0},{2,1},{3,2},{0,3},{5,4},{6,5},{7,6},{4,7},{9,8},{10,9},{11,1... | collective-permute-start | bytes 135176 | tf_op jit(solution)/shard_map/ppermute | solution.py:497
  52.5 13.5 %all-to-all-start.1 = ((bf16[16,64,128]{2,1,0:T(8,128)(2,1)}), bf16[16,64,128]{2,1,0:T(8,128)(2,1)S(1)}, u32[]{:S(2)}, u32[]{:S(2)}) async-start(bf16[16,64,128]{2,1,0:T(8,128)(2,1)} %shard_map.88), calls=%async_computation.1 | async-start | bytes 524288 | tf_op jit(solution)/shard_map/all_to_all | solution.py:461
  71.1 53.2 %copy-start.2 = (bf16[9,192,83]{1,2,0:T(8,128)(2,1)S(1)}, bf16[9,192,83]{1,2,0:T(8,128)(2,1)}, u32[]{:S(2)}) copy-start(bf16[9,192,83]{1,2,0:T(8,128)(2,1)} %param.10) | copy-start | bytes 860548
  104.8 28.1 %all-to-all-start.4 = ((bf16[32,72,128]{2,1,0:T(8,128)(2,1)}), bf16[32,72,128]{2,1,0:T(8,128)(2,1)S(1)}, u32[]{:S(2)}, u32[]{:S(2)}) async-start(bf16[32,72,128]{2,1,0:T(8,128)(2,1)} %shard_map.93), calls=%async_computation.4 | async-start | bytes 1179648 | tf_op jit(solution)/shard_map/all_to_all | solution.py:461
  111.0 7.7 %collective-permute-start.4 = (bf16[192,128]{1,0:T(8,128)(2,1)S(1)}, bf16[192,128]{1,0:T(8,128)(2,1)S(1)}, u32[]{:S(2)}, u32[]{:S(2)}) collective-permute-start(bf16[192,128]{1,0:T(8,128)(2,1)S(1)} %get-tuple-element.38), channel_id=1, source_target_pairs={{0,4},{4,8},{8,12},{1,5},{5,9},{9,13},{2,6},{6,10},{10,14},{3,7},{... | collective-permute-start | bytes 147464 | tf_op jit(solution)/shard_map/ppermute | solution.py:571
  114.3 6.3 %collective-permute-start.5 = (bf16[192,128]{1,0:T(8,128)(2,1)S(1)}, bf16[192,128]{1,0:T(8,128)(2,1)S(1)}, u32[]{:S(2)}, u32[]{:S(2)}) collective-permute-start(bf16[192,128]{1,0:T(8,128)(2,1)S(1)} %get-tuple-element.39), channel_id=1, source_target_pairs={{4,0},{8,4},{12,8},{5,1},{9,5},{13,9},{6,2},{10,6},{14,10},{7,3},{... | collective-permute-start | bytes 147464 | tf_op jit(solution)/shard_map/ppermute | solution.py:572
  120.7 4.7 %collective-permute-start.6 = (bf16[192,128]{1,0:T(8,128)(2,1)S(1)}, bf16[192,128]{1,0:T(8,128)(2,1)S(1)}, u32[]{:S(2)}, u32[]{:S(2)}) collective-permute-start(bf16[192,128]{1,0:T(8,128)(2,1)S(1)} %get-tuple-element.42), channel_id=1, source_target_pairs={{0,1},{1,2},{2,3},{3,0},{4,5},{5,6},{6,7},{7,4},{8,9},{9,10},{10,1... | collective-permute-start | bytes 147464 | tf_op jit(solution)/shard_map/ppermute | solution.py:577
  124.3 5.0 %collective-permute-start.7 = (bf16[192,128]{1,0:T(8,128)(2,1)S(1)}, bf16[192,128]{1,0:T(8,128)(2,1)S(1)}, u32[]{:S(2)}, u32[]{:S(2)}) collective-permute-start(bf16[192,128]{1,0:T(8,128)(2,1)S(1)} %get-tuple-element.43), channel_id=1, source_target_pairs={{1,0},{2,1},{3,2},{0,3},{5,4},{6,5},{7,6},{4,7},{9,8},{10,9},{11,1... | collective-permute-start | bytes 147464 | tf_op jit(solution)/shard_map/ppermute | solution.py:578

commit v7 on v6

--- a/solution.py
+++ b/solution.py
@@ -568,14 +568,19 @@
     )
     parts = swap(weights, plane)
     forward, backward = neighbours("lat", False)
-    top = lax.ppermute(down, "lat", forward)
-    bottom = lax.ppermute(up, "lat", backward)
+    parts, top, bottom = lax.optimization_barrier(
+        (parts, lax.ppermute(down, "lat", forward), lax.ppermute(up, "lat", backward))
+    )
     to_left, to_right = call(
         corners_kernel, 4, [strip, strip], [], top, bottom, to_left, to_right
     )
     forward, backward = neighbours("lon", True)
     left = lax.ppermute(to_right, "lon", forward)
     right = lax.ppermute(to_left, "lon", backward)
+    piece = (PIECE, 128)
+    (copies,) = call(total_kernel, 6, [((RING,) + piece, bf16)], [], parts)
+    parts, left, right = lax.optimization_barrier((swap(copies, "ring"), left, right))
+    (copies,) = call(total_kernel, 6, [((GROUPS,) + piece, bf16)], [], parts)
     (states,) = call(
         states_kernel,
         16,
@@ -592,9 +597,6 @@
         grad_pre, own_grad, latent, gain, w1_turned, top, bottom, left, right,
         far=(0, 1, 2), copies=3,
     )
-    piece = (PIECE, 128)
-    (copies,) = call(total_kernel, 6, [((RING,) + piece, bf16)], [], parts)
-    (copies,) = call(total_kernel, 6, [((GROUPS,) + piece, bf16)], [], swap(copies, "ring"))
     grad_in, grad_out = call(
         weights_kernel,
         8,

time: 135 us -> 127 us (0.941)
  blocking collectives: 55.5 us -> 22.8 us
  starting transfers between devices: 29.1 us -> 41 us
  waiting for transfers between devices: 26.2 us -> 38 us
  Pallas kernels: 20.8 us -> 22.3 us
    all_to_all x3 -> x1, blocking collectives: 55.5 us -> 22.8 us  [swap(): return lax.all_to_all(values, axes, split_axis=0, concat_axis=0, tiled=True)]
    all_to_all x2 -> x4, starting transfers between devices: 10.7 us -> 24 us  [swap(): return lax.all_to_all(values, axes, split_axis=0, concat_axis=0, tiled=True)]
    all_to_all x2 -> x4, waiting for transfers between devices: 8.61 us -> 20 us  [swap(): return lax.all_to_all(values, axes, split_axis=0, concat_axis=0, tiled=True)]
    ppermute x0 -> x2, waiting for transfers between devices: none -> 5.02 us  [the longest x1 3.08 us: on_device(): lax.ppermute(down, 'lat', forward)]
    ppermute x0 -> x2, starting transfers between devices: none -> 4.58 us  [the longest x1 3.29 us: on_device(): lax.ppermute(down, 'lat', forward)]
    ppermute x2 -> x1, starting transfers between devices: 7.26 us -> 3.95 us  [on_device(): top = lax.ppermute(down, 'lat', forward)]
    ppermute x2 -> x1, waiting for transfers between devices: 3.38 us -> 0.34 us  [on_device(): top = lax.ppermute(down, 'lat', forward)]
    ppermute x2 -> x1, waiting for transfers between devices: 5.74 us -> 3.76 us  [on_device(): bottom = lax.ppermute(up, 'lat', backward)]
  transfers between devices with their start and end apart: 10 -> 12, of which waited for: 8 -> 11; matrix products, arithmetic and copies ran while one was open for 1% -> 1% of each run, Pallas kernels for 3% -> 3%
where the time goes in v7:
time: 127 us
  starting transfers between devices  41 us (32%)
  waiting for transfers between devices  38 us (30%)
  blocking collectives  22.8 us (18%)
  Pallas kernels  22.3 us (18%)
  local copies, waits for them, and re-layouts  1.74 us (1%)
    all_to_all x4, starting transfers between devices, swap(): return lax.all_to_all(values, axes, split_axis=0, concat_axis=0, tiled=True)  24 us
    all_to_all x1, blocking collectives, swap(): return lax.all_to_all(values, axes, split_axis=0, concat_axis=0, tiled=True)  22.8 us
    pallas_call x10, Pallas kernels, call(): pl.pallas_call(kernel, out_shape=[(pltpu.HBM if isinstance(given, tuple)...  22.3 us
    all_to_all x4, waiting for transfers between devices, swap(): return lax.all_to_all(values, axes, split_axis=0, concat_axis=0, tiled=True)  20 us
    ppermute x2, waiting for transfers between devices, on_device(): right = lax.ppermute(to_left, 'lon', backward)  7.67 us
    ppermute x2, starting transfers between devices, on_device(): left = lax.ppermute(to_right, 'lon', forward)  7.2 us
    ppermute x1, starting transfers between devices, on_device(): top = lax.ppermute(down, 'lat', forward)  3.95 us
    ppermute x1, waiting for transfers between devices, on_device(): bottom = lax.ppermute(up, 'lat', backward)  3.76 us
  transfers between devices with their start and end apart: 12, of which 11 were waited for; matrix products, arithmetic and copies ran while one was open for 1% of the time, Pallas kernels for 3%

profile of v7, /device:TPU:1, one launch (start us, length us, event | category | flops | bytes accessed | tf_op | source)
XLA Modules:
  0.0 126.7 jit_solution(17583961759767380428)
XLA Ops:
  0.7 2.1 %shard_map.85 = (f32[16,88,128]{2,1,0:T(8,128)S(1)}, bf16[5,88,128]{2,1,0:T(8,128)(2,1)S(1)}, bf16[5,88,128]{2,1,0:T(8,128)(2,1)S(1)}) custom-call(bf16[83,8,128]{2,1,0:T(8,128)(2,1)} %bitcast.25, bf16[83,8,128]{2,1,0:T(8,128)(2,1)} %bitcast.26, bf16[83,8,128]{2,1,0:T(8,128)(2,1)} %target_ref.1, f32[1,83]{1,0:T(1,128)} %bitcast.19), custom_call_target="tpu_custom_call" | custom-call | tf_op jit(solution)/shard_map/pallas_call | solution.py:52
  2.8 4.0 %collective-permute-start = (bf16[5,88,128]{2,1,0:T(8,128)(2,1)S(1)}, bf16[5,88,128]{2,1,0:T(8,128)(2,1)S(1)}, u32[]{:S(2)}, u32[]{:S(2)}) collective-permute-start(bf16[5,88,128]{2,1,0:T(8,128)(2,1)S(1)} %get-tuple-element.32), channel_id=1, source_target_pairs={{0,4},{4,8},{8,12},{1,5},{5,9},{9,13},{2,6},{6,10},{10,14},{3,7},{... | collective-permute-start | bytes 337928 | tf_op jit(solution)/shard_map/ppermute | solution.py:490
  6.7 1.3 %collective-permute-start.1 = (bf16[5,88,128]{2,1,0:T(8,128)(2,1)S(1)}, bf16[5,88,128]{2,1,0:T(8,128)(2,1)S(1)}, u32[]{:S(2)}, u32[]{:S(2)}) collective-permute-start(bf16[5,88,128]{2,1,0:T(8,128)(2,1)S(1)} %get-tuple-element.33), channel_id=1, source_target_pairs={{4,0},{8,4},{12,8},{5,1},{9,5},{13,9},{6,2},{10,6},{14,10},{7,3},{... | collective-permute-start | bytes 337928 | tf_op jit(solution)/shard_map/ppermute | solution.py:491
  8.1 0.3 collective-permute-done.top_ref
  8.5 3.8 %collective-permute-done.1.bottom_ref = bf16[5,88,128]{2,1,0:T(8,128)(2,1)S(1)} collective-permute-done((bf16[5,88,128]{2,1,0:T(8,128)(2,1)S(1)}, bf16[5,88,128]{2,1,0:T(8,128)(2,1)S(1)}, u32[]{:S(2)}, u32[]{:S(2)}) %collective-permute-start.1) | collective-permute-done | bytes 112672 | tf_op jit(solution)/shard_map/ppermute | solution.py:491
  12.2 0.6 shard_map.86
  12.8 5.0 %collective-permute-start.2 = (f32[88,128]{1,0:T(8,128)S(1)}, f32[88,128]{1,0:T(8,128)S(1)}, u32[]{:S(2)}, u32[]{:S(2)}) collective-permute-start(f32[88,128]{1,0:T(8,128)S(1)} %get-tuple-element.34), channel_id=1, source_target_pairs={{0,1},{1,2},{2,3},{3,0},{4,5},{5,6},{6,7},{7,4},{8,9},{9,10},{10,1... | collective-permute-start | bytes 135176 | tf_op jit(solution)/shard_map/ppermute | solution.py:496
  17.8 1.1 pad.15
  19.2 3.5 %collective-permute-done.3.right_ref = f32[88,128]{1,0:T(8,128)S(1)} collective-permute-done((f32[88,128]{1,0:T(8,128)S(1)}, f32[88,128]{1,0:T(8,128)S(1)}, u32[]{:S(2)}, u32[]{:S(2)}) %collective-permute-start.3) | collective-permute-done | bytes 45088 | tf_op jit(solution)/shard_map/ppermute | solution.py:497
  22.8 5.2 %shard_map.87 = (f32[1024,128]{1,0:T(8,128)S(1)}, f32[64,128]{1,0:T(8,128)S(1)}, f32[192,1152]{1,0:T(8,128)}, bf16[192,1152]{1,0:T(8,128)(2,1)}, bf16[864,1152]{1,0:T(8,128)(2,1)}, /*index=5*/f32[88,1152]{1,0:T(8,128)}) custom-call(s32[1]{0:T(128)} %bitcast.member_ref, f32[16,88,128]{2,1,0:T(8,128)S(1)} %get-tuple-element.31.own_ref, ...), custom_call_target="tpu_custom_call" | custom-call | tf_op jit(solution)/shard_map/pallas_call | solution.py:52
  27.9 22.8 %all_to_all.25.forecast_ref = f32[16,64,128]{2,1,0:T(8,128)S(1)} all-to-all(f32[16,64,128]{2,1,0:T(8,128)S(1)} %bitcast.18), channel_id=1, replica_groups=mesh['half'=2,'ring'=8,'lat'=4,'lon'=4] {'half','ring'}, dimensions={0} | all-to-all | bytes 1048576 | tf_op jit(solution)/shard_map/all_to_all | solution.py:461
  50.7 1.8 %shard_map.88 = bf16[16,64,128]{2,1,0:T(8,128)(2,1)} custom-call(f32[16,64,128]{2,1,0:T(8,128)S(1)} %all_to_all.25.forecast_ref, f32[64,128]{1,0:T(8,128)S(1)} %get-tuple-element.37.truth_ref), custom_call_target="tpu_custom_call" | custom-call | tf_op jit(solution)/shard_map/pallas_call | solution.py:52
  52.5 4.6 %all-to-all-start.1 = ((bf16[16,64,128]{2,1,0:T(8,128)(2,1)}), bf16[16,64,128]{2,1,0:T(8,128)(2,1)S(1)}, u32[]{:S(2)}, u32[]{:S(2)}) async-start(bf16[16,64,128]{2,1,0:T(8,128)(2,1)} %shard_map.88), calls=%async_computation.1 | async-start | bytes 524288 | tf_op jit(solution)/shard_map/all_to_all | solution.py:461
  57.3 8.6 %all-to-all-done.1.grad_ref = bf16[16,64,128]{2,1,0:T(8,128)(2,1)S(1)} async-done(((bf16[16,64,128]{2,1,0:T(8,128)(2,1)}), bf16[16,64,128]{2,1,0:T(8,128)(2,1)S(1)}, u32[]{:S(2)}, u32[]{:S(2)}) %all-to-all-start.1) | async-done | bytes 262176 | tf_op jit(solution)/shard_map/all_to_all | solution.py:461
  65.9 6.0 %shard_map.89 = (bf16[192,1152]{1,0:T(8,128)(2,1)}, f32[88,1152]{1,0:T(8,128)}, bf16[32,72,128]{2,1,0:T(8,128)(2,1)}, bf16[192,128]{1,0:T(8,128)(2,1)S(1)}, bf16...) custom-call(bf16[16,64,128]{2,1,0:T(8,128)(2,1)S(1)} %all-to-all-done.1.grad_ref, ...), custom_call_target="tpu_custom_call" | custom-call | tf_op jit(solution)/shard_map/pallas_call | solution.py:52
  71.9 9.1 %all-to-all-start.2 = ((bf16[32,72,128]{2,1,0:T(8,128)(2,1)}), bf16[32,72,128]{2,1,0:T(8,128)(2,1)S(1)}, u32[]{:S(2)}, u32[]{:S(2)}) async-start(bf16[32,72,128]{2,1,0:T(8,128)(2,1)} %get-tuple-element.44), calls=%async_computation.2 | async-start | bytes 1179648 | tf_op jit(solution)/shard_map/all_to_all | solution.py:461
  81.0 3.3 %collective-permute-start.4 = (bf16[192,128]{1,0:T(8,128)(2,1)S(1)}, bf16[192,128]{1,0:T(8,128)(2,1)S(1)}, u32[]{:S(2)}, u32[]{:S(2)}) collective-permute-start(bf16[192,128]{1,0:T(8,128)(2,1)S(1)} %get-tuple-element.45), channel_id=1, source_target_pairs={{0,4},{4,8},{8,12},{1,5},{5,9},{9,13},{2,6},{6,10},{10,14},{3,7},{... | collective-permute-start | bytes 147464 | tf_op jit(solution)/shard_map/ppermute | solution.py:572
  84.3 1.3 %collective-permute-start.5 = (bf16[192,128]{1,0:T(8,128)(2,1)S(1)}, bf16[192,128]{1,0:T(8,128)(2,1)S(1)}, u32[]{:S(2)}, u32[]{:S(2)}) collective-permute-start(bf16[192,128]{1,0:T(8,128)(2,1)S(1)} %get-tuple-element.46), channel_id=1, source_target_pairs={{4,0},{8,4},{12,8},{5,1},{9,5},{13,9},{6,2},{10,6},{14,10},{7,3},{... | collective-permute-start | bytes 147464 | tf_op jit(solution)/shard_map/ppermute | solution.py:572
  85.6 3.1 %collective-permute-done.4.top_ref = bf16[192,128]{1,0:T(8,128)(2,1)S(1)} collective-permute-done((bf16[192,128]{1,0:T(8,128)(2,1)S(1)}, bf16[192,128]{1,0:T(8,128)(2,1)S(1)}, u32[]{:S(2)}, u32[]{:S(2)}) %collective-permute-start.4) | collective-permute-done | bytes 49184 | tf_op jit(solution)/shard_map/ppermute | solution.py:572
  88.7 1.9 %collective-permute-done.5.bottom_ref = bf16[192,128]{1,0:T(8,128)(2,1)S(1)} collective-permute-done((bf16[192,128]{1,0:T(8,128)(2,1)S(1)}, bf16[192,128]{1,0:T(8,128)(2,1)S(1)}, u32[]{:S(2)}, u32[]{:S(2)}) %collective-permute-start.5) | collective-permute-done | bytes 49184 | tf_op jit(solution)/shard_map/ppermute | solution.py:572
  90.7 2.6 %all-to-all-done.2.parts_ref = bf16[32,72,128]{2,1,0:T(8,128)(2,1)S(1)} async-done(((bf16[32,72,128]{2,1,0:T(8,128)(2,1)}), bf16[32,72,128]{2,1,0:T(8,128)(2,1)S(1)}, u32[]{:S(2)}, u32[]{:S(2)}) %all-to-all-start.2) | async-done | bytes 589856 | tf_op jit(solution)/shard_map/all_to_all | solution.py:461
  93.2 0.8 shard_map.90
  94.0 3.9 %all-to-all-start.3 = ((bf16[8,72,128]{2,1,0:T(8,128)(2,1)}), bf16[8,72,128]{2,1,0:T(8,128)(2,1)S(1)}, u32[]{:S(2)}, u32[]{:S(2)}) async-start(bf16[8,72,128]{2,1,0:T(8,128)(2,1)} %shard_map.90), calls=%async_computation.3 | async-start | bytes 294912 | tf_op jit(solution)/shard_map/all_to_all | solution.py:461
  98.0 2.2 %collective-permute-start.6 = (bf16[192,128]{1,0:T(8,128)(2,1)S(1)}, bf16[192,128]{1,0:T(8,128)(2,1)S(1)}, u32[]{:S(2)}, u32[]{:S(2)}) collective-permute-start(bf16[192,128]{1,0:T(8,128)(2,1)S(1)} %get-tuple-element.52), channel_id=1, source_target_pairs={{0,1},{1,2},{2,3},{3,0},{4,5},{5,6},{6,7},{7,4},{8,9},{9,10},{10,1... | collective-permute-start | bytes 147464 | tf_op jit(solution)/shard_map/ppermute | solution.py:578
  100.2 1.2 collective-permute-done.6.left_ref
  101.4 4.1 %collective-permute-done.7.right_ref = bf16[192,128]{1,0:T(8,128)(2,1)S(1)} collective-permute-done((bf16[192,128]{1,0:T(8,128)(2,1)S(1)}, bf16[192,128]{1,0:T(8,128)(2,1)S(1)}, u32[]{:S(2)}, u32[]{:S(2)}) %collective-permute-start.7) | collective-permute-done | bytes 49184 | tf_op jit(solution)/shard_map/ppermute | solution.py:579
  105.6 0.3 all-to-all-done.3.parts_ref
  105.9 0.9 shard_map.93
  106.7 6.4 %all-to-all-start.4 = ((bf16[32,72,128]{2,1,0:T(8,128)(2,1)}), bf16[32,72,128]{2,1,0:T(8,128)(2,1)S(1)}, u32[]{:S(2)}, u32[]{:S(2)}) async-start(bf16[32,72,128]{2,1,0:T(8,128)(2,1)} %shard_map.93), calls=%async_computation.4 | async-start | bytes 1179648 | tf_op jit(solution)/shard_map/all_to_all | solution.py:461
  113.2 3.6 %shard_map.92 = bf16[664,128]{1,0:T(8,128)(2,1)} custom-call(bf16[192,1152]{1,0:T(8,128)(2,1)} %get-tuple-element.41.grad_pre_far, f32[88,1152]{1,0:T(8,128)} %get-tuple-element.42.grad_far, f32[88,1152]{1,0:T(8,128)} %get-tuple-element.43.latent_far, f32[1,83]{1,0:T(1,128)S(1)} %bitcast.21, bf16[792,192]{1,0:T(8,128)(2,1)S(1)} %bitcast.17, ...), custom_call_target="tpu_custom_call" | custom-call | tf_op jit(solution)/shard_map/pallas_call | solution.py:52
  116.8 8.5 %all-to-all-done.4.parts_ref = bf16[32,72,128]{2,1,0:T(8,128)(2,1)S(1)} async-done(((bf16[32,72,128]{2,1,0:T(8,128)(2,1)}), bf16[32,72,128]{2,1,0:T(8,128)(2,1)S(1)}, u32[]{:S(2)}, u32[]{:S(2)}) %all-to-all-start.4) | async-done | bytes 589856 | tf_op jit(solution)/shard_map/all_to_all | solution.py:461
  125.3 1.4 %shard_map.94 = (f32[9,83,192]{2,1,0:T(8,128)}, f32[9,83,192]{2,1,0:T(8,128)}) custom-call(bf16[32,72,128]{2,1,0:T(8,128)(2,1)S(1)} %all-to-all-done.4.parts_ref), custom_call_target="tpu_custom_call" | custom-call | tf_op jit(solution)/shard_map/pallas_call | solution.py:52
  (19 shorter events, 0.9 us)
Async XLA Ops:
  0.6 18.5 %copy-start.1 = (bf16[9,83,192]{2,1,0:T(8,128)(2,1)S(1)}, bf16[9,83,192]{2,1,0:T(8,128)(2,1)}, u32[]{:S(2)}) copy-start(bf16[9,83,192]{2,1,0:T(8,128)(2,1)} %param.11) | copy-start | bytes 860548
  0.6 22.1 %copy-start = (f32[83]{0:T(128)S(1)}, f32[83]{0:T(128)}, u32[]{:S(2)}) copy-start(f32[83]{0:T(128)} %param.9) | copy-start | bytes 1000
  2.8 5.7 %collective-permute-start = (bf16[5,88,128]{2,1,0:T(8,128)(2,1)S(1)}, bf16[5,88,128]{2,1,0:T(8,128)(2,1)S(1)}, u32[]{:S(2)}, u32[]{:S(2)}) collective-permute-start(bf16[5,88,128]{2,1,0:T(8,128)(2,1)S(1)} %get-tuple-element.32), channel_id=1, source_target_pairs={{0,4},{4,8},{8,12},{1,5},{5,9},{9,13},{2,6},{6,10},{10,14},{3,7},{... | collective-permute-start | bytes 337928 | tf_op jit(solution)/shard_map/ppermute | solution.py:490
  6.7 5.5 %collective-permute-start.1 = (bf16[5,88,128]{2,1,0:T(8,128)(2,1)S(1)}, bf16[5,88,128]{2,1,0:T(8,128)(2,1)S(1)}, u32[]{:S(2)}, u32[]{:S(2)}) collective-permute-start(bf16[5,88,128]{2,1,0:T(8,128)(2,1)S(1)} %get-tuple-element.33), channel_id=1, source_target_pairs={{4,0},{8,4},{12,8},{5,1},{9,5},{13,9},{6,2},{10,6},{14,10},{7,3},{... | collective-permute-start | bytes 337928 | tf_op jit(solution)/shard_map/ppermute | solution.py:491
  12.8 6.4 %collective-permute-start.2 = (f32[88,128]{1,0:T(8,128)S(1)}, f32[88,128]{1,0:T(8,128)S(1)}, u32[]{:S(2)}, u32[]{:S(2)}) collective-permute-start(f32[88,128]{1,0:T(8,128)S(1)} %get-tuple-element.34), channel_id=1, source_target_pairs={{0,1},{1,2},{2,3},{3,0},{4,5},{5,6},{6,7},{7,4},{8,9},{9,10},{10,1... | collective-permute-start | bytes 135176 | tf_op jit(solution)/shard_map/ppermute | solution.py:496
  17.8 5.0 %collective-permute-start.3 = (f32[88,128]{1,0:T(8,128)S(1)}, f32[88,128]{1,0:T(8,128)S(1)}, u32[]{:S(2)}, u32[]{:S(2)}) collective-permute-start(f32[88,128]{1,0:T(8,128)S(1)} %get-tuple-element.35), channel_id=1, source_target_pairs={{1,0},{2,1},{3,2},{0,3},{5,4},{6,5},{7,6},{4,7},{9,8},{10,9},{11,1... | collective-permute-start | bytes 135176 | tf_op jit(solution)/shard_map/ppermute | solution.py:497
  52.5 13.5 %all-to-all-start.1 = ((bf16[16,64,128]{2,1,0:T(8,128)(2,1)}), bf16[16,64,128]{2,1,0:T(8,128)(2,1)S(1)}, u32[]{:S(2)}, u32[]{:S(2)}) async-start(bf16[16,64,128]{2,1,0:T(8,128)(2,1)} %shard_map.88), calls=%async_computation.1 | async-start | bytes 524288 | tf_op jit(solution)/shard_map/all_to_all | solution.py:461
  71.9 41.2 %copy-start.2 = (bf16[9,192,83]{1,2,0:T(8,128)(2,1)S(1)}, bf16[9,192,83]{1,2,0:T(8,128)(2,1)}, u32[]{:S(2)}) copy-start(bf16[9,192,83]{1,2,0:T(8,128)(2,1)} %param.10) | copy-start | bytes 860548
  71.9 21.3 %all-to-all-start.2 = ((bf16[32,72,128]{2,1,0:T(8,128)(2,1)}), bf16[32,72,128]{2,1,0:T(8,128)(2,1)S(1)}, u32[]{:S(2)}, u32[]{:S(2)}) async-start(bf16[32,72,128]{2,1,0:T(8,128)(2,1)} %get-tuple-element.44), calls=%async_computation.2 | async-start | bytes 1179648 | tf_op jit(solution)/shard_map/all_to_all | solution.py:461
  81.0 7.7 %collective-permute-start.4 = (bf16[192,128]{1,0:T(8,128)(2,1)S(1)}, bf16[192,128]{1,0:T(8,128)(2,1)S(1)}, u32[]{:S(2)}, u32[]{:S(2)}) collective-permute-start(bf16[192,128]{1,0:T(8,128)(2,1)S(1)} %get-tuple-element.45), channel_id=1, source_target_pairs={{0,4},{4,8},{8,12},{1,5},{5,9},{9,13},{2,6},{6,10},{10,14},{3,7},{... | collective-permute-start | bytes 147464 | tf_op jit(solution)/shard_map/ppermute | solution.py:572
  84.3 6.3 %collective-permute-start.5 = (bf16[192,128]{1,0:T(8,128)(2,1)S(1)}, bf16[192,128]{1,0:T(8,128)(2,1)S(1)}, u32[]{:S(2)}, u32[]{:S(2)}) collective-permute-start(bf16[192,128]{1,0:T(8,128)(2,1)S(1)} %get-tuple-element.46), channel_id=1, source_target_pairs={{4,0},{8,4},{12,8},{5,1},{9,5},{13,9},{6,2},{10,6},{14,10},{7,3},{... | collective-permute-start | bytes 147464 | tf_op jit(solution)/shard_map/ppermute | solution.py:572
  94.0 11.9 %all-to-all-start.3 = ((bf16[8,72,128]{2,1,0:T(8,128)(2,1)}), bf16[8,72,128]{2,1,0:T(8,128)(2,1)S(1)}, u32[]{:S(2)}, u32[]{:S(2)}) async-start(bf16[8,72,128]{2,1,0:T(8,128)(2,1)} %shard_map.90), calls=%async_computation.3 | async-start | bytes 294912 | tf_op jit(solution)/shard_map/all_to_all | solution.py:461
  98.0 3.4 %collective-permute-start.6 = (bf16[192,128]{1,0:T(8,128)(2,1)S(1)}, bf16[192,128]{1,0:T(8,128)(2,1)S(1)}, u32[]{:S(2)}, u32[]{:S(2)}) collective-permute-start(bf16[192,128]{1,0:T(8,128)(2,1)S(1)} %get-tuple-element.52), channel_id=1, source_target_pairs={{0,1},{1,2},{2,3},{3,0},{4,5},{5,6},{6,7},{7,4},{8,9},{9,10},{10,1... | collective-permute-start | bytes 147464 | tf_op jit(solution)/shard_map/ppermute | solution.py:578
  100.2 5.3 %collective-permute-start.7 = (bf16[192,128]{1,0:T(8,128)(2,1)S(1)}, bf16[192,128]{1,0:T(8,128)(2,1)S(1)}, u32[]{:S(2)}, u32[]{:S(2)}) collective-permute-start(bf16[192,128]{1,0:T(8,128)(2,1)S(1)} %get-tuple-element.53), channel_id=1, source_target_pairs={{1,0},{2,1},{3,2},{0,3},{5,4},{6,5},{7,6},{4,7},{9,8},{10,9},{11,1... | collective-permute-start | bytes 147464 | tf_op jit(solution)/shard_map/ppermute | solution.py:579
  106.7 18.6 %all-to-all-start.4 = ((bf16[32,72,128]{2,1,0:T(8,128)(2,1)}), bf16[32,72,128]{2,1,0:T(8,128)(2,1)S(1)}, u32[]{:S(2)}, u32[]{:S(2)}) async-start(bf16[32,72,128]{2,1,0:T(8,128)(2,1)} %shard_map.93), calls=%async_computation.4 | async-start | bytes 1179648 | tf_op jit(solution)/shard_map/all_to_all | solution.py:461

commit v8 on v7

--- a/solution.py
+++ b/solution.py
@@ -19,7 +19,9 @@
 NEAR = 1
 FAR = 2
 RIM = NEAR + FAR
-PITCH = COLS + 2 * RIM
+SIDE = 4
+BESIDE = 2
+PITCH = COLS + 2 * SIDE
 TALL = ROWS + 2 * RIM
 TILES = -(-TALL * PITCH // 128)
 FLAT = 128 * TILES
@@ -159,9 +161,9 @@
     lane = lanes_of(CP)
     left = jnp.zeros((CP, 128), f32)
     right = jnp.zeros((CP, 128), f32)
-    plan = [(latent_row, row, RIM * row, RIM) for row in range(TALL)]
+    plan = [(latent_row, row, SIDE * row, SIDE) for row in range(TALL)]
     plan += [
-        (truth_row, row, RIM * TALL + NEAR * row, NEAR) for row in range(ROWS + 2 * NEAR)
+        (truth_row, row, SIDE * TALL + BESIDE * row, BESIDE) for row in range(ROWS + 2 * NEAR)
     ]
     for source, row, start, width in plan:
         values = source(own_ref, top_ref, bottom_ref, row)
@@ -195,14 +197,14 @@
 ):
     pieces, truths = [], []
     for row in range(TALL):
-        pieces.append((functools.partial(latent_row, own_ref, top_ref, bottom_ref, row), 0, PITCH * row + RIM, COLS))
-        pieces.append((lambda: left_ref[...], RIM * row, PITCH * row, RIM))
-        pieces.append((lambda: right_ref[...], RIM * row, PITCH * row + RIM + COLS, RIM))
+        pieces.append((functools.partial(latent_row, own_ref, top_ref, bottom_ref, row), 0, PITCH * row + SIDE, COLS))
+        pieces.append((lambda: left_ref[...], SIDE * row, PITCH * row, SIDE))
+        pieces.append((lambda: right_ref[...], SIDE * row, PITCH * row + SIDE + COLS, SIDE))
     for row in range(ROWS + 2 * NEAR):
-        flat, lane = PITCH * (row + FAR) + RIM, RIM * TALL + NEAR * row
+        flat, lane = PITCH * (row + FAR) + SIDE, SIDE * TALL + BESIDE * row
         truths.append((functools.partial(truth_row, own_ref, top_ref, bottom_ref, row), 0, flat, COLS))
-        truths.append((lambda: left_ref[...], lane, flat - NEAR, NEAR))
-        truths.append((lambda: right_ref[...], lane, flat + COLS, NEAR))
+        truths.append((lambda: left_ref[...], lane, flat - BESIDE, BESIDE))
+        truths.append((lambda: right_ref[...], lane, flat + COLS, BESIDE))
     gain = gain_column(gain_ref)
     lane = lanes_of(CP)
     inner_low, inner_high = PITCH * FAR, PITCH * (TALL - FAR)
@@ -290,16 +292,18 @@
     grad_ref[...] = grads[...].astype(bf16)
 
 
-def flat_row(values, row, first):
-    index, off = divmod(PITCH * (row + RIM) + RIM, 128)
-    near = pltpu.roll(values(index - first), 128 - off, 1)
-    far = pltpu.roll(values(index + 1 - first), 128 - off, 1)
+def flat_lanes(values, start, count):
+    index, off = divmod(start - 128 * OWN[0], 128)
+    near = pltpu.roll(values(index), 128 - off, 1)
+    if index + 1 == count:
+        return near
+    far = pltpu.roll(values(index + 1), 128 - off, 1)
     return jnp.where(lanes_of(near.shape[0]) < 128 - off, near, far)
 
 
 def backward_kernel(
-    grad_ref, pre_far, hidden_far, window_far, valid_ref, mine_ref, w2_ref,
-    grad_pre_ref, own_grad_ref, weights_ref, up_ref, down_ref, left_ref, right_ref,
+    grad_ref, pre_far, hidden_far, window_far, valid_ref, mine_ref, wide_ref, w2_ref,
+    grad_pre_ref, own_grad_ref, weights_ref, up_ref, down_ref,
     pre_ref, hidden_ref, window_ref, chunks, grad, window, grad_pre, packed, semaphores,
 ):
     moves = started((hidden_far, hidden_ref), (pre_far, pre_ref), (window_far, window_ref), semaphores=semaphores)
@@ -336,10 +340,11 @@
         square = pre * pre
         curve = jnp.tanh(GELU_A * (pre + GELU_B * (square * pre)))
         slope = 0.5 * (1.0 + curve) + 0.5 * pre * (1.0 - curve * curve) * (GELU_A * (1.0 + 3.0 * GELU_B * square))
-        grad_pre[:, span] = (grad_hidden * slope * mine_ref[:, span]).astype(bf16)
+        grad_pre[:, span] = (grad_hidden * slope * wide_ref[:, span]).astype(bf16)
     later += started((grad_pre, grad_pre_ref), semaphores=semaphores.at[4:5])
+    own_pre = (grad_pre[...].astype(f32) * mine_ref[...]).astype(bf16)
     moves[2].wait()
-    grad_in = lax.dot_general(window_ref[...], grad_pre[...], across, preferred_element_type=f32)
+    grad_in = lax.dot_general(window_ref[...], own_pre, across, preferred_element_type=f32)
     for k in range(9):
         values = grad_in[CI * k : CI * k + C, :]
         packed[C * k : C * (k + 1), :] = values[:, 0:128]
@@ -347,34 +352,17 @@
     packed[27 * C :, :] = jnp.zeros((GROUPS * PIECE - 27 * C, 128), f32)
     for place in range(GROUPS):
         weights_ref[place] = packed[PIECE * place : PIECE * place + PIECE, :].astype(bf16)
-    lane = lanes_of(HID)
-    left, right = jnp.zeros((HID, 128), f32), jnp.zeros((HID, 128), f32)
-    for row in range(ROWS):
-        values = flat_row(lambda index: grad_pre[:, tile(index)].astype(f32), row, OWN[0])
-        if row == 0:
-            up_ref[...] = values.astype(bf16)
-        if row == ROWS - 1:
-            down_ref[...] = values.astype(bf16)
-        left = jnp.where(lane == row + 1, pltpu.roll(values, row + 1, 1), left)
-        right = jnp.where(lane == row + 1, pltpu.roll(values, row + 2, 1), right)
-    left_ref[...] = left.astype(bf16)
-    right_ref[...] = right.astype(bf16)
+    for row, sent_ref in ((0, up_ref), (ROWS - 1, down_ref)):
+        start = PITCH * (row + RIM) + SIDE - 1
+        for half in range(2):
+            values = flat_lanes(lambda index: grad_pre[:, tile(index)].astype(f32), start + 128 * half, OWN[1] - OWN[0])
+            sent_ref[:, tile(half)] = values.astype(bf16)
     for move in later:
         move.wait()
 
 
-def corners_kernel(top_ref, bottom_ref, left_ref, right_ref, to_left_ref, to_right_ref):
-    lane = lanes_of(HID)
-    top, bottom = top_ref[...].astype(f32), bottom_ref[...].astype(f32)
-    for step, columns_ref, sent_ref in ((0, left_ref, to_left_ref), (1, right_ref, to_right_ref)):
-        values = columns_ref[...].astype(f32)
-        values = jnp.where(lane == 0, pltpu.roll(top, step, 1) if step else top, values)
-        values = jnp.where(lane == ROWS + 1, pltpu.roll(bottom, ROWS + 1 + step, 1), values)
-        sent_ref[...] = values.astype(bf16)
-
-
 def states_kernel(
-    grad_pre_far, grad_far, latent_far, gain_ref, w1_ref, top_ref, bottom_ref, left_ref, right_ref,
+    grad_pre_far, grad_far, latent_far, gain_ref, w1_ref, top_ref, bottom_ref,
     states_ref,
     own_pre, grad, latent, grad_pre, partial, shifted, result, semaphores,
 ):
@@ -388,14 +376,11 @@
             return own_pre[:, tile(index - OWN[0])].astype(f32)
         return jnp.zeros((HID, 128), f32)
 
-    pieces = [
-        (lambda: top_ref[...].astype(f32), 0, PITCH * (RIM - 1) + RIM, COLS),
-        (lambda: bottom_ref[...].astype(f32), 0, PITCH * (RIM + ROWS) + RIM, COLS),
-    ]
-    for row in range(ROWS + 2):
-        flat = PITCH * (row + RIM - 1) + RIM
-        pieces.append((lambda: left_ref[...].astype(f32), row, flat - 1, 1))
-        pieces.append((lambda: right_ref[...].astype(f32), row, flat + COLS, 1))
+    pieces = []
+    for row, strip_ref in ((RIM - 1, top_ref), (RIM + ROWS, bottom_ref)):
+        for half, width in ((0, 128), (1, COLS + 2 - 128)):
+            values = functools.partial(lambda ref, index: ref[:, tile(index)].astype(f32), strip_ref, half)
+            pieces.append((values, 0, PITCH * row + SIDE - 1 + 128 * half, width))
     for index, values in flat_tiles(pieces, *SPREAD, HID, base):
         grad_pre[:, tile(index - SPREAD[0])] = values.astype(bf16)
     for first in range(0, span, 512):
@@ -421,7 +406,8 @@
         mean_both = jnp.sum(pull * unit, axis=0, keepdims=True) * (1.0 / C)
         shifted[:, tile(index)] = grad[:, tile(index)] + scale * (pull - mean_pull - unit * mean_both)
     for row in range(ROWS):
-        values = flat_row(lambda index: shifted[:, tile(index)], row, OWN[0])
+        start = PITCH * (row + RIM) + SIDE
+        values = flat_lanes(lambda index: shifted[:, tile(index)], start, OWN[1] - OWN[0])
         result[pl.ds(row, C, stride=ROWS), :] = values[0:C]
     states_ref[...] = result[...].astype(bf16)
 
@@ -497,11 +483,13 @@
     right = lax.ppermute(to_left, "lon", backward)
 
     place = jnp.arange(FLAT, dtype=jnp.int32)
-    row, column = place // PITCH - RIM, place % PITCH - RIM
+    row, column = place // PITCH - RIM, place % PITCH - SIDE
     line = row + ROWS * lax.axis_index("lat")
     valid = ((line >= 0) & (line < ROWS * lax.axis_size("lat"))).astype(f32)[None]
     mine = ((row >= 0) & (row < ROWS) & (column >= 0) & (column < COLS)).astype(f32)[None]
     mine = mine[:, 128 * OWN[0] : 128 * OWN[1]]
+    wide = ((row >= 0) & (row < ROWS) & (column >= -1) & (column <= COLS)).astype(f32)[None]
+    wide = wide[:, 128 * OWN[0] : 128 * OWN[1]]
     w1_stack = padded(first_stencil_kernel, 2, CI).transpose(1, 0, 2).reshape(HID, 9 * CI)
     w2_stack = padded(second_stencil_kernel, 1, CP).reshape(9 * CP, HID)
     w2_turned = padded(second_stencil_kernel, 1, CI).transpose(2, 0, 1).reshape(HID, 9 * CI)
@@ -543,15 +531,15 @@
         spread, truth,
     )
     grads = swap(grads, member_axes)
-    strip = ((HID, 128), bf16)
-    grad_pre, own_grad, weights, up, down, to_left, to_right = call(
+    strip = ((HID, 256), bf16)
+    grad_pre, own_grad, weights, up, down = call(
         backward_kernel,
         22,
         [
             ((HID, own_lanes), (bf16,)),
             ((CP, own_lanes), (f32,)),
             ((GROUPS, PIECE, 128), bf16),
-            strip, strip, strip, strip,
+            strip, strip,
         ],
         [
             ((HID, own_lanes), f32),
@@ -563,7 +551,7 @@
             ((HID, own_lanes), bf16),
             ((GROUPS * PIECE, 128), f32),
         ],
-        grads, pre, hidden, window, valid, mine, w2_turned,
+        grads, pre, hidden, window, valid, mine, wide, w2_turned,
         far=(1, 2, 3), copies=5,
     )
     parts = swap(weights, plane)
@@ -571,16 +559,9 @@
     parts, top, bottom = lax.optimization_barrier(
         (parts, lax.ppermute(down, "lat", forward), lax.ppermute(up, "lat", backward))
     )
-    to_left, to_right = call(
-        corners_kernel, 4, [strip, strip], [], top, bottom, to_left, to_right
-    )
-    forward, backward = neighbours("lon", True)
-    left = lax.ppermute(to_right, "lon", forward)
-    right = lax.ppermute(to_left, "lon", backward)
     piece = (PIECE, 128)
     (copies,) = call(total_kernel, 6, [((RING,) + piece, bf16)], [], parts)
-    parts, left, right = lax.optimization_barrier((swap(copies, "ring"), left, right))
-    (copies,) = call(total_kernel, 6, [((GROUPS,) + piece, bf16)], [], parts)
+    (copies,) = call(total_kernel, 6, [((GROUPS,) + piece, bf16)], [], swap(copies, "ring"))
     (states,) = call(
         states_kernel,
         16,
@@ -594,7 +575,7 @@
             ((CP, own_lanes), f32),
             ((C * ROWS, COLS), f32),
         ],
-        grad_pre, own_grad, latent, gain, w1_turned, top, bottom, left, right,
+        grad_pre, own_grad, latent, gain, w1_turned, top, bottom,
         far=(0, 1, 2), copies=3,
     )
     grad_in, grad_out = call(

time: 127 us -> 127 us (level)
  blocking collectives: 22.8 us -> 34.4 us
  waiting for transfers between devices: 38 us -> 32.5 us
  starting transfers between devices: 41 us -> 35.9 us
  Pallas kernels: 22.3 us -> 21 us
    all_to_all x1 -> x2, blocking collectives: 22.8 us -> 34.4 us  [swap(): return lax.all_to_all(values, axes, split_axis=0, concat_axis=0, tiled=True)]
    ppermute x2 -> x1, waiting for transfers between devices: 7.67 us -> 3.54 us  [on_device(): right = lax.ppermute(to_left, 'lon', backward)]
    all_to_all x4 -> x3, starting transfers between devices: 24 us -> 21.1 us  [swap(): return lax.all_to_all(values, axes, split_axis=0, concat_axis=0, tiled=True)]
    ppermute x2 -> x1, starting transfers between devices: 7.2 us -> 4.98 us  [on_device(): left = lax.ppermute(to_right, 'lon', forward)]
    pallas_call x10 -> x9, Pallas kernels: 22.3 us -> 21 us  [call(): pl.pallas_call(kernel, out_shape=[(pltpu.HBM if isinstance(given, tuple)...]
    all_to_all x4 -> x3, waiting for transfers between devices: 20 us -> 18.8 us  [swap(): return lax.all_to_all(values, axes, split_axis=0, concat_axis=0, tiled=True)]
  transfers between devices with their start and end apart: 12 -> 9, of which waited for: 11 -> 8; matrix products, arithmetic and copies ran while one was open for 1% -> 1% of each run, Pallas kernels for 3% -> 3%
where the time goes in v8:
time: 127 us
  starting transfers between devices  35.9 us (28%)
  blocking collectives  34.4 us (27%)
  waiting for transfers between devices  32.5 us (26%)
  Pallas kernels  21 us (17%)
  local copies, waits for them, and re-layouts  1.74 us (1%)
    all_to_all x2, blocking collectives, swap(): return lax.all_to_all(values, axes, split_axis=0, concat_axis=0, tiled=True)  34.4 us
    all_to_all x3, starting transfers between devices, swap(): return lax.all_to_all(values, axes, split_axis=0, concat_axis=0, tiled=True)  21.1 us
    pallas_call x9, Pallas kernels, call(): pl.pallas_call(kernel, out_shape=[(pltpu.HBM if isinstance(given, tuple)...  21 us
    all_to_all x3, waiting for transfers between devices, swap(): return lax.all_to_all(values, axes, split_axis=0, concat_axis=0, tiled=True)  18.8 us
    ppermute x1, starting transfers between devices, on_device(): left = lax.ppermute(to_right, 'lon', forward)  4.98 us
    ppermute x1, waiting for transfers between devices, on_device(): lax.ppermute(down, 'lat', forward)  4.13 us
    ppermute x1, starting transfers between devices, on_device(): top = lax.ppermute(down, 'lat', forward)  3.95 us
    ppermute x1, waiting for transfers between devices, on_device(): bottom = lax.ppermute(up, 'lat', backward)  3.76 us
  transfers between devices with their start and end apart: 9, of which 8 were waited for; matrix products, arithmetic and copies ran while one was open for 1% of the time, Pallas kernels for 3%

profile of v8, /device:TPU:1, one launch (start us, length us, event | category | flops | bytes accessed | tf_op | source)
XLA Modules:
  0.0 126.6 jit_solution(16016418300449632532)
XLA Ops:
  0.7 2.1 %shard_map.85 = (f32[16,88,128]{2,1,0:T(8,128)S(1)}, bf16[5,88,128]{2,1,0:T(8,128)(2,1)S(1)}, bf16[5,88,128]{2,1,0:T(8,128)(2,1)S(1)}) custom-call(bf16[83,8,128]{2,1,0:T(8,128)(2,1)} %bitcast.25, bf16[83,8,128]{2,1,0:T(8,128)(2,1)} %bitcast.26, bf16[83,8,128]{2,1,0:T(8,128)(2,1)} %target_ref.1, f32[1,83]{1,0:T(1,128)} %bitcast.19), custom_call_target="tpu_custom_call" | custom-call | tf_op jit(solution)/shard_map/pallas_call | solution.py:54
  2.8 4.0 %collective-permute-start = (bf16[5,88,128]{2,1,0:T(8,128)(2,1)S(1)}, bf16[5,88,128]{2,1,0:T(8,128)(2,1)S(1)}, u32[]{:S(2)}, u32[]{:S(2)}) collective-permute-start(bf16[5,88,128]{2,1,0:T(8,128)(2,1)S(1)} %get-tuple-element.25), channel_id=1, source_target_pairs={{0,4},{4,8},{8,12},{1,5},{5,9},{9,13},{2,6},{6,10},{10,14},{3,7},{... | collective-permute-start | bytes 337928 | tf_op jit(solution)/shard_map/ppermute | solution.py:476
  6.7 1.3 %collective-permute-start.1 = (bf16[5,88,128]{2,1,0:T(8,128)(2,1)S(1)}, bf16[5,88,128]{2,1,0:T(8,128)(2,1)S(1)}, u32[]{:S(2)}, u32[]{:S(2)}) collective-permute-start(bf16[5,88,128]{2,1,0:T(8,128)(2,1)S(1)} %get-tuple-element.26), channel_id=1, source_target_pairs={{4,0},{8,4},{12,8},{5,1},{9,5},{13,9},{6,2},{10,6},{14,10},{7,3},{... | collective-permute-start | bytes 337928 | tf_op jit(solution)/shard_map/ppermute | solution.py:477
  8.1 0.3 collective-permute-done.top_ref
  8.5 3.8 %collective-permute-done.1.bottom_ref = bf16[5,88,128]{2,1,0:T(8,128)(2,1)S(1)} collective-permute-done((bf16[5,88,128]{2,1,0:T(8,128)(2,1)S(1)}, bf16[5,88,128]{2,1,0:T(8,128)(2,1)S(1)}, u32[]{:S(2)}, u32[]{:S(2)}) %collective-permute-start.1) | collective-permute-done | bytes 112672 | tf_op jit(solution)/shard_map/ppermute | solution.py:477
  12.2 0.6 shard_map.86
  12.8 5.0 %collective-permute-start.2 = (f32[88,128]{1,0:T(8,128)S(1)}, f32[88,128]{1,0:T(8,128)S(1)}, u32[]{:S(2)}, u32[]{:S(2)}) collective-permute-start(f32[88,128]{1,0:T(8,128)S(1)} %get-tuple-element.27), channel_id=1, source_target_pairs={{0,1},{1,2},{2,3},{3,0},{4,5},{5,6},{6,7},{7,4},{8,9},{9,10},{10,1... | collective-permute-start | bytes 135176 | tf_op jit(solution)/shard_map/ppermute | solution.py:482
  17.8 1.1 pad.15
  18.9 0.2 copy.11.w1_ref
  19.1 0.1 pad.16
  19.2 3.5 %collective-permute-done.3.right_ref = f32[88,128]{1,0:T(8,128)S(1)} collective-permute-done((f32[88,128]{1,0:T(8,128)S(1)}, f32[88,128]{1,0:T(8,128)S(1)}, u32[]{:S(2)}, u32[]{:S(2)}) %collective-permute-start.3) | collective-permute-done | bytes 45088 | tf_op jit(solution)/shard_map/ppermute | solution.py:483
  22.8 5.2 %shard_map.87 = (f32[1024,128]{1,0:T(8,128)S(1)}, f32[64,128]{1,0:T(8,128)S(1)}, f32[192,1152]{1,0:T(8,128)}, bf16[192,1152]{1,0:T(8,128)(2,1)}, bf16[864,1152]{1,0:T(8,128)(2,1)}, /*index=5*/f32[88,1152]{1,0:T(8,128)}) custom-call(s32[1]{0:T(128)} %bitcast.member_ref, f32[16,88,128]{2,1,0:T(8,128)S(1)} %get-tuple-element.24.own_ref, ...), custom_call_target="tpu_custom_call" | custom-call | tf_op jit(solution)/shard_map/pallas_call | solution.py:54
  27.9 22.8 %all_to_all.25.forecast_ref = f32[16,64,128]{2,1,0:T(8,128)S(1)} all-to-all(f32[16,64,128]{2,1,0:T(8,128)S(1)} %bitcast.18), channel_id=1, replica_groups=mesh['half'=2,'ring'=8,'lat'=4,'lon'=4] {'half','ring'}, dimensions={0} | all-to-all | bytes 1048576 | tf_op jit(solution)/shard_map/all_to_all | solution.py:447
  50.7 1.8 %shard_map.88 = bf16[16,64,128]{2,1,0:T(8,128)(2,1)} custom-call(f32[16,64,128]{2,1,0:T(8,128)S(1)} %all_to_all.25.forecast_ref, f32[64,128]{1,0:T(8,128)S(1)} %get-tuple-element.30.truth_ref), custom_call_target="tpu_custom_call" | custom-call | tf_op jit(solution)/shard_map/pallas_call | solution.py:54
  52.5 4.6 %all-to-all-start.1 = ((bf16[16,64,128]{2,1,0:T(8,128)(2,1)}), bf16[16,64,128]{2,1,0:T(8,128)(2,1)S(1)}, u32[]{:S(2)}, u32[]{:S(2)}) async-start(bf16[16,64,128]{2,1,0:T(8,128)(2,1)} %shard_map.88), calls=%async_computation.1 | async-start | bytes 524288 | tf_op jit(solution)/shard_map/all_to_all | solution.py:447
  57.0 0.1 pad.17
  57.1 0.2 copy.12.w2_ref
  57.3 8.6 %all-to-all-done.1.grad_ref = bf16[16,64,128]{2,1,0:T(8,128)(2,1)S(1)} async-done(((bf16[16,64,128]{2,1,0:T(8,128)(2,1)}), bf16[16,64,128]{2,1,0:T(8,128)(2,1)S(1)}, u32[]{:S(2)}, u32[]{:S(2)}) %all-to-all-start.1) | async-done | bytes 262176 | tf_op jit(solution)/shard_map/all_to_all | solution.py:447
  65.9 5.7 %shard_map.89 = (bf16[192,1152]{1,0:T(8,128)(2,1)}, f32[88,1152]{1,0:T(8,128)}, bf16[32,72,128]{2,1,0:T(8,128)(2,1)}, bf16[192,256]{1,0:T(8,128)(2,1)S(1)}, bf16[192,256]{1,0:T(8,128)(2,1)S(1)}) custom-call(bf16[16,64,128]{2,1,0:T(8,128)(2,1)S(1)} %all-to-all-done.1.grad_ref, f32[192,1152]{1,0:T(8,128)} %get-tuple-element.31.pre_far, ...), custom_call_target="tpu_custom_call" | custom-call | tf_op jit(solution)/shard_map/pallas_call | solution.py:54
  71.7 9.1 %all-to-all-start.2 = ((bf16[32,72,128]{2,1,0:T(8,128)(2,1)}), bf16[32,72,128]{2,1,0:T(8,128)(2,1)S(1)}, u32[]{:S(2)}, u32[]{:S(2)}) async-start(bf16[32,72,128]{2,1,0:T(8,128)(2,1)} %get-tuple-element.37), calls=%async_computation.2 | async-start | bytes 1179648 | tf_op jit(solution)/shard_map/all_to_all | solution.py:447
  80.8 3.3 %collective-permute-start.4 = (bf16[192,256]{1,0:T(8,128)(2,1)S(1)}, bf16[192,256]{1,0:T(8,128)(2,1)S(1)}, u32[]{:S(2)}, u32[]{:S(2)}) collective-permute-start(bf16[192,256]{1,0:T(8,128)(2,1)S(1)} %get-tuple-element.38), channel_id=1, source_target_pairs={{0,4},{4,8},{8,12},{1,5},{5,9},{9,13},{2,6},{6,10},{10,14},{3,7},{... | collective-permute-start | bytes 294920 | tf_op jit(solution)/shard_map/ppermute | solution.py:560
  84.1 1.3 %collective-permute-start.5 = (bf16[192,256]{1,0:T(8,128)(2,1)S(1)}, bf16[192,256]{1,0:T(8,128)(2,1)S(1)}, u32[]{:S(2)}, u32[]{:S(2)}) collective-permute-start(bf16[192,256]{1,0:T(8,128)(2,1)S(1)} %get-tuple-element.39), channel_id=1, source_target_pairs={{4,0},{8,4},{12,8},{5,1},{9,5},{13,9},{6,2},{10,6},{14,10},{7,3},{... | collective-permute-start | bytes 294920 | tf_op jit(solution)/shard_map/ppermute | solution.py:560
  85.4 4.1 %collective-permute-done.4.top_ref = bf16[192,256]{1,0:T(8,128)(2,1)S(1)} collective-permute-done((bf16[192,256]{1,0:T(8,128)(2,1)S(1)}, bf16[192,256]{1,0:T(8,128)(2,1)S(1)}, u32[]{:S(2)}, u32[]{:S(2)}) %collective-permute-start.4) | collective-permute-done | bytes 98336 | tf_op jit(solution)/shard_map/ppermute | solution.py:560
  89.5 1.9 %collective-permute-done.5.bottom_ref = bf16[192,256]{1,0:T(8,128)(2,1)S(1)} collective-permute-done((bf16[192,256]{1,0:T(8,128)(2,1)S(1)}, bf16[192,256]{1,0:T(8,128)(2,1)S(1)}, u32[]{:S(2)}, u32[]{:S(2)}) %collective-permute-start.5) | collective-permute-done | bytes 98336 | tf_op jit(solution)/shard_map/ppermute | solution.py:560
  91.4 1.5 %all-to-all-done.2.parts_ref = bf16[32,72,128]{2,1,0:T(8,128)(2,1)S(1)} async-done(((bf16[32,72,128]{2,1,0:T(8,128)(2,1)}), bf16[32,72,128]{2,1,0:T(8,128)(2,1)S(1)}, u32[]{:S(2)}, u32[]{:S(2)}) %all-to-all-start.2) | async-done | bytes 589856 | tf_op jit(solution)/shard_map/all_to_all | solution.py:447
  92.9 0.1 shard_map.91
  93.0 11.7 %all_to_all.26.parts_ref = bf16[8,72,128]{2,1,0:T(8,128)(2,1)S(1)} all-to-all(bf16[8,72,128]{2,1,0:T(8,128)(2,1)S(1)} %shard_map.91), channel_id=1, replica_groups=mesh['half'=2,'ring'=8,'lat'=4,'lon'=4] {'ring'}, dimensions={0} | all-to-all | bytes 294912 | tf_op jit(solution)/shard_map/all_to_all | solution.py:447
  104.7 0.9 shard_map.92
  105.6 7.4 %all-to-all-start.4 = ((bf16[32,72,128]{2,1,0:T(8,128)(2,1)}), bf16[32,72,128]{2,1,0:T(8,128)(2,1)S(1)}, u32[]{:S(2)}, u32[]{:S(2)}) async-start(bf16[32,72,128]{2,1,0:T(8,128)(2,1)} %shard_map.92), calls=%async_computation.4 | async-start | bytes 1179648 | tf_op jit(solution)/shard_map/all_to_all | solution.py:447
  113.1 3.4 %shard_map.90 = bf16[664,128]{1,0:T(8,128)(2,1)} custom-call(bf16[192,1152]{1,0:T(8,128)(2,1)} %get-tuple-element.34.grad_pre_far, f32[88,1152]{1,0:T(8,128)} %get-tuple-element.35.grad_far, f32[88,1152]{1,0:T(8,128)} %get-tuple-element.36.latent_far, f32[1,83]{1,0:T(1,128)S(1)} %bitcast.21, bf16[792,192]{1,0:T(8,128)(2,1)S(1)} %bitcast.17, ...), custom_call_target="tpu_custom_call" | custom-call | tf_op jit(solution)/shard_map/pallas_call | solution.py:54
  116.5 8.7 %all-to-all-done.4.parts_ref = bf16[32,72,128]{2,1,0:T(8,128)(2,1)S(1)} async-done(((bf16[32,72,128]{2,1,0:T(8,128)(2,1)}), bf16[32,72,128]{2,1,0:T(8,128)(2,1)S(1)}, u32[]{:S(2)}, u32[]{:S(2)}) %all-to-all-start.4) | async-done | bytes 589856 | tf_op jit(solution)/shard_map/all_to_all | solution.py:447
  125.2 1.4 %shard_map.93 = (f32[9,83,192]{2,1,0:T(8,128)}, f32[9,83,192]{2,1,0:T(8,128)}) custom-call(bf16[32,72,128]{2,1,0:T(8,128)(2,1)S(1)} %all-to-all-done.4.parts_ref), custom_call_target="tpu_custom_call" | custom-call | tf_op jit(solution)/shard_map/pallas_call | solution.py:54
  (13 shorter events, 0.2 us)
Async XLA Ops:
  0.6 18.5 %copy-start.1 = (bf16[9,83,192]{2,1,0:T(8,128)(2,1)S(1)}, bf16[9,83,192]{2,1,0:T(8,128)(2,1)}, u32[]{:S(2)}) copy-start(bf16[9,83,192]{2,1,0:T(8,128)(2,1)} %param.11) | copy-start | bytes 860548
  0.6 22.1 %copy-start = (f32[83]{0:T(128)S(1)}, f32[83]{0:T(128)}, u32[]{:S(2)}) copy-start(f32[83]{0:T(128)} %param.9) | copy-start | bytes 1000
  2.8 5.7 %collective-permute-start = (bf16[5,88,128]{2,1,0:T(8,128)(2,1)S(1)}, bf16[5,88,128]{2,1,0:T(8,128)(2,1)S(1)}, u32[]{:S(2)}, u32[]{:S(2)}) collective-permute-start(bf16[5,88,128]{2,1,0:T(8,128)(2,1)S(1)} %get-tuple-element.25), channel_id=1, source_target_pairs={{0,4},{4,8},{8,12},{1,5},{5,9},{9,13},{2,6},{6,10},{10,14},{3,7},{... | collective-permute-start | bytes 337928 | tf_op jit(solution)/shard_map/ppermute | solution.py:476
  6.7 5.5 %collective-permute-start.1 = (bf16[5,88,128]{2,1,0:T(8,128)(2,1)S(1)}, bf16[5,88,128]{2,1,0:T(8,128)(2,1)S(1)}, u32[]{:S(2)}, u32[]{:S(2)}) collective-permute-start(bf16[5,88,128]{2,1,0:T(8,128)(2,1)S(1)} %get-tuple-element.26), channel_id=1, source_target_pairs={{4,0},{8,4},{12,8},{5,1},{9,5},{13,9},{6,2},{10,6},{14,10},{7,3},{... | collective-permute-start | bytes 337928 | tf_op jit(solution)/shard_map/ppermute | solution.py:477
  12.8 6.4 %collective-permute-start.2 = (f32[88,128]{1,0:T(8,128)S(1)}, f32[88,128]{1,0:T(8,128)S(1)}, u32[]{:S(2)}, u32[]{:S(2)}) collective-permute-start(f32[88,128]{1,0:T(8,128)S(1)} %get-tuple-element.27), channel_id=1, source_target_pairs={{0,1},{1,2},{2,3},{3,0},{4,5},{5,6},{6,7},{7,4},{8,9},{9,10},{10,1... | collective-permute-start | bytes 135176 | tf_op jit(solution)/shard_map/ppermute | solution.py:482
  17.8 5.0 %collective-permute-start.3 = (f32[88,128]{1,0:T(8,128)S(1)}, f32[88,128]{1,0:T(8,128)S(1)}, u32[]{:S(2)}, u32[]{:S(2)}) collective-permute-start(f32[88,128]{1,0:T(8,128)S(1)} %get-tuple-element.28), channel_id=1, source_target_pairs={{1,0},{2,1},{3,2},{0,3},{5,4},{6,5},{7,6},{4,7},{9,8},{10,9},{11,1... | collective-permute-start | bytes 135176 | tf_op jit(solution)/shard_map/ppermute | solution.py:483
  52.5 13.5 %all-to-all-start.1 = ((bf16[16,64,128]{2,1,0:T(8,128)(2,1)}), bf16[16,64,128]{2,1,0:T(8,128)(2,1)S(1)}, u32[]{:S(2)}, u32[]{:S(2)}) async-start(bf16[16,64,128]{2,1,0:T(8,128)(2,1)} %shard_map.88), calls=%async_computation.1 | async-start | bytes 524288 | tf_op jit(solution)/shard_map/all_to_all | solution.py:447
  71.7 41.4 %copy-start.2 = (bf16[9,192,83]{1,2,0:T(8,128)(2,1)S(1)}, bf16[9,192,83]{1,2,0:T(8,128)(2,1)}, u32[]{:S(2)}) copy-start(bf16[9,192,83]{1,2,0:T(8,128)(2,1)} %param.10) | copy-start | bytes 860548
  71.7 21.3 %all-to-all-start.2 = ((bf16[32,72,128]{2,1,0:T(8,128)(2,1)}), bf16[32,72,128]{2,1,0:T(8,128)(2,1)S(1)}, u32[]{:S(2)}, u32[]{:S(2)}) async-start(bf16[32,72,128]{2,1,0:T(8,128)(2,1)} %get-tuple-element.37), calls=%async_computation.2 | async-start | bytes 1179648 | tf_op jit(solution)/shard_map/all_to_all | solution.py:447
  80.8 8.7 %collective-permute-start.4 = (bf16[192,256]{1,0:T(8,128)(2,1)S(1)}, bf16[192,256]{1,0:T(8,128)(2,1)S(1)}, u32[]{:S(2)}, u32[]{:S(2)}) collective-permute-start(bf16[192,256]{1,0:T(8,128)(2,1)S(1)} %get-tuple-element.38), channel_id=1, source_target_pairs={{0,4},{4,8},{8,12},{1,5},{5,9},{9,13},{2,6},{6,10},{10,14},{3,7},{... | collective-permute-start | bytes 294920 | tf_op jit(solution)/shard_map/ppermute | solution.py:560
  84.1 7.4 %collective-permute-start.5 = (bf16[192,256]{1,0:T(8,128)(2,1)S(1)}, bf16[192,256]{1,0:T(8,128)(2,1)S(1)}, u32[]{:S(2)}, u32[]{:S(2)}) collective-permute-start(bf16[192,256]{1,0:T(8,128)(2,1)S(1)} %get-tuple-element.39), channel_id=1, source_target_pairs={{4,0},{8,4},{12,8},{5,1},{9,5},{13,9},{6,2},{10,6},{14,10},{7,3},{... | collective-permute-start | bytes 294920 | tf_op jit(solution)/shard_map/ppermute | solution.py:560
  105.6 19.6 %all-to-all-start.4 = ((bf16[32,72,128]{2,1,0:T(8,128)(2,1)}), bf16[32,72,128]{2,1,0:T(8,128)(2,1)S(1)}, u32[]{:S(2)}, u32[]{:S(2)}) async-start(bf16[32,72,128]{2,1,0:T(8,128)(2,1)} %shard_map.92), calls=%async_computation.4 | async-start | bytes 1179648 | tf_op jit(solution)/shard_map/all_to_all | solution.py:447

commit v9 on v8

--- a/solution.py
+++ b/solution.py
@@ -101,7 +101,7 @@
 
 
 def rows_kernel(
-    emb_ref, pert_ref, target_ref, gain_ref, own_ref, up_ref, down_ref, emb, pert, target, first, second, truth, semaphores,
+    emb_ref, pert_ref, target_ref, gain_ref, own_ref, up_ref, down_ref, left_ref, right_ref, emb, pert, target, first, second, truth, semaphores,
 ):
     moves = started((emb_ref, emb), (pert_ref, pert), (target_ref, target), semaphores=semaphores)
     for move, source, wide in zip(moves, (emb, pert, target), (first, second, truth)):
@@ -113,12 +113,19 @@
     def row_of(source, r):
         return jnp.concatenate([source[pl.ds(r, C, stride=ROWS), :], rest], axis=0)
 
+    lane = lanes_of(CP)
+    left, right = jnp.zeros((CP, 128), f32), jnp.zeros((CP, 128), f32)
     for r in range(ROWS):
         parts = row_of(first, r), row_of(second, r)
         goal = row_of(truth, r)
         latent = parts[0] + parts[1]
         own_ref[r] = latent
         own_ref[ROWS + r] = goal
+        sides = (latent, SIDE * (RIM + r), SIDE), (goal, SIDE * TALL + BESIDE * (NEAR + r), BESIDE)
+        for values, start, width in sides:
+            here = (lane >= start) & (lane < start + width)
+            left = jnp.where(here, pltpu.roll(values, start % 128, 1), left)
+            right = jnp.where(here, pltpu.roll(values, (start + width) % 128, 1), right)
         if RIM <= r < ROWS - RIM:
             continue
         sent, first_row = (up_ref, 0) if r < RIM else (down_ref, ROWS - RIM)
@@ -131,6 +138,8 @@
             centered, scale = centred(latent)
             index = r - NEAR if r < RIM else r - first_row
             sent[2 * NEAR + index] = (centered * scale * gain).astype(bf16)
+    left_ref[...] = left
+    right_ref[...] = right
 
 
 def latent_row(own_ref, top_ref, bottom_ref, row):
@@ -157,21 +166,9 @@
     return bottom_ref[base + row - NEAR - ROWS].astype(f32)
 
 
-def columns_kernel(own_ref, top_ref, bottom_ref, left_ref, right_ref):
-    lane = lanes_of(CP)
-    left = jnp.zeros((CP, 128), f32)
-    right = jnp.zeros((CP, 128), f32)
-    plan = [(latent_row, row, SIDE * row, SIDE) for row in range(TALL)]
-    plan += [
-        (truth_row, row, SIDE * TALL + BESIDE * row, BESIDE) for row in range(ROWS + 2 * NEAR)
-    ]
-    for source, row, start, width in plan:
-        values = source(own_ref, top_ref, bottom_ref, row)
-        here = (lane >= start) & (lane < start + width)
-        left = jnp.where(here, pltpu.roll(values, start % 128, 1), left)
-        right = jnp.where(here, pltpu.roll(values, (start + width) % 128, 1), right)
-    left_ref[...] = left
-    right_ref[...] = right
+def columns_kernel(left_ref, right_ref, both_ref):
+    both_ref[0] = left_ref[...]
+    both_ref[1] = right_ref[...]
 
 
 def flat_tiles(pieces, first, last, height=CP, base=None):
@@ -191,21 +188,44 @@
 
 
 def forward_kernel(
-    member_ref, own_ref, top_ref, bottom_ref, left_ref, right_ref, gain_ref, valid_ref, mine_ref, w1_ref, w2_ref,
+    member_ref, own_ref, top_ref, bottom_ref, left_ref, right_ref, above_ref, below_ref, gain_ref, valid_ref, mine_ref, w1_ref, w2_ref,
     forecast_ref, truth_ref, pre_ref, hidden_ref, window_ref, latent_ref,
     latent, normed, window, hidden, partial, truth, pre_kept, hidden_kept, semaphores,
 ):
+    gain = gain_column(gain_ref)
+
+    def side_of(row, near, rows):
+        if row < near:
+            return above_ref, row + ROWS
+        if row < near + rows:
+            return None, row
+        return below_ref, row - ROWS
+
+    scaled_sides = {}
+
+    def side(ref, which, far):
+        if ref is None:
+            return (left_ref, right_ref)[which][...]
+        if not far:
+            return ref[which]
+        if (id(ref), which) not in scaled_sides:
+            centered, scale = centred(ref[which])
+            scaled_sides[id(ref), which] = centered * scale * gain
+        return scaled_sides[id(ref), which]
+
     pieces, truths = [], []
     for row in range(TALL):
+        ref, place = side_of(row, RIM, ROWS)
+        far = row < FAR or row >= TALL - FAR
         pieces.append((functools.partial(latent_row, own_ref, top_ref, bottom_ref, row), 0, PITCH * row + SIDE, COLS))
-        pieces.append((lambda: left_ref[...], SIDE * row, PITCH * row, SIDE))
-        pieces.append((lambda: right_ref[...], SIDE * row, PITCH * row + SIDE + COLS, SIDE))
+        for which, flat in ((0, PITCH * row), (1, PITCH * row + SIDE + COLS)):
+            pieces.append((functools.partial(side, ref, which, far), SIDE * place, flat, SIDE))
     for row in range(ROWS + 2 * NEAR):
-        flat, lane = PITCH * (row + FAR) + SIDE, SIDE * TALL + BESIDE * row
+        ref, place = side_of(row, NEAR, ROWS)
+        flat, lane = PITCH * (row + FAR) + SIDE, SIDE * TALL + BESIDE * place
         truths.append((functools.partial(truth_row, own_ref, top_ref, bottom_ref, row), 0, flat, COLS))
-        truths.append((lambda: left_ref[...], lane, flat - BESIDE, BESIDE))
-        truths.append((lambda: right_ref[...], lane, flat + COLS, BESIDE))
-    gain = gain_column(gain_ref)
+        truths.append((functools.partial(side, ref, 0, False), lane, flat - BESIDE, BESIDE))
+        truths.append((functools.partial(side, ref, 1, False), lane, flat + COLS, BESIDE))
     lane = lanes_of(CP)
     inner_low, inner_high = PITCH * FAR, PITCH * (TALL - FAR)
     normed[CP:CI, :] = jnp.zeros((CI - CP, FLAT), f32)
@@ -464,10 +484,10 @@
     gain = feature_scale_factor[None]
     block = (C, ROWS, COLS)
     rim = ((3 * NEAR + FAR, CP, 128), bf16)
-    own, up, down = call(
+    own, up, down, to_left, to_right = call(
         rows_kernel,
         6,
-        [((2 * ROWS, CP, 128), f32), rim, rim],
+        [((2 * ROWS, CP, 128), f32), rim, rim, ((CP, 128), f32), ((CP, 128), f32)],
         [(block, bf16)] * 3 + [((C * ROWS, COLS), f32)] * 3,
         embeddings.reshape(block), entry_perturbation.reshape(block), target, gain,
         far=(0, 1, 2), home=(3,), copies=3,
@@ -475,12 +495,13 @@
     forward, backward = neighbours("lat", False)
     top = lax.ppermute(down, "lat", forward)
     bottom = lax.ppermute(up, "lat", backward)
-    to_left, to_right = call(
-        columns_kernel, 6, [((CP, 128), f32)] * 2, [], own, top, bottom, close=(0, 1, 2)
-    )
+    to_below, to_above = forward, backward
     forward, backward = neighbours("lon", True)
     left = lax.ppermute(to_right, "lon", forward)
     right = lax.ppermute(to_left, "lon", backward)
+    (both,) = call(columns_kernel, 6, [((2, CP, 128), f32)], [], left, right, close=(0, 1))
+    above = lax.ppermute(both, "lat", to_below)
+    below = lax.ppermute(both, "lat", to_above)
 
     place = jnp.arange(FLAT, dtype=jnp.int32)
     row, column = place // PITCH - RIM, place % PITCH - SIDE
@@ -519,8 +540,8 @@
             ((HID, own_lanes), f32),
             ((HID, own_lanes), bf16),
         ],
-        member, own, top, bottom, left, right, gain, valid, mine, w1_stack, w2_stack,
-        smem=1, close=(1, 2, 3, 4, 5), copies=7,
+        member, own, top, bottom, left, right, above, below, gain, valid, mine, w1_stack, w2_stack,
+        smem=1, close=(1, 2, 3, 4, 5, 6, 7), copies=7,
     )
     spread = swap(forecast.reshape(MEMBERS, CHUNK, 128), member_axes)
     (grads,) = call(

time: 127 us -> 125 us (0.984)
  starting transfers between devices: 35.9 us -> 42.4 us
  waiting for transfers between devices: 32.5 us -> 26.8 us
  blocking collectives: 34.4 us -> 31.3 us
    ppermute x0 -> x2, starting transfers between devices: none -> 4.87 us  [the longest x1 3.58 us: on_device(): above = lax.ppermute(both, 'lat', to_below)]
    ppermute x1, waiting for transfers between devices: 3.76 us -> 0.01 us  [on_device(): bottom = lax.ppermute(up, 'lat', backward)]
    all_to_all x2, blocking collectives: 34.4 us -> 31.3 us  [swap(): return lax.all_to_all(values, axes, split_axis=0, concat_axis=0, tiled=True)]
    ppermute x1, waiting for transfers between devices: 3.54 us -> 0.43 us  [on_device(): right = lax.ppermute(to_left, 'lon', backward)]
    all_to_all x3, starting transfers between devices: 21.1 us -> 24.1 us  [swap(): return lax.all_to_all(values, axes, split_axis=0, concat_axis=0, tiled=True)]
    ppermute x0 -> x2, waiting for transfers between devices: none -> 2.51 us  [the longest x1 2.51 us: on_device(): below = lax.ppermute(both, 'lat', to_above)]
  transfers between devices with their start and end apart: 9 -> 11, of which waited for: 8 -> 7; matrix products, arithmetic and copies ran while one was open for 1% -> 1% of each run, Pallas kernels for 3% -> 3%
where the time goes in v9:
time: 125 us; the launch traced here: 124 us
  starting transfers between devices  42.4 us (34%)
  blocking collectives  31.3 us (25%)
  waiting for transfers between devices  26.8 us (21%)
  Pallas kernels  20.7 us (17%)
  local copies, waits for them, and re-layouts  1.74 us (1%)
    all_to_all x2, blocking collectives, swap(): return lax.all_to_all(values, axes, split_axis=0, concat_axis=0, tiled=True)  31.3 us
    all_to_all x3, starting transfers between devices, swap(): return lax.all_to_all(values, axes, split_axis=0, concat_axis=0, tiled=True)  24.1 us
    pallas_call x9, Pallas kernels, call(): pl.pallas_call(kernel, out_shape=[(pltpu.HBM if isinstance(given, tuple)...  20.7 us
    all_to_all x3, waiting for transfers between devices, swap(): return lax.all_to_all(values, axes, split_axis=0, concat_axis=0, tiled=True)  17.8 us
    ppermute x1, starting transfers between devices, on_device(): left = lax.ppermute(to_right, 'lon', forward)  4.38 us
    ppermute x1, waiting for transfers between devices, on_device(): lax.ppermute(down, 'lat', forward)  4.13 us
    ppermute x1, starting transfers between devices, on_device(): above = lax.ppermute(both, 'lat', to_below)  3.58 us
    ppermute x1, starting transfers between devices, on_device(): lax.ppermute(down, 'lat', forward)  3.3 us
  transfers between devices with their start and end apart: 11, of which 7 were waited for; matrix products, arithmetic and copies ran while one was open for 1% of the time, Pallas kernels for 3%

profile of v9, /device:TPU:1, one launch (start us, length us, event | category | flops | bytes accessed | tf_op | source)
XLA Modules:
  0.0 123.9 jit_solution(16026293558410454316)
XLA Ops:
  0.7 2.4 %shard_map.85 = (f32[16,88,128]{2,1,0:T(8,128)S(1)}, bf16[5,88,128]{2,1,0:T(8,128)(2,1)S(1)}, bf16[5,88,128]{2,1,0:T(8,128)(2,1)S(1)}, f32[88,128]{1,0:T(8,128)S(1)}, f32[88,128]{1,0:T(8,128)S(1)}) custom-call(bf16[83,8,128]{2,1,0:T(8,128)(2,1)} %bitcast.25, bf16[83,8,128]{2,1,0:T(8,128)(2,1)} %bitcast.26, bf16[83,8,128]{2,1,0:T(8,128)(2,1)} %target_ref.1, ...), custom_call_target="tpu_custom_call" | custom-call | tf_op jit(solution)/shard_map/pallas_call | solution.py:54
  3.0 4.4 %collective-permute-start.2 = (f32[88,128]{1,0:T(8,128)S(1)}, f32[88,128]{1,0:T(8,128)S(1)}, u32[]{:S(2)}, u32[]{:S(2)}) collective-permute-start(f32[88,128]{1,0:T(8,128)S(1)} %get-tuple-element.27), channel_id=1, source_target_pairs={{0,1},{1,2},{2,3},{3,0},{4,5},{5,6},{6,7},{7,4},{8,9},{9,10},{10,1... | collective-permute-start | bytes 135176 | tf_op jit(solution)/shard_map/ppermute | solution.py:500
  7.4 3.1 %collective-permute-start = (bf16[5,88,128]{2,1,0:T(8,128)(2,1)S(1)}, bf16[5,88,128]{2,1,0:T(8,128)(2,1)S(1)}, u32[]{:S(2)}, u32[]{:S(2)}) collective-permute-start(bf16[5,88,128]{2,1,0:T(8,128)(2,1)S(1)} %get-tuple-element.25), channel_id=1, source_target_pairs={{0,4},{4,8},{8,12},{1,5},{5,9},{9,13},{2,6},{6,10},{10,14},{3,7},{... | collective-permute-start | bytes 337928 | tf_op jit(solution)/shard_map/ppermute | solution.py:496
  10.5 1.3 %collective-permute-start.1 = (bf16[5,88,128]{2,1,0:T(8,128)(2,1)S(1)}, bf16[5,88,128]{2,1,0:T(8,128)(2,1)S(1)}, u32[]{:S(2)}, u32[]{:S(2)}) collective-permute-start(bf16[5,88,128]{2,1,0:T(8,128)(2,1)S(1)} %get-tuple-element.26), channel_id=1, source_target_pairs={{4,0},{8,4},{12,8},{5,1},{9,5},{13,9},{6,2},{10,6},{14,10},{7,3},{... | collective-permute-start | bytes 337928 | tf_op jit(solution)/shard_map/ppermute | solution.py:497
  11.9 0.4 collective-permute-done.3.right_ref
  12.4 3.6 %collective-permute-start.4 = (f32[2,88,128]{2,1,0:T(8,128)S(1)}, f32[2,88,128]{2,1,0:T(8,128)S(1)}, u32[]{:S(2)}, u32[]{:S(2)}) collective-permute-start(f32[2,88,128]{2,1,0:T(8,128)S(1)} %shard_map.86), channel_id=1, source_target_pairs={{0,4},{4,8},{8,12},{1,5},{5,9},{9,13},{2,6},{6,10},{10,14},{3,7},{... | collective-permute-start | bytes 270344 | tf_op jit(solution)/shard_map/ppermute | solution.py:503
  16.0 1.3 %collective-permute-start.5 = (f32[2,88,128]{2,1,0:T(8,128)S(1)}, f32[2,88,128]{2,1,0:T(8,128)S(1)}, u32[]{:S(2)}, u32[]{:S(2)}) collective-permute-start(f32[2,88,128]{2,1,0:T(8,128)S(1)} %shard_map.86), channel_id=1, source_target_pairs={{4,0},{8,4},{12,8},{5,1},{9,5},{13,9},{6,2},{10,6},{14,10},{7,3},{... | collective-permute-start | bytes 270344 | tf_op jit(solution)/shard_map/ppermute | solution.py:504
  17.3 1.1 pad.15
  18.4 0.2 copy.11.w1_ref
  18.6 0.1 pad.16
  18.7 2.5 %collective-permute-done.5.below_ref = f32[2,88,128]{2,1,0:T(8,128)S(1)} collective-permute-done((f32[2,88,128]{2,1,0:T(8,128)S(1)}, f32[2,88,128]{2,1,0:T(8,128)S(1)}, u32[]{:S(2)}, u32[]{:S(2)}) %collective-permute-start.5) | collective-permute-done | bytes 90144 | tf_op jit(solution)/shard_map/ppermute | solution.py:504
  21.2 5.1 %shard_map.87 = (f32[1024,128]{1,0:T(8,128)S(1)}, f32[64,128]{1,0:T(8,128)S(1)}, f32[192,1152]{1,0:T(8,128)}, bf16[192,1152]{1,0:T(8,128)(2,1)}, bf16[864,1152]{1,0:T(8,128)(2,1)}, /*index=5*/f32[88,1152]{1,0:T(8,128)}) custom-call(s32[1]{0:T(128)} %bitcast.member_ref, f32[16,88,128]{2,1,0:T(8,128)S(1)} %get-tuple-element.24.own_ref, ...), custom_call_target="tpu_custom_call" | custom-call | tf_op jit(solution)/shard_map/pallas_call | solution.py:54
  26.4 19.7 %all_to_all.25.forecast_ref = f32[16,64,128]{2,1,0:T(8,128)S(1)} all-to-all(f32[16,64,128]{2,1,0:T(8,128)S(1)} %bitcast.18), channel_id=1, replica_groups=mesh['half'=2,'ring'=8,'lat'=4,'lon'=4] {'half','ring'}, dimensions={0} | all-to-all | bytes 1048576 | tf_op jit(solution)/shard_map/all_to_all | solution.py:467
  46.0 1.8 %shard_map.88 = bf16[16,64,128]{2,1,0:T(8,128)(2,1)} custom-call(f32[16,64,128]{2,1,0:T(8,128)S(1)} %all_to_all.25.forecast_ref, f32[64,128]{1,0:T(8,128)S(1)} %get-tuple-element.30.truth_ref), custom_call_target="tpu_custom_call" | custom-call | tf_op jit(solution)/shard_map/pallas_call | solution.py:54
  47.8 6.8 %all-to-all-start.1 = ((bf16[16,64,128]{2,1,0:T(8,128)(2,1)}), bf16[16,64,128]{2,1,0:T(8,128)(2,1)S(1)}, u32[]{:S(2)}, u32[]{:S(2)}) async-start(bf16[16,64,128]{2,1,0:T(8,128)(2,1)} %shard_map.88), calls=%async_computation.1 | async-start | bytes 524288 | tf_op jit(solution)/shard_map/all_to_all | solution.py:467
  54.7 0.1 pad.17
  54.8 0.2 copy.12.w2_ref
  55.0 7.6 %all-to-all-done.1.grad_ref = bf16[16,64,128]{2,1,0:T(8,128)(2,1)S(1)} async-done(((bf16[16,64,128]{2,1,0:T(8,128)(2,1)}), bf16[16,64,128]{2,1,0:T(8,128)(2,1)S(1)}, u32[]{:S(2)}, u32[]{:S(2)}) %all-to-all-start.1) | async-done | bytes 262176 | tf_op jit(solution)/shard_map/all_to_all | solution.py:467
  62.5 5.7 %shard_map.89 = (bf16[192,1152]{1,0:T(8,128)(2,1)}, f32[88,1152]{1,0:T(8,128)}, bf16[32,72,128]{2,1,0:T(8,128)(2,1)}, bf16[192,256]{1,0:T(8,128)(2,1)S(1)}, bf16[192,256]{1,0:T(8,128)(2,1)S(1)}) custom-call(bf16[16,64,128]{2,1,0:T(8,128)(2,1)S(1)} %all-to-all-done.1.grad_ref, f32[192,1152]{1,0:T(8,128)} %get-tuple-element.31.pre_far, ...), custom_call_target="tpu_custom_call" | custom-call | tf_op jit(solution)/shard_map/pallas_call | solution.py:54
  68.3 9.8 %all-to-all-start.2 = ((bf16[32,72,128]{2,1,0:T(8,128)(2,1)}), bf16[32,72,128]{2,1,0:T(8,128)(2,1)S(1)}, u32[]{:S(2)}, u32[]{:S(2)}) async-start(bf16[32,72,128]{2,1,0:T(8,128)(2,1)} %get-tuple-element.37), calls=%async_computation.2 | async-start | bytes 1179648 | tf_op jit(solution)/shard_map/all_to_all | solution.py:467
  78.1 3.3 %collective-permute-start.6 = (bf16[192,256]{1,0:T(8,128)(2,1)S(1)}, bf16[192,256]{1,0:T(8,128)(2,1)S(1)}, u32[]{:S(2)}, u32[]{:S(2)}) collective-permute-start(bf16[192,256]{1,0:T(8,128)(2,1)S(1)} %get-tuple-element.38), channel_id=1, source_target_pairs={{0,4},{4,8},{8,12},{1,5},{5,9},{9,13},{2,6},{6,10},{10,14},{3,7},{... | collective-permute-start | bytes 294920 | tf_op jit(solution)/shard_map/ppermute | solution.py:581
  81.4 1.3 %collective-permute-start.7 = (bf16[192,256]{1,0:T(8,128)(2,1)S(1)}, bf16[192,256]{1,0:T(8,128)(2,1)S(1)}, u32[]{:S(2)}, u32[]{:S(2)}) collective-permute-start(bf16[192,256]{1,0:T(8,128)(2,1)S(1)} %get-tuple-element.39), channel_id=1, source_target_pairs={{4,0},{8,4},{12,8},{5,1},{9,5},{13,9},{6,2},{10,6},{14,10},{7,3},{... | collective-permute-start | bytes 294920 | tf_op jit(solution)/shard_map/ppermute | solution.py:581
  82.7 4.1 %collective-permute-done.6.top_ref = bf16[192,256]{1,0:T(8,128)(2,1)S(1)} collective-permute-done((bf16[192,256]{1,0:T(8,128)(2,1)S(1)}, bf16[192,256]{1,0:T(8,128)(2,1)S(1)}, u32[]{:S(2)}, u32[]{:S(2)}) %collective-permute-start.6) | collective-permute-done | bytes 98336 | tf_op jit(solution)/shard_map/ppermute | solution.py:581
  86.8 1.9 %collective-permute-done.7.bottom_ref = bf16[192,256]{1,0:T(8,128)(2,1)S(1)} collective-permute-done((bf16[192,256]{1,0:T(8,128)(2,1)S(1)}, bf16[192,256]{1,0:T(8,128)(2,1)S(1)}, u32[]{:S(2)}, u32[]{:S(2)}) %collective-permute-start.7) | collective-permute-done | bytes 98336 | tf_op jit(solution)/shard_map/ppermute | solution.py:581
  88.8 1.5 %all-to-all-done.2.parts_ref = bf16[32,72,128]{2,1,0:T(8,128)(2,1)S(1)} async-done(((bf16[32,72,128]{2,1,0:T(8,128)(2,1)}), bf16[32,72,128]{2,1,0:T(8,128)(2,1)S(1)}, u32[]{:S(2)}, u32[]{:S(2)}) %all-to-all-start.2) | async-done | bytes 589856 | tf_op jit(solution)/shard_map/all_to_all | solution.py:467
  90.3 0.1 shard_map.91
  90.4 11.6 %all_to_all.26.parts_ref = bf16[8,72,128]{2,1,0:T(8,128)(2,1)S(1)} all-to-all(bf16[8,72,128]{2,1,0:T(8,128)(2,1)S(1)} %shard_map.91), channel_id=1, replica_groups=mesh['half'=2,'ring'=8,'lat'=4,'lon'=4] {'ring'}, dimensions={0} | all-to-all | bytes 294912 | tf_op jit(solution)/shard_map/all_to_all | solution.py:467
  102.0 0.9 shard_map.92
  102.9 7.4 %all-to-all-start.4 = ((bf16[32,72,128]{2,1,0:T(8,128)(2,1)}), bf16[32,72,128]{2,1,0:T(8,128)(2,1)S(1)}, u32[]{:S(2)}, u32[]{:S(2)}) async-start(bf16[32,72,128]{2,1,0:T(8,128)(2,1)} %shard_map.92), calls=%async_computation.4 | async-start | bytes 1179648 | tf_op jit(solution)/shard_map/all_to_all | solution.py:467
  110.4 3.4 %shard_map.90 = bf16[664,128]{1,0:T(8,128)(2,1)} custom-call(bf16[192,1152]{1,0:T(8,128)(2,1)} %get-tuple-element.34.grad_pre_far, f32[88,1152]{1,0:T(8,128)} %get-tuple-element.35.grad_far, f32[88,1152]{1,0:T(8,128)} %get-tuple-element.36.latent_far, f32[1,83]{1,0:T(1,128)S(1)} %bitcast.21, bf16[792,192]{1,0:T(8,128)(2,1)S(1)} %bitcast.17, ...), custom_call_target="tpu_custom_call" | custom-call | tf_op jit(solution)/shard_map/pallas_call | solution.py:54
  113.8 8.7 %all-to-all-done.4.parts_ref = bf16[32,72,128]{2,1,0:T(8,128)(2,1)S(1)} async-done(((bf16[32,72,128]{2,1,0:T(8,128)(2,1)}), bf16[32,72,128]{2,1,0:T(8,128)(2,1)S(1)}, u32[]{:S(2)}, u32[]{:S(2)}) %all-to-all-start.4) | async-done | bytes 589856 | tf_op jit(solution)/shard_map/all_to_all | solution.py:467
  122.5 1.4 %shard_map.93 = (f32[9,83,192]{2,1,0:T(8,128)}, f32[9,83,192]{2,1,0:T(8,128)}) custom-call(bf16[32,72,128]{2,1,0:T(8,128)(2,1)S(1)} %all-to-all-done.4.parts_ref), custom_call_target="tpu_custom_call" | custom-call | tf_op jit(solution)/shard_map/pallas_call | solution.py:54
  (17 shorter events, 0.2 us)
Async XLA Ops:
  0.6 20.6 %copy-start = (f32[83]{0:T(128)S(1)}, f32[83]{0:T(128)}, u32[]{:S(2)}) copy-start(f32[83]{0:T(128)} %param.9) | copy-start | bytes 1000
  0.6 18.0 %copy-start.1 = (bf16[9,83,192]{2,1,0:T(8,128)(2,1)S(1)}, bf16[9,83,192]{2,1,0:T(8,128)(2,1)}, u32[]{:S(2)}) copy-start(bf16[9,83,192]{2,1,0:T(8,128)(2,1)} %param.11) | copy-start | bytes 860548
  3.0 8.9 %collective-permute-start.2 = (f32[88,128]{1,0:T(8,128)S(1)}, f32[88,128]{1,0:T(8,128)S(1)}, u32[]{:S(2)}, u32[]{:S(2)}) collective-permute-start(f32[88,128]{1,0:T(8,128)S(1)} %get-tuple-element.27), channel_id=1, source_target_pairs={{0,1},{1,2},{2,3},{3,0},{4,5},{5,6},{6,7},{7,4},{8,9},{9,10},{10,1... | collective-permute-start | bytes 135176 | tf_op jit(solution)/shard_map/ppermute | solution.py:500
  7.4 5.0 %collective-permute-start.3 = (f32[88,128]{1,0:T(8,128)S(1)}, f32[88,128]{1,0:T(8,128)S(1)}, u32[]{:S(2)}, u32[]{:S(2)}) collective-permute-start(f32[88,128]{1,0:T(8,128)S(1)} %get-tuple-element.28), channel_id=1, source_target_pairs={{1,0},{2,1},{3,2},{0,3},{5,4},{6,5},{7,6},{4,7},{9,8},{10,9},{11,1... | collective-permute-start | bytes 135176 | tf_op jit(solution)/shard_map/ppermute | solution.py:501
  7.4 11.3 %collective-permute-start = (bf16[5,88,128]{2,1,0:T(8,128)(2,1)S(1)}, bf16[5,88,128]{2,1,0:T(8,128)(2,1)S(1)}, u32[]{:S(2)}, u32[]{:S(2)}) collective-permute-start(bf16[5,88,128]{2,1,0:T(8,128)(2,1)S(1)} %get-tuple-element.25), channel_id=1, source_target_pairs={{0,4},{4,8},{8,12},{1,5},{5,9},{9,13},{2,6},{6,10},{10,14},{3,7},{... | collective-permute-start | bytes 337928 | tf_op jit(solution)/shard_map/ppermute | solution.py:496
  10.5 8.2 %collective-permute-start.1 = (bf16[5,88,128]{2,1,0:T(8,128)(2,1)S(1)}, bf16[5,88,128]{2,1,0:T(8,128)(2,1)S(1)}, u32[]{:S(2)}, u32[]{:S(2)}) collective-permute-start(bf16[5,88,128]{2,1,0:T(8,128)(2,1)S(1)} %get-tuple-element.26), channel_id=1, source_target_pairs={{4,0},{8,4},{12,8},{5,1},{9,5},{13,9},{6,2},{10,6},{14,10},{7,3},{... | collective-permute-start | bytes 337928 | tf_op jit(solution)/shard_map/ppermute | solution.py:497
  12.4 6.3 %collective-permute-start.4 = (f32[2,88,128]{2,1,0:T(8,128)S(1)}, f32[2,88,128]{2,1,0:T(8,128)S(1)}, u32[]{:S(2)}, u32[]{:S(2)}) collective-permute-start(f32[2,88,128]{2,1,0:T(8,128)S(1)} %shard_map.86), channel_id=1, source_target_pairs={{0,4},{4,8},{8,12},{1,5},{5,9},{9,13},{2,6},{6,10},{10,14},{3,7},{... | collective-permute-start | bytes 270344 | tf_op jit(solution)/shard_map/ppermute | solution.py:503
  16.0 5.3 %collective-permute-start.5 = (f32[2,88,128]{2,1,0:T(8,128)S(1)}, f32[2,88,128]{2,1,0:T(8,128)S(1)}, u32[]{:S(2)}, u32[]{:S(2)}) collective-permute-start(f32[2,88,128]{2,1,0:T(8,128)S(1)} %shard_map.86), channel_id=1, source_target_pairs={{4,0},{8,4},{12,8},{5,1},{9,5},{13,9},{6,2},{10,6},{14,10},{7,3},{... | collective-permute-start | bytes 270344 | tf_op jit(solution)/shard_map/ppermute | solution.py:504
  47.8 14.7 %all-to-all-start.1 = ((bf16[16,64,128]{2,1,0:T(8,128)(2,1)}), bf16[16,64,128]{2,1,0:T(8,128)(2,1)S(1)}, u32[]{:S(2)}, u32[]{:S(2)}) async-start(bf16[16,64,128]{2,1,0:T(8,128)(2,1)} %shard_map.88), calls=%async_computation.1 | async-start | bytes 524288 | tf_op jit(solution)/shard_map/all_to_all | solution.py:467
  68.3 42.1 %copy-start.2 = (bf16[9,192,83]{1,2,0:T(8,128)(2,1)S(1)}, bf16[9,192,83]{1,2,0:T(8,128)(2,1)}, u32[]{:S(2)}) copy-start(bf16[9,192,83]{1,2,0:T(8,128)(2,1)} %param.10) | copy-start | bytes 860548
  68.3 22.0 %all-to-all-start.2 = ((bf16[32,72,128]{2,1,0:T(8,128)(2,1)}), bf16[32,72,128]{2,1,0:T(8,128)(2,1)S(1)}, u32[]{:S(2)}, u32[]{:S(2)}) async-start(bf16[32,72,128]{2,1,0:T(8,128)(2,1)} %get-tuple-element.37), calls=%async_computation.2 | async-start | bytes 1179648 | tf_op jit(solution)/shard_map/all_to_all | solution.py:467
  78.1 8.7 %collective-permute-start.6 = (bf16[192,256]{1,0:T(8,128)(2,1)S(1)}, bf16[192,256]{1,0:T(8,128)(2,1)S(1)}, u32[]{:S(2)}, u32[]{:S(2)}) collective-permute-start(bf16[192,256]{1,0:T(8,128)(2,1)S(1)} %get-tuple-element.38), channel_id=1, source_target_pairs={{0,4},{4,8},{8,12},{1,5},{5,9},{9,13},{2,6},{6,10},{10,14},{3,7},{... | collective-permute-start | bytes 294920 | tf_op jit(solution)/shard_map/ppermute | solution.py:581
  81.4 7.4 %collective-permute-start.7 = (bf16[192,256]{1,0:T(8,128)(2,1)S(1)}, bf16[192,256]{1,0:T(8,128)(2,1)S(1)}, u32[]{:S(2)}, u32[]{:S(2)}) collective-permute-start(bf16[192,256]{1,0:T(8,128)(2,1)S(1)} %get-tuple-element.39), channel_id=1, source_target_pairs={{4,0},{8,4},{12,8},{5,1},{9,5},{13,9},{6,2},{10,6},{14,10},{7,3},{... | collective-permute-start | bytes 294920 | tf_op jit(solution)/shard_map/ppermute | solution.py:581
  102.9 19.6 %all-to-all-start.4 = ((bf16[32,72,128]{2,1,0:T(8,128)(2,1)}), bf16[32,72,128]{2,1,0:T(8,128)(2,1)S(1)}, u32[]{:S(2)}, u32[]{:S(2)}) async-start(bf16[32,72,128]{2,1,0:T(8,128)(2,1)} %shard_map.92), calls=%async_computation.4 | async-start | bytes 1179648 | tf_op jit(solution)/shard_map/all_to_all | solution.py:467

commit v10 on v9

--- a/solution.py
+++ b/solution.py
@@ -577,12 +577,12 @@
     )
     parts = swap(weights, plane)
     forward, backward = neighbours("lat", False)
-    parts, top, bottom = lax.optimization_barrier(
-        (parts, lax.ppermute(down, "lat", forward), lax.ppermute(up, "lat", backward))
-    )
+    parts, top = lax.optimization_barrier((parts, lax.ppermute(down, "lat", forward)))
+    bottom = lax.ppermute(up, "lat", backward)
     piece = (PIECE, 128)
     (copies,) = call(total_kernel, 6, [((RING,) + piece, bf16)], [], parts)
-    (copies,) = call(total_kernel, 6, [((GROUPS,) + piece, bf16)], [], swap(copies, "ring"))
+    parts, bottom = lax.optimization_barrier((swap(copies, "ring"), bottom))
+    (copies,) = call(total_kernel, 6, [((GROUPS,) + piece, bf16)], [], parts)
     (states,) = call(
         states_kernel,
         16,

time: 125 us -> 125 us (level)
  blocking collectives: 31.3 us -> 19.7 us
  waiting for transfers between devices: 26.8 us -> 34.8 us
  starting transfers between devices: 42.4 us -> 45.9 us
    all_to_all x2 -> x1, blocking collectives: 31.3 us -> 19.7 us  [swap(): return lax.all_to_all(values, axes, split_axis=0, concat_axis=0, tiled=True)]
    ppermute x1 -> x2, waiting for transfers between devices: 0.01 us -> 4.36 us  [on_device(): bottom = lax.ppermute(up, 'lat', backward)]
    all_to_all x3 -> x4, waiting for transfers between devices: 17.8 us -> 22 us  [swap(): return lax.all_to_all(values, axes, split_axis=0, concat_axis=0, tiled=True)]
    all_to_all x3 -> x4, starting transfers between devices: 24.1 us -> 27.7 us  [swap(): return lax.all_to_all(values, axes, split_axis=0, concat_axis=0, tiled=True)]
    ppermute x1 -> x0, waiting for transfers between devices: 1.94 us -> none  [on_device(): lax.ppermute(up, 'lat', backward)]
    ppermute x1, waiting for transfers between devices: 4.13 us -> 5.43 us  [on_device(): lax.ppermute(down, 'lat', forward)]
    ppermute x1 -> x0, starting transfers between devices: 1.29 us -> none  [on_device(): lax.ppermute(up, 'lat', backward)]
    ppermute x1 -> x2, starting transfers between devices: 1.29 us -> 2.57 us  [on_device(): bottom = lax.ppermute(up, 'lat', backward)]
  transfers between devices with their start and end apart: 11 -> 12, of which waited for: 7 -> 8; matrix products, arithmetic and copies ran while one was open for 1% -> 1% of each run, Pallas kernels for 3% -> 3%
where the time goes in v10:
time: 125 us; the launch traced here: 124 us
  starting transfers between devices  45.9 us (37%)
  waiting for transfers between devices  34.8 us (28%)
  Pallas kernels  21.4 us (17%)
  blocking collectives  19.7 us (16%)
  local copies, waits for them, and re-layouts  1.74 us (1%)
    all_to_all x4, starting transfers between devices, swap(): return lax.all_to_all(values, axes, split_axis=0, concat_axis=0, tiled=True)  27.7 us
    all_to_all x4, waiting for transfers between devices, swap(): return lax.all_to_all(values, axes, split_axis=0, concat_axis=0, tiled=True)  22 us
    pallas_call x9, Pallas kernels, call(): pl.pallas_call(kernel, out_shape=[(pltpu.HBM if isinstance(given, tuple)...  21.4 us
    all_to_all x1, blocking collectives, swap(): return lax.all_to_all(values, axes, split_axis=0, concat_axis=0, tiled=True)  19.7 us
    ppermute x1, waiting for transfers between devices, on_device(): lax.ppermute(down, 'lat', forward)  5.43 us
    ppermute x1, starting transfers between devices, on_device(): left = lax.ppermute(to_right, 'lon', forward)  4.38 us
    ppermute x2, waiting for transfers between devices, on_device(): bottom = lax.ppermute(up, 'lat', backward)  4.36 us
    ppermute x1, starting transfers between devices, on_device(): above = lax.ppermute(both, 'lat', to_below)  3.58 us
  transfers between devices with their start and end apart: 12, of which 8 were waited for; matrix products, arithmetic and copies ran while one was open for 1% of the time, Pallas kernels for 3%

profile of v10, /device:TPU:1, one launch (start us, length us, event | category | flops | bytes accessed | tf_op | source)
XLA Modules:
  0.0 124.4 jit_solution(7779423007772801030)
XLA Ops:
  0.7 2.4 %shard_map.85 = (f32[16,88,128]{2,1,0:T(8,128)S(1)}, bf16[5,88,128]{2,1,0:T(8,128)(2,1)S(1)}, bf16[5,88,128]{2,1,0:T(8,128)(2,1)S(1)}, f32[88,128]{1,0:T(8,128)S(1)}, f32[88,128]{1,0:T(8,128)S(1)}) custom-call(bf16[83,8,128]{2,1,0:T(8,128)(2,1)} %bitcast.25, bf16[83,8,128]{2,1,0:T(8,128)(2,1)} %bitcast.26, bf16[83,8,128]{2,1,0:T(8,128)(2,1)} %target_ref.1, ...), custom_call_target="tpu_custom_call" | custom-call | tf_op jit(solution)/shard_map/pallas_call | solution.py:54
  3.0 4.4 %collective-permute-start.2 = (f32[88,128]{1,0:T(8,128)S(1)}, f32[88,128]{1,0:T(8,128)S(1)}, u32[]{:S(2)}, u32[]{:S(2)}) collective-permute-start(f32[88,128]{1,0:T(8,128)S(1)} %get-tuple-element.28), channel_id=1, source_target_pairs={{0,1},{1,2},{2,3},{3,0},{4,5},{5,6},{6,7},{7,4},{8,9},{9,10},{10,1... | collective-permute-start | bytes 135176 | tf_op jit(solution)/shard_map/ppermute | solution.py:500
  7.4 3.1 %collective-permute-start = (bf16[5,88,128]{2,1,0:T(8,128)(2,1)S(1)}, bf16[5,88,128]{2,1,0:T(8,128)(2,1)S(1)}, u32[]{:S(2)}, u32[]{:S(2)}) collective-permute-start(bf16[5,88,128]{2,1,0:T(8,128)(2,1)S(1)} %get-tuple-element.26), channel_id=1, source_target_pairs={{0,4},{4,8},{8,12},{1,5},{5,9},{9,13},{2,6},{6,10},{10,14},{3,7},{... | collective-permute-start | bytes 337928 | tf_op jit(solution)/shard_map/ppermute | solution.py:496
  10.5 1.3 %collective-permute-start.1 = (bf16[5,88,128]{2,1,0:T(8,128)(2,1)S(1)}, bf16[5,88,128]{2,1,0:T(8,128)(2,1)S(1)}, u32[]{:S(2)}, u32[]{:S(2)}) collective-permute-start(bf16[5,88,128]{2,1,0:T(8,128)(2,1)S(1)} %get-tuple-element.27), channel_id=1, source_target_pairs={{4,0},{8,4},{12,8},{5,1},{9,5},{13,9},{6,2},{10,6},{14,10},{7,3},{... | collective-permute-start | bytes 337928 | tf_op jit(solution)/shard_map/ppermute | solution.py:497
  11.9 0.4 collective-permute-done.3.right_ref
  12.4 3.6 %collective-permute-start.4 = (f32[2,88,128]{2,1,0:T(8,128)S(1)}, f32[2,88,128]{2,1,0:T(8,128)S(1)}, u32[]{:S(2)}, u32[]{:S(2)}) collective-permute-start(f32[2,88,128]{2,1,0:T(8,128)S(1)} %shard_map.86), channel_id=1, source_target_pairs={{0,4},{4,8},{8,12},{1,5},{5,9},{9,13},{2,6},{6,10},{10,14},{3,7},{... | collective-permute-start | bytes 270344 | tf_op jit(solution)/shard_map/ppermute | solution.py:503
  16.0 1.3 %collective-permute-start.5 = (f32[2,88,128]{2,1,0:T(8,128)S(1)}, f32[2,88,128]{2,1,0:T(8,128)S(1)}, u32[]{:S(2)}, u32[]{:S(2)}) collective-permute-start(f32[2,88,128]{2,1,0:T(8,128)S(1)} %shard_map.86), channel_id=1, source_target_pairs={{4,0},{8,4},{12,8},{5,1},{9,5},{13,9},{6,2},{10,6},{14,10},{7,3},{... | collective-permute-start | bytes 270344 | tf_op jit(solution)/shard_map/ppermute | solution.py:504
  17.3 1.1 pad.15
  18.4 0.2 copy.11.w1_ref
  18.7 2.5 %collective-permute-done.5.below_ref = f32[2,88,128]{2,1,0:T(8,128)S(1)} collective-permute-done((f32[2,88,128]{2,1,0:T(8,128)S(1)}, f32[2,88,128]{2,1,0:T(8,128)S(1)}, u32[]{:S(2)}, u32[]{:S(2)}) %collective-permute-start.5) | collective-permute-done | bytes 90144 | tf_op jit(solution)/shard_map/ppermute | solution.py:504
  21.2 5.1 %shard_map.87 = (f32[1024,128]{1,0:T(8,128)S(1)}, f32[64,128]{1,0:T(8,128)S(1)}, f32[192,1152]{1,0:T(8,128)}, bf16[192,1152]{1,0:T(8,128)(2,1)}, bf16[864,1152]{1,0:T(8,128)(2,1)}, /*index=5*/f32[88,1152]{1,0:T(8,128)}) custom-call(s32[1]{0:T(128)} %bitcast.member_ref, f32[16,88,128]{2,1,0:T(8,128)S(1)} %get-tuple-element.25.own_ref, ...), custom_call_target="tpu_custom_call" | custom-call | tf_op jit(solution)/shard_map/pallas_call | solution.py:54
  26.4 19.7 %all_to_all.25.forecast_ref = f32[16,64,128]{2,1,0:T(8,128)S(1)} all-to-all(f32[16,64,128]{2,1,0:T(8,128)S(1)} %bitcast.18), channel_id=1, replica_groups=mesh['half'=2,'ring'=8,'lat'=4,'lon'=4] {'half','ring'}, dimensions={0} | all-to-all | bytes 1048576 | tf_op jit(solution)/shard_map/all_to_all | solution.py:467
  46.0 1.8 %shard_map.88 = bf16[16,64,128]{2,1,0:T(8,128)(2,1)} custom-call(f32[16,64,128]{2,1,0:T(8,128)S(1)} %all_to_all.25.forecast_ref, f32[64,128]{1,0:T(8,128)S(1)} %get-tuple-element.31.truth_ref), custom_call_target="tpu_custom_call" | custom-call | tf_op jit(solution)/shard_map/pallas_call | solution.py:54
  47.8 6.8 %all-to-all-start.1 = ((bf16[16,64,128]{2,1,0:T(8,128)(2,1)}), bf16[16,64,128]{2,1,0:T(8,128)(2,1)S(1)}, u32[]{:S(2)}, u32[]{:S(2)}) async-start(bf16[16,64,128]{2,1,0:T(8,128)(2,1)} %shard_map.88), calls=%async_computation.1 | async-start | bytes 524288 | tf_op jit(solution)/shard_map/all_to_all | solution.py:467
  54.7 0.1 pad.17
  54.8 0.2 copy.12.w2_ref
  55.0 7.6 %all-to-all-done.1.grad_ref = bf16[16,64,128]{2,1,0:T(8,128)(2,1)S(1)} async-done(((bf16[16,64,128]{2,1,0:T(8,128)(2,1)}), bf16[16,64,128]{2,1,0:T(8,128)(2,1)S(1)}, u32[]{:S(2)}, u32[]{:S(2)}) %all-to-all-start.1) | async-done | bytes 262176 | tf_op jit(solution)/shard_map/all_to_all | solution.py:467
  62.5 5.7 %shard_map.89 = (bf16[192,1152]{1,0:T(8,128)(2,1)}, f32[88,1152]{1,0:T(8,128)}, bf16[32,72,128]{2,1,0:T(8,128)(2,1)}, bf16[192,256]{1,0:T(8,128)(2,1)S(1)}, bf16[192,256]{1,0:T(8,128)(2,1)S(1)}) custom-call(bf16[16,64,128]{2,1,0:T(8,128)(2,1)S(1)} %all-to-all-done.1.grad_ref, f32[192,1152]{1,0:T(8,128)} %get-tuple-element.32.pre_far, ...), custom_call_target="tpu_custom_call" | custom-call | tf_op jit(solution)/shard_map/pallas_call | solution.py:54
  68.3 9.8 %all-to-all-start.2 = ((bf16[32,72,128]{2,1,0:T(8,128)(2,1)}), bf16[32,72,128]{2,1,0:T(8,128)(2,1)S(1)}, u32[]{:S(2)}, u32[]{:S(2)}) async-start(bf16[32,72,128]{2,1,0:T(8,128)(2,1)} %get-tuple-element.38), calls=%async_computation.2 | async-start | bytes 1179648 | tf_op jit(solution)/shard_map/all_to_all | solution.py:467
  78.1 3.3 %collective-permute-start.6 = (bf16[192,256]{1,0:T(8,128)(2,1)S(1)}, bf16[192,256]{1,0:T(8,128)(2,1)S(1)}, u32[]{:S(2)}, u32[]{:S(2)}) collective-permute-start(bf16[192,256]{1,0:T(8,128)(2,1)S(1)} %get-tuple-element.39), channel_id=1, source_target_pairs={{0,4},{4,8},{8,12},{1,5},{5,9},{9,13},{2,6},{6,10},{10,14},{3,7},{... | collective-permute-start | bytes 294920 | tf_op jit(solution)/shard_map/ppermute | solution.py:580
  81.4 5.4 %collective-permute-done.6.top_ref = bf16[192,256]{1,0:T(8,128)(2,1)S(1)} collective-permute-done((bf16[192,256]{1,0:T(8,128)(2,1)S(1)}, bf16[192,256]{1,0:T(8,128)(2,1)S(1)}, u32[]{:S(2)}, u32[]{:S(2)}) %collective-permute-start.6) | collective-permute-done | bytes 98336 | tf_op jit(solution)/shard_map/ppermute | solution.py:580
  86.8 3.5 %all-to-all-done.2.parts_ref = bf16[32,72,128]{2,1,0:T(8,128)(2,1)S(1)} async-done(((bf16[32,72,128]{2,1,0:T(8,128)(2,1)}), bf16[32,72,128]{2,1,0:T(8,128)(2,1)S(1)}, u32[]{:S(2)}, u32[]{:S(2)}) %all-to-all-start.2) | async-done | bytes 589856 | tf_op jit(solution)/shard_map/all_to_all | solution.py:467
  90.3 0.8 shard_map.90
  91.1 3.9 %all-to-all-start.3 = ((bf16[8,72,128]{2,1,0:T(8,128)(2,1)}), bf16[8,72,128]{2,1,0:T(8,128)(2,1)S(1)}, u32[]{:S(2)}, u32[]{:S(2)}) async-start(bf16[8,72,128]{2,1,0:T(8,128)(2,1)} %shard_map.90), calls=%async_computation.3 | async-start | bytes 294912 | tf_op jit(solution)/shard_map/all_to_all | solution.py:467
  94.9 1.3 %collective-permute-start.7 = (bf16[192,256]{1,0:T(8,128)(2,1)S(1)}, bf16[192,256]{1,0:T(8,128)(2,1)S(1)}, u32[]{:S(2)}, u32[]{:S(2)}) collective-permute-start(bf16[192,256]{1,0:T(8,128)(2,1)S(1)} %get-tuple-element.42), channel_id=1, source_target_pairs={{4,0},{8,4},{12,8},{5,1},{9,5},{13,9},{6,2},{10,6},{14,10},{7,3},{... | collective-permute-start | bytes 294920 | tf_op jit(solution)/shard_map/ppermute | solution.py:581
  96.2 4.4 %collective-permute-done.7.bottom_ref = bf16[192,256]{1,0:T(8,128)(2,1)S(1)} collective-permute-done((bf16[192,256]{1,0:T(8,128)(2,1)S(1)}, bf16[192,256]{1,0:T(8,128)(2,1)S(1)}, u32[]{:S(2)}, u32[]{:S(2)}) %collective-permute-start.7) | collective-permute-done | bytes 98336 | tf_op jit(solution)/shard_map/ppermute | solution.py:581
  100.6 2.3 %all-to-all-done.3.parts_ref = bf16[8,72,128]{2,1,0:T(8,128)(2,1)S(1)} async-done(((bf16[8,72,128]{2,1,0:T(8,128)(2,1)}), bf16[8,72,128]{2,1,0:T(8,128)(2,1)S(1)}, u32[]{:S(2)}, u32[]{:S(2)}) %all-to-all-start.3) | async-done | bytes 147488 | tf_op jit(solution)/shard_map/all_to_all | solution.py:467
  102.9 0.9 shard_map.92
  103.7 7.1 %all-to-all-start.4 = ((bf16[32,72,128]{2,1,0:T(8,128)(2,1)}), bf16[32,72,128]{2,1,0:T(8,128)(2,1)S(1)}, u32[]{:S(2)}, u32[]{:S(2)}) async-start(bf16[32,72,128]{2,1,0:T(8,128)(2,1)} %shard_map.92), calls=%async_computation.4 | async-start | bytes 1179648 | tf_op jit(solution)/shard_map/all_to_all | solution.py:467
  111.0 3.4 %shard_map.91 = bf16[664,128]{1,0:T(8,128)(2,1)} custom-call(bf16[192,1152]{1,0:T(8,128)(2,1)} %get-tuple-element.35.grad_pre_far, f32[88,1152]{1,0:T(8,128)} %get-tuple-element.36.grad_far, f32[88,1152]{1,0:T(8,128)} %get-tuple-element.37.latent_far, f32[1,83]{1,0:T(1,128)S(1)} %bitcast.21, bf16[792,192]{1,0:T(8,128)(2,1)S(1)} %bitcast.17, ...), custom_call_target="tpu_custom_call" | custom-call | tf_op jit(solution)/shard_map/pallas_call | solution.py:54
  114.4 8.7 %all-to-all-done.4.parts_ref = bf16[32,72,128]{2,1,0:T(8,128)(2,1)S(1)} async-done(((bf16[32,72,128]{2,1,0:T(8,128)(2,1)}), bf16[32,72,128]{2,1,0:T(8,128)(2,1)S(1)}, u32[]{:S(2)}, u32[]{:S(2)}) %all-to-all-start.4) | async-done | bytes 589856 | tf_op jit(solution)/shard_map/all_to_all | solution.py:467
  123.1 1.4 %shard_map.93 = (f32[9,83,192]{2,1,0:T(8,128)}, f32[9,83,192]{2,1,0:T(8,128)}) custom-call(bf16[32,72,128]{2,1,0:T(8,128)(2,1)S(1)} %all-to-all-done.4.parts_ref), custom_call_target="tpu_custom_call" | custom-call | tf_op jit(solution)/shard_map/pallas_call | solution.py:54
  (18 shorter events, 0.3 us)
Async XLA Ops:
  0.6 20.6 %copy-start = (f32[83]{0:T(128)S(1)}, f32[83]{0:T(128)}, u32[]{:S(2)}) copy-start(f32[83]{0:T(128)} %param.9) | copy-start | bytes 1000
  0.6 18.0 %copy-start.1 = (bf16[9,83,192]{2,1,0:T(8,128)(2,1)S(1)}, bf16[9,83,192]{2,1,0:T(8,128)(2,1)}, u32[]{:S(2)}) copy-start(bf16[9,83,192]{2,1,0:T(8,128)(2,1)} %param.11) | copy-start | bytes 860548
  3.0 8.9 %collective-permute-start.2 = (f32[88,128]{1,0:T(8,128)S(1)}, f32[88,128]{1,0:T(8,128)S(1)}, u32[]{:S(2)}, u32[]{:S(2)}) collective-permute-start(f32[88,128]{1,0:T(8,128)S(1)} %get-tuple-element.28), channel_id=1, source_target_pairs={{0,1},{1,2},{2,3},{3,0},{4,5},{5,6},{6,7},{7,4},{8,9},{9,10},{10,1... | collective-permute-start | bytes 135176 | tf_op jit(solution)/shard_map/ppermute | solution.py:500
  7.4 5.0 %collective-permute-start.3 = (f32[88,128]{1,0:T(8,128)S(1)}, f32[88,128]{1,0:T(8,128)S(1)}, u32[]{:S(2)}, u32[]{:S(2)}) collective-permute-start(f32[88,128]{1,0:T(8,128)S(1)} %get-tuple-element.29), channel_id=1, source_target_pairs={{1,0},{2,1},{3,2},{0,3},{5,4},{6,5},{7,6},{4,7},{9,8},{10,9},{11,1... | collective-permute-start | bytes 135176 | tf_op jit(solution)/shard_map/ppermute | solution.py:501
  7.4 11.3 %collective-permute-start = (bf16[5,88,128]{2,1,0:T(8,128)(2,1)S(1)}, bf16[5,88,128]{2,1,0:T(8,128)(2,1)S(1)}, u32[]{:S(2)}, u32[]{:S(2)}) collective-permute-start(bf16[5,88,128]{2,1,0:T(8,128)(2,1)S(1)} %get-tuple-element.26), channel_id=1, source_target_pairs={{0,4},{4,8},{8,12},{1,5},{5,9},{9,13},{2,6},{6,10},{10,14},{3,7},{... | collective-permute-start | bytes 337928 | tf_op jit(solution)/shard_map/ppermute | solution.py:496
  10.5 8.2 %collective-permute-start.1 = (bf16[5,88,128]{2,1,0:T(8,128)(2,1)S(1)}, bf16[5,88,128]{2,1,0:T(8,128)(2,1)S(1)}, u32[]{:S(2)}, u32[]{:S(2)}) collective-permute-start(bf16[5,88,128]{2,1,0:T(8,128)(2,1)S(1)} %get-tuple-element.27), channel_id=1, source_target_pairs={{4,0},{8,4},{12,8},{5,1},{9,5},{13,9},{6,2},{10,6},{14,10},{7,3},{... | collective-permute-start | bytes 337928 | tf_op jit(solution)/shard_map/ppermute | solution.py:497
  12.4 6.3 %collective-permute-start.4 = (f32[2,88,128]{2,1,0:T(8,128)S(1)}, f32[2,88,128]{2,1,0:T(8,128)S(1)}, u32[]{:S(2)}, u32[]{:S(2)}) collective-permute-start(f32[2,88,128]{2,1,0:T(8,128)S(1)} %shard_map.86), channel_id=1, source_target_pairs={{0,4},{4,8},{8,12},{1,5},{5,9},{9,13},{2,6},{6,10},{10,14},{3,7},{... | collective-permute-start | bytes 270344 | tf_op jit(solution)/shard_map/ppermute | solution.py:503
  16.0 5.3 %collective-permute-start.5 = (f32[2,88,128]{2,1,0:T(8,128)S(1)}, f32[2,88,128]{2,1,0:T(8,128)S(1)}, u32[]{:S(2)}, u32[]{:S(2)}) collective-permute-start(f32[2,88,128]{2,1,0:T(8,128)S(1)} %shard_map.86), channel_id=1, source_target_pairs={{4,0},{8,4},{12,8},{5,1},{9,5},{13,9},{6,2},{10,6},{14,10},{7,3},{... | collective-permute-start | bytes 270344 | tf_op jit(solution)/shard_map/ppermute | solution.py:504
  47.8 14.7 %all-to-all-start.1 = ((bf16[16,64,128]{2,1,0:T(8,128)(2,1)}), bf16[16,64,128]{2,1,0:T(8,128)(2,1)S(1)}, u32[]{:S(2)}, u32[]{:S(2)}) async-start(bf16[16,64,128]{2,1,0:T(8,128)(2,1)} %shard_map.88), calls=%async_computation.1 | async-start | bytes 524288 | tf_op jit(solution)/shard_map/all_to_all | solution.py:467
  68.3 42.6 %copy-start.2 = (bf16[9,192,83]{1,2,0:T(8,128)(2,1)S(1)}, bf16[9,192,83]{1,2,0:T(8,128)(2,1)}, u32[]{:S(2)}) copy-start(bf16[9,192,83]{1,2,0:T(8,128)(2,1)} %param.10) | copy-start | bytes 860548
  68.3 22.0 %all-to-all-start.2 = ((bf16[32,72,128]{2,1,0:T(8,128)(2,1)}), bf16[32,72,128]{2,1,0:T(8,128)(2,1)S(1)}, u32[]{:S(2)}, u32[]{:S(2)}) async-start(bf16[32,72,128]{2,1,0:T(8,128)(2,1)} %get-tuple-element.38), calls=%async_computation.2 | async-start | bytes 1179648 | tf_op jit(solution)/shard_map/all_to_all | solution.py:467
  78.1 8.7 %collective-permute-start.6 = (bf16[192,256]{1,0:T(8,128)(2,1)S(1)}, bf16[192,256]{1,0:T(8,128)(2,1)S(1)}, u32[]{:S(2)}, u32[]{:S(2)}) collective-permute-start(bf16[192,256]{1,0:T(8,128)(2,1)S(1)} %get-tuple-element.39), channel_id=1, source_target_pairs={{0,4},{4,8},{8,12},{1,5},{5,9},{9,13},{2,6},{6,10},{10,14},{3,7},{... | collective-permute-start | bytes 294920 | tf_op jit(solution)/shard_map/ppermute | solution.py:580
  91.1 11.8 %all-to-all-start.3 = ((bf16[8,72,128]{2,1,0:T(8,128)(2,1)}), bf16[8,72,128]{2,1,0:T(8,128)(2,1)S(1)}, u32[]{:S(2)}, u32[]{:S(2)}) async-start(bf16[8,72,128]{2,1,0:T(8,128)(2,1)} %shard_map.90), calls=%async_computation.3 | async-start | bytes 294912 | tf_op jit(solution)/shard_map/all_to_all | solution.py:467
  94.9 5.6 %collective-permute-start.7 = (bf16[192,256]{1,0:T(8,128)(2,1)S(1)}, bf16[192,256]{1,0:T(8,128)(2,1)S(1)}, u32[]{:S(2)}, u32[]{:S(2)}) collective-permute-start(bf16[192,256]{1,0:T(8,128)(2,1)S(1)} %get-tuple-element.42), channel_id=1, source_target_pairs={{4,0},{8,4},{12,8},{5,1},{9,5},{13,9},{6,2},{10,6},{14,10},{7,3},{... | collective-permute-start | bytes 294920 | tf_op jit(solution)/shard_map/ppermute | solution.py:581
  103.7 19.3 %all-to-all-start.4 = ((bf16[32,72,128]{2,1,0:T(8,128)(2,1)}), bf16[32,72,128]{2,1,0:T(8,128)(2,1)S(1)}, u32[]{:S(2)}, u32[]{:S(2)}) async-start(bf16[32,72,128]{2,1,0:T(8,128)(2,1)} %shard_map.92), calls=%async_computation.4 | async-start | bytes 1179648 | tf_op jit(solution)/shard_map/all_to_all | solution.py:467

commit v11 on v9

--- a/solution.py
+++ b/solution.py
@@ -188,9 +188,9 @@
 
 
 def forward_kernel(
-    member_ref, own_ref, top_ref, bottom_ref, left_ref, right_ref, above_ref, below_ref, gain_ref, valid_ref, mine_ref, w1_ref, w2_ref,
-    forecast_ref, truth_ref, pre_ref, hidden_ref, window_ref, latent_ref,
-    latent, normed, window, hidden, partial, truth, pre_kept, hidden_kept, semaphores,
+    own_ref, top_ref, bottom_ref, left_ref, right_ref, above_ref, below_ref, gain_ref, valid_ref, mine_ref, w1_ref, w2_ref,
+    forecast_ref, pre_ref, hidden_ref, window_ref, latent_ref,
+    latent, normed, window, hidden, partial, pre_kept, hidden_kept, semaphores,
 ):
     gain = gain_column(gain_ref)
 
@@ -213,19 +213,13 @@
             scaled_sides[id(ref), which] = centered * scale * gain
         return scaled_sides[id(ref), which]
 
-    pieces, truths = [], []
+    pieces = []
     for row in range(TALL):
         ref, place = side_of(row, RIM, ROWS)
         far = row < FAR or row >= TALL - FAR
         pieces.append((functools.partial(latent_row, own_ref, top_ref, bottom_ref, row), 0, PITCH * row + SIDE, COLS))
         for which, flat in ((0, PITCH * row), (1, PITCH * row + SIDE + COLS)):
             pieces.append((functools.partial(side, ref, which, far), SIDE * place, flat, SIDE))
-    for row in range(ROWS + 2 * NEAR):
-        ref, place = side_of(row, NEAR, ROWS)
-        flat, lane = PITCH * (row + FAR) + SIDE, SIDE * TALL + BESIDE * place
-        truths.append((functools.partial(truth_row, own_ref, top_ref, bottom_ref, row), 0, flat, COLS))
-        truths.append((functools.partial(side, ref, 0, False), lane, flat - BESIDE, BESIDE))
-        truths.append((functools.partial(side, ref, 1, False), lane, flat + COLS, BESIDE))
     lane = lanes_of(CP)
     inner_low, inner_high = PITCH * FAR, PITCH * (TALL - FAR)
     normed[CP:CI, :] = jnp.zeros((CI - CP, FLAT), f32)
@@ -242,11 +236,7 @@
         normed[0:CP, tile(index)] = values * valid_ref[:, tile(index)]
     own = pl.ds(128 * OWN[0], 128 * (OWN[1] - OWN[0]))
     moves = started((latent.at[:, own], latent_ref), semaphores=semaphores)
-    for index, values in flat_tiles(truths, *SPREAD):
-        truth[pl.ds(CP * (index - SPREAD[0]), CP), :] = values
     filled = CP * (SPREAD[1] - SPREAD[0])
-    truth[filled:, :] = jnp.zeros((MEMBERS * CHUNK - filled, 128), f32)
-    truth_ref[...] = truth[pl.ds(pl.multiple_of(member_ref[0] * CHUNK, 8), CHUNK), :]
 
     for group in range(CI // 16):
         values = normed[16 * group : 16 * group + 16, :]
@@ -287,6 +277,27 @@
     forecast_ref[filled:, :] = jnp.zeros((MEMBERS * CHUNK - filled, 128), f32)
     for move in moves:
         move.wait()
+
+
+def truth_kernel(
+    member_ref, own_ref, top_ref, bottom_ref, left_ref, right_ref, above_ref, below_ref, truth_ref, truth,
+):
+    pieces = []
+    for row in range(ROWS + 2 * NEAR):
+        sides, place = (left_ref, right_ref), row
+        if row < NEAR:
+            sides, place = (above_ref.at[0], above_ref.at[1]), row + ROWS
+        elif row >= NEAR + ROWS:
+            sides, place = (below_ref.at[0], below_ref.at[1]), row - ROWS
+        flat, lane = PITCH * (row + FAR) + SIDE, SIDE * TALL + BESIDE * place
+        pieces.append((functools.partial(truth_row, own_ref, top_ref, bottom_ref, row), 0, flat, COLS))
+        for ref, flat_side in zip(sides, (flat - BESIDE, flat + COLS)):
+            pieces.append((functools.partial(lambda ref: ref[...], ref), lane, flat_side, BESIDE))
+    for index, values in flat_tiles(pieces, *SPREAD):
+        truth[pl.ds(CP * (index - SPREAD[0]), CP), :] = values
+    filled = CP * (SPREAD[1] - SPREAD[0])
+    truth[filled:, :] = jnp.zeros((MEMBERS * CHUNK - filled, 128), f32)
+    truth_ref[...] = truth[pl.ds(pl.multiple_of(member_ref[0] * CHUNK, 8), CHUNK), :]
 
 
 def soft_slope(values):
@@ -519,12 +530,11 @@
     member = lax.axis_index(member_axes).astype(jnp.int32)[None]
     own_lanes = OWN_LANES
     spread_lanes = 128 * (SPREAD[1] - SPREAD[0])
-    forecast, truth, pre, hidden, window, latent = call(
+    forecast, pre, hidden, window, latent = call(
         forward_kernel,
         26,
         [
             ((MEMBERS * CHUNK, 128), f32),
-            ((CHUNK, 128), f32),
             ((HID, own_lanes), (f32,)),
             ((HID, own_lanes), (bf16,)),
             ((9 * CI, own_lanes), (bf16,)),
@@ -536,12 +546,19 @@
             ((9 * CI, FLAT), bf16),
             ((HID, FLAT), bf16),
             ((9 * CP, FLAT), f32),
-            ((MEMBERS * CHUNK, 128), f32),
             ((HID, own_lanes), f32),
             ((HID, own_lanes), bf16),
         ],
-        member, own, top, bottom, left, right, above, below, gain, valid, mine, w1_stack, w2_stack,
-        smem=1, close=(1, 2, 3, 4, 5, 6, 7), copies=7,
+        own, top, bottom, left, right, above, below, gain, valid, mine, w1_stack, w2_stack,
+        close=(0, 1, 2, 3, 4, 5, 6), copies=7,
+    )
+    (truth,) = call(
+        truth_kernel,
+        8,
+        [((CHUNK, 128), f32)],
+        [((MEMBERS * CHUNK, 128), f32)],
+        member, own, top, bottom, left, right, above, below,
+        smem=1,
     )
     spread = swap(forecast.reshape(MEMBERS, CHUNK, 128), member_axes)
     (grads,) = call(

time: 125 us -> 125 us (level)
  blocking collectives: 31.3 us -> 11.6 us
  waiting for transfers between devices: 26.8 us -> 37.8 us
  starting transfers between devices: 42.4 us -> 50.8 us
    all_to_all x2 -> x1, blocking collectives: 31.3 us -> 11.6 us  [swap(): return lax.all_to_all(values, axes, split_axis=0, concat_axis=0, tiled=True)]
    all_to_all x3 -> x4, waiting for transfers between devices: 17.8 us -> 28.8 us  [swap(): return lax.all_to_all(values, axes, split_axis=0, concat_axis=0, tiled=True)]
    all_to_all x3 -> x4, starting transfers between devices: 24.1 us -> 32.5 us  [swap(): return lax.all_to_all(values, axes, split_axis=0, concat_axis=0, tiled=True)]
    pallas_call x9 -> x10, Pallas kernels: 20.7 us -> 21.6 us  [call(): pl.pallas_call(kernel, out_shape=[(pltpu.HBM if isinstance(given, tuple)...]
  transfers between devices with their start and end apart: 11 -> 12, of which waited for: 7 -> 8; matrix products, arithmetic and copies ran while one was open for 1% -> 1% of each run, Pallas kernels for 3% -> 3%
where the time goes in v11:
time: 125 us
  starting transfers between devices  50.8 us (41%)
  waiting for transfers between devices  37.8 us (30%)
  Pallas kernels  21.6 us (17%)
  blocking collectives  11.6 us (9%)
  local copies, waits for them, and re-layouts  1.74 us (1%)
    all_to_all x4, starting transfers between devices, swap(): return lax.all_to_all(values, axes, split_axis=0, concat_axis=0, tiled=True)  32.5 us
    all_to_all x4, waiting for transfers between devices, swap(): return lax.all_to_all(values, axes, split_axis=0, concat_axis=0, tiled=True)  28.8 us
    pallas_call x10, Pallas kernels, call(): pl.pallas_call(kernel, out_shape=[(pltpu.HBM if isinstance(given, tuple)...  21.6 us
    all_to_all x1, blocking collectives, swap(): return lax.all_to_all(values, axes, split_axis=0, concat_axis=0, tiled=True)  11.6 us
    ppermute x1, starting transfers between devices, on_device(): left = lax.ppermute(to_right, 'lon', forward)  4.38 us
    ppermute x1, waiting for transfers between devices, on_device(): lax.ppermute(down, 'lat', forward)  4.13 us
    ppermute x1, starting transfers between devices, on_device(): above = lax.ppermute(both, 'lat', to_below)  3.58 us
    ppermute x1, starting transfers between devices, on_device(): lax.ppermute(down, 'lat', forward)  3.3 us
  transfers between devices with their start and end apart: 12, of which 8 were waited for; matrix products, arithmetic and copies ran while one was open for 1% of the time, Pallas kernels for 3%

profile of v11, /device:TPU:1, one launch (start us, length us, event | category | flops | bytes accessed | tf_op | source)
XLA Modules:
  0.0 124.6 jit_solution(12997510076825329891)
XLA Ops:
  0.7 2.4 %shard_map.85 = (f32[16,88,128]{2,1,0:T(8,128)S(1)}, bf16[5,88,128]{2,1,0:T(8,128)(2,1)S(1)}, bf16[5,88,128]{2,1,0:T(8,128)(2,1)S(1)}, f32[88,128]{1,0:T(8,128)S(1)}, f32[88,128]{1,0:T(8,128)S(1)}) custom-call(bf16[83,8,128]{2,1,0:T(8,128)(2,1)} %bitcast.24, bf16[83,8,128]{2,1,0:T(8,128)(2,1)} %bitcast.25, bf16[83,8,128]{2,1,0:T(8,128)(2,1)} %target_ref.1, ...), custom_call_target="tpu_custom_call" | custom-call | tf_op jit(solution)/shard_map/pallas_call | solution.py:54
  3.0 4.4 %collective-permute-start.2 = (f32[88,128]{1,0:T(8,128)S(1)}, f32[88,128]{1,0:T(8,128)S(1)}, u32[]{:S(2)}, u32[]{:S(2)}) collective-permute-start(f32[88,128]{1,0:T(8,128)S(1)} %get-tuple-element.26), channel_id=1, source_target_pairs={{0,1},{1,2},{2,3},{3,0},{4,5},{5,6},{6,7},{7,4},{8,9},{9,10},{10,1... | collective-permute-start | bytes 135176 | tf_op jit(solution)/shard_map/ppermute | solution.py:511
  7.4 3.1 %collective-permute-start = (bf16[5,88,128]{2,1,0:T(8,128)(2,1)S(1)}, bf16[5,88,128]{2,1,0:T(8,128)(2,1)S(1)}, u32[]{:S(2)}, u32[]{:S(2)}) collective-permute-start(bf16[5,88,128]{2,1,0:T(8,128)(2,1)S(1)} %get-tuple-element.24), channel_id=1, source_target_pairs={{0,4},{4,8},{8,12},{1,5},{5,9},{9,13},{2,6},{6,10},{10,14},{3,7},{... | collective-permute-start | bytes 337928 | tf_op jit(solution)/shard_map/ppermute | solution.py:507
  10.5 1.3 %collective-permute-start.1 = (bf16[5,88,128]{2,1,0:T(8,128)(2,1)S(1)}, bf16[5,88,128]{2,1,0:T(8,128)(2,1)S(1)}, u32[]{:S(2)}, u32[]{:S(2)}) collective-permute-start(bf16[5,88,128]{2,1,0:T(8,128)(2,1)S(1)} %get-tuple-element.25), channel_id=1, source_target_pairs={{4,0},{8,4},{12,8},{5,1},{9,5},{13,9},{6,2},{10,6},{14,10},{7,3},{... | collective-permute-start | bytes 337928 | tf_op jit(solution)/shard_map/ppermute | solution.py:508
  11.9 0.4 collective-permute-done.3.right_ref
  12.4 3.6 %collective-permute-start.4 = (f32[2,88,128]{2,1,0:T(8,128)S(1)}, f32[2,88,128]{2,1,0:T(8,128)S(1)}, u32[]{:S(2)}, u32[]{:S(2)}) collective-permute-start(f32[2,88,128]{2,1,0:T(8,128)S(1)} %shard_map.86), channel_id=1, source_target_pairs={{0,4},{4,8},{8,12},{1,5},{5,9},{9,13},{2,6},{6,10},{10,14},{3,7},{... | collective-permute-start | bytes 270344 | tf_op jit(solution)/shard_map/ppermute | solution.py:514
  16.0 1.3 %collective-permute-start.5 = (f32[2,88,128]{2,1,0:T(8,128)S(1)}, f32[2,88,128]{2,1,0:T(8,128)S(1)}, u32[]{:S(2)}, u32[]{:S(2)}) collective-permute-start(f32[2,88,128]{2,1,0:T(8,128)S(1)} %shard_map.86), channel_id=1, source_target_pairs={{4,0},{8,4},{12,8},{5,1},{9,5},{13,9},{6,2},{10,6},{14,10},{7,3},{... | collective-permute-start | bytes 270344 | tf_op jit(solution)/shard_map/ppermute | solution.py:515
  17.3 1.1 pad.15
  18.4 0.2 copy.11.w1_ref
  18.7 2.5 %collective-permute-done.5.below_ref = f32[2,88,128]{2,1,0:T(8,128)S(1)} collective-permute-done((f32[2,88,128]{2,1,0:T(8,128)S(1)}, f32[2,88,128]{2,1,0:T(8,128)S(1)}, u32[]{:S(2)}, u32[]{:S(2)}) %collective-permute-start.5) | collective-permute-done | bytes 90144 | tf_op jit(solution)/shard_map/ppermute | solution.py:515
  21.2 5.6 %shard_map.87 = (f32[1024,128]{1,0:T(8,128)}, f32[192,1152]{1,0:T(8,128)}, bf16[192,1152]{1,0:T(8,128)(2,1)}, bf16[864,1152]{1,0:T(8,128)(2,1)}, f32[88,1152]{1,0:T(8,128)}) custom-call(f32[16,88,128]{2,1,0:T(8,128)S(1)} %get-tuple-element.23.own_ref, bf16[5,88,128]{2,1,0:T(8,128)(2,1)S(1)} %collective-permute-done.top_ref, ...), custom_call_target="tpu_custom_call" | custom-call | tf_op jit(solution)/shard_map/pallas_call | solution.py:54
  26.9 8.4 %all-to-all-start = ((f32[16,64,128]{2,1,0:T(8,128)}), f32[16,64,128]{2,1,0:T(8,128)S(1)}, u32[]{:S(2)}, u32[]{:S(2)}) async-start(f32[16,64,128]{2,1,0:T(8,128)} %bitcast.6), calls=%async_computation | async-start | bytes 1048576 | tf_op jit(solution)/shard_map/all_to_all | solution.py:478
  35.3 0.4 shard_map.88.truth_ref
  35.7 11.0 %all-to-all-done.forecast_ref = f32[16,64,128]{2,1,0:T(8,128)S(1)} async-done(((f32[16,64,128]{2,1,0:T(8,128)}), f32[16,64,128]{2,1,0:T(8,128)S(1)}, u32[]{:S(2)}, u32[]{:S(2)}) %all-to-all-start) | async-done | bytes 524320 | tf_op jit(solution)/shard_map/all_to_all | solution.py:478
  46.8 1.8 %shard_map.89 = bf16[16,64,128]{2,1,0:T(8,128)(2,1)} custom-call(f32[16,64,128]{2,1,0:T(8,128)S(1)} %all-to-all-done.forecast_ref, f32[64,128]{1,0:T(8,128)S(1)} %shard_map.88.truth_ref), custom_call_target="tpu_custom_call" | custom-call | tf_op jit(solution)/shard_map/pallas_call | solution.py:54
  48.6 6.8 %all-to-all-start.1 = ((bf16[16,64,128]{2,1,0:T(8,128)(2,1)}), bf16[16,64,128]{2,1,0:T(8,128)(2,1)S(1)}, u32[]{:S(2)}, u32[]{:S(2)}) async-start(bf16[16,64,128]{2,1,0:T(8,128)(2,1)} %shard_map.89), calls=%async_computation.1 | async-start | bytes 524288 | tf_op jit(solution)/shard_map/all_to_all | solution.py:478
  55.5 0.2 copy.12.w2_ref
  55.7 7.6 %all-to-all-done.1.grad_ref = bf16[16,64,128]{2,1,0:T(8,128)(2,1)S(1)} async-done(((bf16[16,64,128]{2,1,0:T(8,128)(2,1)}), bf16[16,64,128]{2,1,0:T(8,128)(2,1)S(1)}, u32[]{:S(2)}, u32[]{:S(2)}) %all-to-all-start.1) | async-done | bytes 262176 | tf_op jit(solution)/shard_map/all_to_all | solution.py:478
  63.3 5.7 %shard_map.90 = (bf16[192,1152]{1,0:T(8,128)(2,1)}, f32[88,1152]{1,0:T(8,128)}, bf16[32,72,128]{2,1,0:T(8,128)(2,1)}, bf16[192,256]{1,0:T(8,128)(2,1)S(1)}, bf16[192,256]{1,0:T(8,128)(2,1)S(1)}) custom-call(bf16[16,64,128]{2,1,0:T(8,128)(2,1)S(1)} %all-to-all-done.1.grad_ref, f32[192,1152]{1,0:T(8,128)} %get-tuple-element.29.pre_far, ...), custom_call_target="tpu_custom_call" | custom-call | tf_op jit(solution)/shard_map/pallas_call | solution.py:54
  69.0 9.8 %all-to-all-start.2 = ((bf16[32,72,128]{2,1,0:T(8,128)(2,1)}), bf16[32,72,128]{2,1,0:T(8,128)(2,1)S(1)}, u32[]{:S(2)}, u32[]{:S(2)}) async-start(bf16[32,72,128]{2,1,0:T(8,128)(2,1)} %get-tuple-element.35), calls=%async_computation.2 | async-start | bytes 1179648 | tf_op jit(solution)/shard_map/all_to_all | solution.py:478
  78.8 3.3 %collective-permute-start.6 = (bf16[192,256]{1,0:T(8,128)(2,1)S(1)}, bf16[192,256]{1,0:T(8,128)(2,1)S(1)}, u32[]{:S(2)}, u32[]{:S(2)}) collective-permute-start(bf16[192,256]{1,0:T(8,128)(2,1)S(1)} %get-tuple-element.36), channel_id=1, source_target_pairs={{0,4},{4,8},{8,12},{1,5},{5,9},{9,13},{2,6},{6,10},{10,14},{3,7},{... | collective-permute-start | bytes 294920 | tf_op jit(solution)/shard_map/ppermute | solution.py:598
  82.1 1.3 %collective-permute-start.7 = (bf16[192,256]{1,0:T(8,128)(2,1)S(1)}, bf16[192,256]{1,0:T(8,128)(2,1)S(1)}, u32[]{:S(2)}, u32[]{:S(2)}) collective-permute-start(bf16[192,256]{1,0:T(8,128)(2,1)S(1)} %get-tuple-element.37), channel_id=1, source_target_pairs={{4,0},{8,4},{12,8},{5,1},{9,5},{13,9},{6,2},{10,6},{14,10},{7,3},{... | collective-permute-start | bytes 294920 | tf_op jit(solution)/shard_map/ppermute | solution.py:598
  83.4 4.1 %collective-permute-done.6.top_ref = bf16[192,256]{1,0:T(8,128)(2,1)S(1)} collective-permute-done((bf16[192,256]{1,0:T(8,128)(2,1)S(1)}, bf16[192,256]{1,0:T(8,128)(2,1)S(1)}, u32[]{:S(2)}, u32[]{:S(2)}) %collective-permute-start.6) | collective-permute-done | bytes 98336 | tf_op jit(solution)/shard_map/ppermute | solution.py:598
  87.6 1.9 %collective-permute-done.7.bottom_ref = bf16[192,256]{1,0:T(8,128)(2,1)S(1)} collective-permute-done((bf16[192,256]{1,0:T(8,128)(2,1)S(1)}, bf16[192,256]{1,0:T(8,128)(2,1)S(1)}, u32[]{:S(2)}, u32[]{:S(2)}) %collective-permute-start.7) | collective-permute-done | bytes 98336 | tf_op jit(solution)/shard_map/ppermute | solution.py:598
  89.5 1.5 %all-to-all-done.2.parts_ref = bf16[32,72,128]{2,1,0:T(8,128)(2,1)S(1)} async-done(((bf16[32,72,128]{2,1,0:T(8,128)(2,1)}), bf16[32,72,128]{2,1,0:T(8,128)(2,1)S(1)}, u32[]{:S(2)}, u32[]{:S(2)}) %all-to-all-start.2) | async-done | bytes 589856 | tf_op jit(solution)/shard_map/all_to_all | solution.py:478
  91.0 0.1 shard_map.92
  91.1 11.6 %all_to_all.25.parts_ref = bf16[8,72,128]{2,1,0:T(8,128)(2,1)S(1)} all-to-all(bf16[8,72,128]{2,1,0:T(8,128)(2,1)S(1)} %shard_map.92), channel_id=1, replica_groups=mesh['half'=2,'ring'=8,'lat'=4,'lon'=4] {'ring'}, dimensions={0} | all-to-all | bytes 294912 | tf_op jit(solution)/shard_map/all_to_all | solution.py:478
  102.7 0.9 shard_map.93
  103.6 7.4 %all-to-all-start.4 = ((bf16[32,72,128]{2,1,0:T(8,128)(2,1)}), bf16[32,72,128]{2,1,0:T(8,128)(2,1)S(1)}, u32[]{:S(2)}, u32[]{:S(2)}) async-start(bf16[32,72,128]{2,1,0:T(8,128)(2,1)} %shard_map.93), calls=%async_computation.4 | async-start | bytes 1179648 | tf_op jit(solution)/shard_map/all_to_all | solution.py:478
  111.1 3.4 %shard_map.91 = bf16[664,128]{1,0:T(8,128)(2,1)} custom-call(bf16[192,1152]{1,0:T(8,128)(2,1)} %get-tuple-element.32.grad_pre_far, f32[88,1152]{1,0:T(8,128)} %get-tuple-element.33.grad_far, f32[88,1152]{1,0:T(8,128)} %get-tuple-element.34.latent_far, f32[1,83]{1,0:T(1,128)S(1)} %bitcast.20, bf16[792,192]{1,0:T(8,128)(2,1)S(1)} %bitcast.17, ...), custom_call_target="tpu_custom_call" | custom-call | tf_op jit(solution)/shard_map/pallas_call | solution.py:54
  114.6 8.7 %all-to-all-done.4.parts_ref = bf16[32,72,128]{2,1,0:T(8,128)(2,1)S(1)} async-done(((bf16[32,72,128]{2,1,0:T(8,128)(2,1)}), bf16[32,72,128]{2,1,0:T(8,128)(2,1)S(1)}, u32[]{:S(2)}, u32[]{:S(2)}) %all-to-all-start.4) | async-done | bytes 589856 | tf_op jit(solution)/shard_map/all_to_all | solution.py:478
  123.2 1.4 %shard_map.94 = (f32[9,83,192]{2,1,0:T(8,128)}, f32[9,83,192]{2,1,0:T(8,128)}) custom-call(bf16[32,72,128]{2,1,0:T(8,128)(2,1)S(1)} %all-to-all-done.4.parts_ref), custom_call_target="tpu_custom_call" | custom-call | tf_op jit(solution)/shard_map/pallas_call | solution.py:54
  (19 shorter events, 0.4 us)
Async XLA Ops:
  0.6 20.6 %copy-start = (f32[83]{0:T(128)S(1)}, f32[83]{0:T(128)}, u32[]{:S(2)}) copy-start(f32[83]{0:T(128)} %param.9) | copy-start | bytes 1000
  0.6 18.0 %copy-start.1 = (bf16[9,83,192]{2,1,0:T(8,128)(2,1)S(1)}, bf16[9,83,192]{2,1,0:T(8,128)(2,1)}, u32[]{:S(2)}) copy-start(bf16[9,83,192]{2,1,0:T(8,128)(2,1)} %param.11) | copy-start | bytes 860548
  3.0 8.9 %collective-permute-start.2 = (f32[88,128]{1,0:T(8,128)S(1)}, f32[88,128]{1,0:T(8,128)S(1)}, u32[]{:S(2)}, u32[]{:S(2)}) collective-permute-start(f32[88,128]{1,0:T(8,128)S(1)} %get-tuple-element.26), channel_id=1, source_target_pairs={{0,1},{1,2},{2,3},{3,0},{4,5},{5,6},{6,7},{7,4},{8,9},{9,10},{10,1... | collective-permute-start | bytes 135176 | tf_op jit(solution)/shard_map/ppermute | solution.py:511
  7.4 5.0 %collective-permute-start.3 = (f32[88,128]{1,0:T(8,128)S(1)}, f32[88,128]{1,0:T(8,128)S(1)}, u32[]{:S(2)}, u32[]{:S(2)}) collective-permute-start(f32[88,128]{1,0:T(8,128)S(1)} %get-tuple-element.27), channel_id=1, source_target_pairs={{1,0},{2,1},{3,2},{0,3},{5,4},{6,5},{7,6},{4,7},{9,8},{10,9},{11,1... | collective-permute-start | bytes 135176 | tf_op jit(solution)/shard_map/ppermute | solution.py:512
  7.4 11.3 %collective-permute-start = (bf16[5,88,128]{2,1,0:T(8,128)(2,1)S(1)}, bf16[5,88,128]{2,1,0:T(8,128)(2,1)S(1)}, u32[]{:S(2)}, u32[]{:S(2)}) collective-permute-start(bf16[5,88,128]{2,1,0:T(8,128)(2,1)S(1)} %get-tuple-element.24), channel_id=1, source_target_pairs={{0,4},{4,8},{8,12},{1,5},{5,9},{9,13},{2,6},{6,10},{10,14},{3,7},{... | collective-permute-start | bytes 337928 | tf_op jit(solution)/shard_map/ppermute | solution.py:507
  10.5 8.2 %collective-permute-start.1 = (bf16[5,88,128]{2,1,0:T(8,128)(2,1)S(1)}, bf16[5,88,128]{2,1,0:T(8,128)(2,1)S(1)}, u32[]{:S(2)}, u32[]{:S(2)}) collective-permute-start(bf16[5,88,128]{2,1,0:T(8,128)(2,1)S(1)} %get-tuple-element.25), channel_id=1, source_target_pairs={{4,0},{8,4},{12,8},{5,1},{9,5},{13,9},{6,2},{10,6},{14,10},{7,3},{... | collective-permute-start | bytes 337928 | tf_op jit(solution)/shard_map/ppermute | solution.py:508
  12.4 6.3 %collective-permute-start.4 = (f32[2,88,128]{2,1,0:T(8,128)S(1)}, f32[2,88,128]{2,1,0:T(8,128)S(1)}, u32[]{:S(2)}, u32[]{:S(2)}) collective-permute-start(f32[2,88,128]{2,1,0:T(8,128)S(1)} %shard_map.86), channel_id=1, source_target_pairs={{0,4},{4,8},{8,12},{1,5},{5,9},{9,13},{2,6},{6,10},{10,14},{3,7},{... | collective-permute-start | bytes 270344 | tf_op jit(solution)/shard_map/ppermute | solution.py:514
  16.0 5.3 %collective-permute-start.5 = (f32[2,88,128]{2,1,0:T(8,128)S(1)}, f32[2,88,128]{2,1,0:T(8,128)S(1)}, u32[]{:S(2)}, u32[]{:S(2)}) collective-permute-start(f32[2,88,128]{2,1,0:T(8,128)S(1)} %shard_map.86), channel_id=1, source_target_pairs={{4,0},{8,4},{12,8},{5,1},{9,5},{13,9},{6,2},{10,6},{14,10},{7,3},{... | collective-permute-start | bytes 270344 | tf_op jit(solution)/shard_map/ppermute | solution.py:515
  26.9 19.9 %all-to-all-start = ((f32[16,64,128]{2,1,0:T(8,128)}), f32[16,64,128]{2,1,0:T(8,128)S(1)}, u32[]{:S(2)}, u32[]{:S(2)}) async-start(f32[16,64,128]{2,1,0:T(8,128)} %bitcast.6), calls=%async_computation | async-start | bytes 1048576 | tf_op jit(solution)/shard_map/all_to_all | solution.py:478
  48.6 14.7 %all-to-all-start.1 = ((bf16[16,64,128]{2,1,0:T(8,128)(2,1)}), bf16[16,64,128]{2,1,0:T(8,128)(2,1)S(1)}, u32[]{:S(2)}, u32[]{:S(2)}) async-start(bf16[16,64,128]{2,1,0:T(8,128)(2,1)} %shard_map.89), calls=%async_computation.1 | async-start | bytes 524288 | tf_op jit(solution)/shard_map/all_to_all | solution.py:478
  69.0 42.1 %copy-start.2 = (bf16[9,192,83]{1,2,0:T(8,128)(2,1)S(1)}, bf16[9,192,83]{1,2,0:T(8,128)(2,1)}, u32[]{:S(2)}) copy-start(bf16[9,192,83]{1,2,0:T(8,128)(2,1)} %param.10) | copy-start | bytes 860548
  69.0 22.0 %all-to-all-start.2 = ((bf16[32,72,128]{2,1,0:T(8,128)(2,1)}), bf16[32,72,128]{2,1,0:T(8,128)(2,1)S(1)}, u32[]{:S(2)}, u32[]{:S(2)}) async-start(bf16[32,72,128]{2,1,0:T(8,128)(2,1)} %get-tuple-element.35), calls=%async_computation.2 | async-start | bytes 1179648 | tf_op jit(solution)/shard_map/all_to_all | solution.py:478
  78.8 8.7 %collective-permute-start.6 = (bf16[192,256]{1,0:T(8,128)(2,1)S(1)}, bf16[192,256]{1,0:T(8,128)(2,1)S(1)}, u32[]{:S(2)}, u32[]{:S(2)}) collective-permute-start(bf16[192,256]{1,0:T(8,128)(2,1)S(1)} %get-tuple-element.36), channel_id=1, source_target_pairs={{0,4},{4,8},{8,12},{1,5},{5,9},{9,13},{2,6},{6,10},{10,14},{3,7},{... | collective-permute-start | bytes 294920 | tf_op jit(solution)/shard_map/ppermute | solution.py:598
  82.1 7.4 %collective-permute-start.7 = (bf16[192,256]{1,0:T(8,128)(2,1)S(1)}, bf16[192,256]{1,0:T(8,128)(2,1)S(1)}, u32[]{:S(2)}, u32[]{:S(2)}) collective-permute-start(bf16[192,256]{1,0:T(8,128)(2,1)S(1)} %get-tuple-element.37), channel_id=1, source_target_pairs={{4,0},{8,4},{12,8},{5,1},{9,5},{13,9},{6,2},{10,6},{14,10},{7,3},{... | collective-permute-start | bytes 294920 | tf_op jit(solution)/shard_map/ppermute | solution.py:598
  103.6 19.6 %all-to-all-start.4 = ((bf16[32,72,128]{2,1,0:T(8,128)(2,1)}), bf16[32,72,128]{2,1,0:T(8,128)(2,1)S(1)}, u32[]{:S(2)}, u32[]{:S(2)}) async-start(bf16[32,72,128]{2,1,0:T(8,128)(2,1)} %shard_map.93), calls=%async_computation.4 | async-start | bytes 1179648 | tf_op jit(solution)/shard_map/all_to_all | solution.py:478
